TPU v7x, 32 devices: a whole 2x2x4 slice. The times are simulated.
32 devices in a mesh: fsdp: 2 (over x), ctx: 4 (over z), tp: 4 (over y, core).
Axes of the slice: x: 2, y: 2, z: 4, core: 2. Of those that a mesh axis runs over, the one named last changes fastest.
Arguments:
- inputs: bfloat16 [4, 736, 1152], P('fsdp', 'ctx'), may hold values from -6 to 6
- cotangent: bfloat16 [4, 736, 1152], P('fsdp', 'ctx'), may hold values from -6 to 6
- valid_count: int32 [4], P('fsdp'), may hold values from 369 to 736, as said below
- norm_gain: float32 [2, 2, 1152], replicated, may hold values from 0.5 to 1.5
- norm_bias: float32 [2, 2, 1152], replicated, may hold values from -1.8 to 1.8
- w_qkv: bfloat16 [2, 1152, 3, 1152], P(None, ('fsdp', 'ctx'), None, 'tp'), may hold values from -0.25 to 0.25
- bias_qv: float32 [2, 2, 1152], P(None, None, 'tp'), may hold values from -3 to 3
- w_out: bfloat16 [2, 1152, 1152], P(None, ('fsdp', 'ctx'), 'tp'), may hold values from -1.5 to 1.5
- w_up: bfloat16 [2, 1152, 4304], P(None, ('fsdp', 'ctx'), 'tp'), may hold values from -0.1875 to 0.1875
- bias_up: float32 [2, 4304], P(None, 'tp'), may hold values from -3 to 3
- w_down: bfloat16 [2, 1152, 4304], P(None, ('fsdp', 'ctx'), 'tp'), may hold values from -0.09375 to 0.09375
- bias_resid: float32 [2, 2, 1152], replicated, may hold values from -1.8 to 1.8
Outputs:
- output: bfloat16 [4, 736, 1152], P('fsdp', 'ctx')
- grad_inputs: float32 [4, 736, 1152], P('fsdp', 'ctx')
- grad_norm_gain: float32 [2, 2, 1152], replicated
- grad_norm_bias: float32 [2, 2, 1152], replicated
- grad_qkv: float32 [2, 1152, 3, 1152], P(None, ('fsdp', 'ctx'), None, 'tp')
- grad_bias_qv: float32 [2, 2, 1152], P(None, None, 'tp')
- grad_out: float32 [2, 1152, 1152], P(None, ('fsdp', 'ctx'), 'tp')
- grad_up: float32 [2, 1152, 4304], P(None, ('fsdp', 'ctx'), 'tp')
- grad_bias_up: float32 [2, 4304], P(None, 'tp')
- grad_down: float32 [2, 1152, 4304], P(None, ('fsdp', 'ctx'), 'tp')
- grad_bias_resid: float32 [2, 2, 1152], replicated
Inputs may be any that keep to these rules, and one draw needn't show every extreme that they name: `valid_count`: some image has no padding.
All inputs are finite; a program needn't handle non-finite values.
Results may differ from a plain program's by a relative error of at most 0.028.
The roundings to bfloat16 on the way count: a program that leaves them out, or rounds other values in their place, can miss the bound.
Values may be sent and summed in bfloat16 or wider, within the bound.
A program may use at most 192 MiB of HBM per device.

v0:
```python
import jax
import jax.numpy as jnp
from jax import lax
from jax.sharding import PartitionSpec as P

HEAD_DIM = 72


norm_eps = 1e-06
gelu_root = 0.7978845608028654
gelu_cubic = 0.044715
masked_score = -1e30


def layer_norm(values, scale_vec, shift_vec):
    centre = jnp.mean(values, axis=-1, keepdims=True)
    centred = values - centre
    spread = jnp.mean(centred * centred, axis=-1, keepdims=True)
    return centred * lax.rsqrt(spread + norm_eps) * scale_vec + shift_vec


def gelu_tanh(values):
    return (
        0.5
        * values
        * (1.0 + jnp.tanh(gelu_root * (values + gelu_cubic * values * values * values)))
    )


def fetch_weights(qkv_rows, up_rows, out_rows, down_rows):
    return (
        lax.all_gather(qkv_rows, ("fsdp", "ctx"), axis=0, tiled=True),
        lax.all_gather(up_rows, ("fsdp", "ctx"), axis=0, tiled=True),
        lax.all_gather(out_rows, ("fsdp", "ctx"), axis=0, tiled=True),
        lax.all_gather(down_rows, ("fsdp", "ctx"), axis=0, tiled=True),
    )


def split_heads(array_in):
    return array_in.reshape(
        array_in.shape[0], array_in.shape[1], array_in.shape[2] // HEAD_DIM, HEAD_DIM
    )


def attend(queries, all_keys, all_values, key_valid):
    images, query_rows, head_width = queries.shape
    score_scale = HEAD_DIM ** (-0.5)
    scores = (
        jnp.einsum(
            "bqhe,bkhe->bhqk",
            split_heads(queries),
            split_heads(all_keys),
            preferred_element_type=jnp.float32,
        )
        * score_scale
    )
    scores = jnp.where(key_valid[:, None, None, :], scores, masked_score)
    highest = jnp.max(scores, axis=-1, keepdims=True)
    weights = jnp.exp(scores - highest)
    attn_probs = weights / jnp.sum(weights, axis=-1, keepdims=True)
    low_probs = attn_probs.astype(jnp.bfloat16)
    mixed_heads = jnp.einsum(
        "bhqk,bkhe->bqhe", low_probs, split_heads(all_values), preferred_element_type=jnp.float32
    )
    return (
        attn_probs,
        low_probs,
        mixed_heads.reshape(images, query_rows, head_width).astype(jnp.bfloat16),
    )


def run_layer(stream, weights, vectors, key_valid, finish):
    qkv_full, up_full, out_full, down_full = weights
    gains, shifts, qv_bias, up_bias, resid_bias = vectors
    low_first = layer_norm(stream, gains[0], shifts[0]).astype(jnp.bfloat16)
    projected = jnp.einsum("bcd,dkt->bckt", low_first, qkv_full, preferred_element_type=jnp.float32)
    queries = (projected[:, :, 0] + qv_bias[0]).astype(jnp.bfloat16)
    own_keys = projected[:, :, 1].astype(jnp.bfloat16)
    own_values = (projected[:, :, 2] + qv_bias[1]).astype(jnp.bfloat16)
    all_keys, all_values = (
        lax.all_gather(own_keys, "ctx", axis=1, tiled=True),
        lax.all_gather(own_values, "ctx", axis=1, tiled=True),
    )
    attn_probs, low_probs, mixed_heads = attend(queries, all_keys, all_values, key_valid)
    attn_part = jnp.einsum("bct,dt->bcd", mixed_heads, out_full, preferred_element_type=jnp.float32)
    attn_total = lax.psum(attn_part, "tp")
    middle = stream + (attn_total + resid_bias[0])
    low_second = layer_norm(middle, gains[1], shifts[1]).astype(jnp.bfloat16)
    pre_act = (
        jnp.einsum("bcd,df->bcf", low_second, up_full, preferred_element_type=jnp.float32) + up_bias
    )
    hidden = gelu_tanh(pre_act).astype(jnp.bfloat16)
    if not finish:
        return (
            stream,
            low_first,
            queries,
            all_keys,
            all_values,
            attn_probs,
            low_probs,
            mixed_heads,
            middle,
            low_second,
            pre_act,
            hidden,
        )
    mlp_part = jnp.einsum("bcf,df->bcd", hidden, down_full, preferred_element_type=jnp.float32)
    mlp_total = lax.psum(mlp_part, "tp")
    return middle + (mlp_total + resid_bias[1])


def back_layer(grad_stream, saved, weights, vectors):
    (
        stream,
        low_first,
        queries,
        all_keys,
        all_values,
        attn_probs,
        low_probs,
        mixed_heads,
        middle,
        low_second,
        pre_act,
        hidden,
    ) = saved
    qkv_full, up_full, out_full, down_full = weights
    gains, shifts, qv_bias, up_bias, resid_bias = vectors
    grad_low = grad_stream.astype(jnp.bfloat16)
    down_bias_grad = jnp.sum(grad_low, axis=(0, 1), dtype=jnp.float32)
    down_grad = jnp.einsum("bcd,bcf->df", grad_low, hidden, preferred_element_type=jnp.float32)
    hidden_grad = jnp.einsum("bcd,df->bcf", grad_low, down_full, preferred_element_type=jnp.float32)
    _, gelu_back = jax.vjp(gelu_tanh, pre_act)
    pre_grad = gelu_back(hidden_grad)[0].astype(jnp.bfloat16)
    up_bias_grad = jnp.sum(pre_grad, axis=(0, 1), dtype=jnp.float32)
    up_grad = jnp.einsum("bcd,bcf->df", low_second, pre_grad, preferred_element_type=jnp.float32)
    second_part = jnp.einsum("bcf,df->bcd", pre_grad, up_full, preferred_element_type=jnp.float32)
    second_grad = lax.psum(second_part, "tp")
    _, second_back = jax.vjp(layer_norm, middle, gains[1], shifts[1])
    middle_term, gain_two, shift_two = second_back(second_grad)
    middle_grad = grad_stream + middle_term
    middle_low = middle_grad.astype(jnp.bfloat16)
    out_bias_grad = jnp.sum(middle_low, axis=(0, 1), dtype=jnp.float32)
    out_grad = jnp.einsum(
        "bcd,bct->dt", middle_low, mixed_heads, preferred_element_type=jnp.float32
    )
    mixed_grad = jnp.einsum(
        "bcd,dt->bct", middle_low, out_full, preferred_element_type=jnp.float32
    ).astype(jnp.bfloat16)
    images, query_rows, head_width = queries.shape
    key_rows = all_keys.shape[1]
    score_scale = HEAD_DIM ** (-0.5)
    mixed_split = split_heads(mixed_grad)
    prob_grad = jnp.einsum(
        "bqhe,bkhe->bhqk", mixed_split, split_heads(all_values), preferred_element_type=jnp.float32
    )
    value_terms = jnp.einsum(
        "bhqk,bqhe->bkhe", low_probs, mixed_split, preferred_element_type=jnp.float32
    ).reshape(images, key_rows, head_width)
    inner = jnp.sum(attn_probs * prob_grad, axis=-1, keepdims=True)
    score_grad = (attn_probs * (prob_grad - inner)).astype(jnp.bfloat16)
    query_grad = (
        (
            score_scale
            * jnp.einsum(
                "bhqk,bkhe->bqhe",
                score_grad,
                split_heads(all_keys),
                preferred_element_type=jnp.float32,
            )
        )
        .reshape(images, query_rows, head_width)
        .astype(jnp.bfloat16)
    )
    key_terms = (
        score_scale
        * jnp.einsum(
            "bhqk,bqhe->bkhe", score_grad, split_heads(queries), preferred_element_type=jnp.float32
        )
    ).reshape(images, key_rows, head_width)
    key_sum, value_sum = (
        lax.psum_scatter(key_terms, "ctx", scatter_dimension=1, tiled=True),
        lax.psum_scatter(value_terms, "ctx", scatter_dimension=1, tiled=True),
    )
    key_grad = key_sum.astype(jnp.bfloat16)
    value_grad = value_sum.astype(jnp.bfloat16)
    stacked_grads = jnp.stack([query_grad, key_grad, value_grad], axis=2)
    qv_grad = jnp.stack(
        [
            jnp.sum(query_grad, axis=(0, 1), dtype=jnp.float32),
            jnp.sum(value_grad, axis=(0, 1), dtype=jnp.float32),
        ]
    )
    qkv_grad = jnp.einsum(
        "bcd,bckt->dkt", low_first, stacked_grads, preferred_element_type=jnp.float32
    )
    first_part = jnp.einsum(
        "bckt,dkt->bcd", stacked_grads, qkv_full, preferred_element_type=jnp.float32
    )
    first_grad = lax.psum(first_part, "tp")
    _, first_back = jax.vjp(layer_norm, stream, gains[0], shifts[0])
    stream_term, gain_one, shift_one = first_back(first_grad)
    below_grad = middle_grad + stream_term
    gain_pair = jnp.stack([gain_one, gain_two])
    shift_pair = jnp.stack([shift_one, shift_two])
    large_grads = (qkv_grad, up_grad, out_grad, down_grad)
    small_grads = (
        gain_pair,
        shift_pair,
        qv_grad,
        up_bias_grad,
        jnp.stack([out_bias_grad, down_bias_grad]),
    )
    return (below_grad, large_grads, small_grads)


def stack_layers(member, source):
    return jnp.stack([per_layer[member] for per_layer in source])


def per_device(
    inputs,
    cotangent,
    valid_count,
    norm_gain,
    norm_bias,
    w_qkv,
    bias_qv,
    w_out,
    w_up,
    bias_up,
    w_down,
    bias_resid,
):
    block_rows = inputs.shape[1]
    full_rows = block_rows * lax.axis_size("ctx")
    positions = lax.axis_index("ctx") * block_rows + jnp.arange(block_rows, dtype=jnp.int32)
    query_valid = (positions[None, :] < valid_count[:, None]).astype(jnp.float32)
    key_valid = jnp.arange(full_rows, dtype=jnp.int32)[None, :] < valid_count[:, None]
    layer_count = w_qkv.shape[0]
    stream = inputs.astype(jnp.float32)
    layer_inputs = []
    kept_weights = []
    for layer_at in range(layer_count):
        weights = fetch_weights(w_qkv[layer_at], w_up[layer_at], w_out[layer_at], w_down[layer_at])
        vectors = (
            norm_gain[layer_at],
            norm_bias[layer_at],
            bias_qv[layer_at],
            bias_up[layer_at],
            bias_resid[layer_at],
        )
        layer_inputs.append(stream)
        kept_weights.append(weights)
        stream = run_layer(stream, weights, vectors, key_valid, True)
    output = stream.astype(jnp.bfloat16)
    grad_stream = cotangent.astype(jnp.float32) * query_valid[:, :, None]
    large_list = [None] * layer_count
    small_list = [None] * layer_count
    for layer_at in reversed(range(layer_count)):
        vectors = (
            norm_gain[layer_at],
            norm_bias[layer_at],
            bias_qv[layer_at],
            bias_up[layer_at],
            bias_resid[layer_at],
        )
        weights = fetch_weights(w_qkv[layer_at], w_up[layer_at], w_out[layer_at], w_down[layer_at])
        saved = run_layer(layer_inputs[layer_at], weights, vectors, key_valid, False)
        grad_stream, large_grads, small_grads = back_layer(grad_stream, saved, weights, vectors)
        large_list[layer_at] = (
            lax.psum_scatter(
                large_grads[0].astype(jnp.bfloat16),
                ("fsdp", "ctx"),
                scatter_dimension=0,
                tiled=True,
            ).astype(jnp.float32),
            lax.psum_scatter(
                large_grads[1].astype(jnp.bfloat16),
                ("fsdp", "ctx"),
                scatter_dimension=0,
                tiled=True,
            ).astype(jnp.float32),
            lax.psum_scatter(
                large_grads[2].astype(jnp.bfloat16),
                ("fsdp", "ctx"),
                scatter_dimension=0,
                tiled=True,
            ).astype(jnp.float32),
            lax.psum_scatter(
                large_grads[3].astype(jnp.bfloat16),
                ("fsdp", "ctx"),
                scatter_dimension=0,
                tiled=True,
            ).astype(jnp.float32),
        )
        small_list[layer_at] = (
            lax.psum(small_grads[0].astype(jnp.bfloat16), ("fsdp", "ctx")).astype(jnp.float32),
            lax.psum(small_grads[1].astype(jnp.bfloat16), ("fsdp", "ctx")).astype(jnp.float32),
            lax.psum(small_grads[2].astype(jnp.bfloat16), ("fsdp", "ctx")).astype(jnp.float32),
            lax.psum(small_grads[3].astype(jnp.bfloat16), ("fsdp", "ctx")).astype(jnp.float32),
            lax.psum(small_grads[4].astype(jnp.bfloat16), ("fsdp", "ctx")).astype(jnp.float32),
        )
    return (
        output,
        grad_stream,
        stack_layers(0, small_list),
        stack_layers(1, small_list),
        stack_layers(0, large_list),
        stack_layers(2, small_list),
        stack_layers(2, large_list),
        stack_layers(1, large_list),
        stack_layers(3, small_list),
        stack_layers(3, large_list),
        stack_layers(4, small_list),
    )


def solution(mesh):
    placed = (
        P("fsdp", "ctx", None),
        P("fsdp", "ctx", None),
        P("fsdp"),
        P(),
        P(),
        P(None, ("fsdp", "ctx"), None, "tp"),
        P(None, None, "tp"),
        P(None, ("fsdp", "ctx"), "tp"),
        P(None, ("fsdp", "ctx"), "tp"),
        P(None, "tp"),
        P(None, ("fsdp", "ctx"), "tp"),
        P(),
    )
    return jax.shard_map(
        per_device,
        mesh=mesh,
        in_specs=placed,
        out_specs=(
            P("fsdp", "ctx", None),
            P("fsdp", "ctx", None),
            P(),
            P(),
            P(None, ("fsdp", "ctx"), None, "tp"),
            P(None, None, "tp"),
            P(None, ("fsdp", "ctx"), "tp"),
            P(None, ("fsdp", "ctx"), "tp"),
            P(None, "tp"),
            P(None, ("fsdp", "ctx"), "tp"),
            P(),
        ),
        check_vma=False,
    )
```

profile of v0, /device:TPU:0, one launch (start us, length us, event | category | flops | bytes accessed | tf_op | source)
XLA Modules:
  0.0 1671.2 jit_solution(14836445747485011114)
XLA Ops:
  12.8 42.8 %all-gather.2 = bf16[1,1152,288]{2,1,0:T(8,128)(2,1)} all-gather(bf16[1,144,288]{2,1,0:T(8,128)(2,1)S(1)} %get-tuple-element.79), channel_id=4, replica_groups=mesh['fsdp'=2,'ctx'=4,'tp'=4] {'fsdp','ctx'}, dimensions={1}, use_global_device_ids=true | all-gather | bytes 746496 | tf_op jit(solution)/shard_map/all_gather | solution.py:34
  144.0 40.6 %all-reduce.10.cloned.1.call-done = f32[2,184,1152]{2,1,0:T(8,128)} async-done(((f32[2,184,1152]{2,1,0:T(8,128)}), f32[2,184,1152]{2,1,0:T(8,128)}) %all-reduce.10.cloned.1.call-update) | async-done | bytes 1695760 | tf_op jit(solution)/shard_map/psum | solution.py:86
  186.6 55.6 %all-gather.19.cloned.1.call-done = bf16[1,1152,1076]{2,1,0:T(8,128)(2,1)} async-done(((bf16[1,144,1076]{2,1,0:T(8,128)(2,1)}), bf16[1,1152,1076]{2,1,0:T(8,128)(2,1)}) %all-gather.19.cloned.1.call-update) | async-done | bytes 2479120 | tf_op jit(solution)/shard_map/all_gather | solution.py:33
  246.8 51.6 %all-gather.21.cloned.1.call-done = bf16[1,1152,1076]{2,1,0:T(8,128)(2,1)} async-done(((bf16[1,144,1076]{2,1,0:T(8,128)(2,1)}), bf16[1,1152,1076]{2,1,0:T(8,128)(2,1)}) %all-gather.21.cloned.1.call-update) | async-done | bytes 2479120 | tf_op jit(solution)/shard_map/all_gather | solution.py:35
  304.8 36.1 %all-gather.7 = bf16[1,1152,288]{2,1,0:T(8,128)(2,1)} all-gather(bf16[1,144,288]{2,1,0:T(8,128)(2,1)S(1)} %get-tuple-element.78), channel_id=9, replica_groups=mesh['fsdp'=2,'ctx'=4,'tp'=4] {'fsdp','ctx'}, dimensions={1}, use_global_device_ids=true | all-gather | bytes 746496 | tf_op jit(solution)/shard_map/all_gather | solution.py:34
  349.2 55.6 %all-gather.23.cloned.1.call-done = bf16[1,1152,3,288]{3,1,2,0:T(8,128)(2,1)} async-done(((bf16[1,144,3,288]{3,1,2,0:T(8,128)(2,1)}), bf16[1,1152,3,288]{3,1,2,0:T(8,128)(2,1)}) %all-gather.23.cloned.1.call-update) | async-done | bytes 1990672 | tf_op jit(solution)/shard_map/all_gather | solution.py:32
  476.4 41.6 %all-reduce.14.cloned.1.call-done = f32[2,184,1152]{2,1,0:T(8,128)} async-done(((f32[2,184,1152]{2,1,0:T(8,128)}), f32[2,184,1152]{2,1,0:T(8,128)}) %all-reduce.14.cloned.1.call-update) | async-done | bytes 1695760 | tf_op jit(solution)/shard_map/psum | solution.py:86
  521.2 53.9 %all-gather.25.cloned.1.call-done = bf16[1,1152,1076]{2,1,0:T(8,128)(2,1)} async-done(((bf16[1,144,1076]{2,1,0:T(8,128)(2,1)}), bf16[1,1152,1076]{2,1,0:T(8,128)(2,1)}) %all-gather.25.cloned.1.call-update) | async-done | bytes 2479120 | tf_op jit(solution)/shard_map/all_gather | solution.py:33
  580.3 51.2 %all-gather.27.cloned.1.call-done = bf16[1,1152,1076]{2,1,0:T(8,128)(2,1)} async-done(((bf16[1,144,1076]{2,1,0:T(8,128)(2,1)}), bf16[1,1152,1076]{2,1,0:T(8,128)(2,1)}) %all-gather.27.cloned.1.call-update) | async-done | bytes 2479120 | tf_op jit(solution)/shard_map/all_gather | solution.py:35
  641.4 43.2 %all-reduce.16.cloned.1.call-done = f32[2,184,1152]{2,1,0:T(8,128)} async-done(((f32[2,184,1152]{2,1,0:T(8,128)}), f32[2,184,1152]{2,1,0:T(8,128)}) %all-reduce.16.cloned.1.call-update) | async-done | bytes 1695760 | tf_op jit(solution)/shard_map/psum | solution.py:139
  717.8 29.6 %reduce-scatter.15.cloned.1.call-done = f32[2,184,288]{2,1,0:T(8,128)} async-done(((f32[2,736,288]{2,1,0:T(8,128)}), f32[2,184,288]{2,1,0:T(8,128)}) %reduce-scatter.15.cloned.1.call-update) | async-done | bytes 423952 | tf_op jit(solution)/shard_map/reduce_scatter | solution.py:184
  749.2 46.5 %reduce-scatter.13.cloned.1.call-done = f32[2,184,288]{2,1,0:T(8,128)} async-done(((f32[2,736,288]{2,1,0:T(8,128)}), f32[2,184,288]{2,1,0:T(8,128)}) %reduce-scatter.13.cloned.1.call-update) | async-done | bytes 423952 | tf_op jit(solution)/shard_map/reduce_scatter | solution.py:183
  802.3 44.3 %all-reduce.18.cloned.1.call-done = f32[2,184,1152]{2,1,0:T(8,128)} async-done(((f32[2,184,1152]{2,1,0:T(8,128)}), f32[2,184,1152]{2,1,0:T(8,128)}) %all-reduce.18.cloned.1.call-update) | async-done | bytes 1695760 | tf_op jit(solution)/shard_map/psum | solution.py:201
  859.9 45.1 %all-reduce.20.cloned.1.call-done = f32[2,184,1152]{2,1,0:T(8,128)} async-done(((f32[2,184,1152]{2,1,0:T(8,128)}), f32[2,184,1152]{2,1,0:T(8,128)}) %all-reduce.20.cloned.1.call-update) | async-done | bytes 1695760 | tf_op jit(solution)/shard_map/psum | solution.py:139
  968.1 47.1 %reduce-scatter.17.cloned.1.call-done = f32[2,184,288]{2,1,0:T(8,128)} async-done(((f32[2,736,288]{2,1,0:T(8,128)}), f32[2,184,288]{2,1,0:T(8,128)}) %reduce-scatter.17.cloned.1.call-update) | async-done | bytes 423952 | tf_op jit(solution)/shard_map/reduce_scatter | solution.py:183
  1026.8 52.8 %reduce-scatter.27.cloned.1.call-done = bf16[144,288]{1,0:T(8,128)(2,1)} async-done(((bf16[1152,288]{1,0:T(8,128)(2,1)}), bf16[144,288]{1,0:T(8,128)(2,1)}) %reduce-scatter.27.cloned.1.call-update) | async-done | bytes 82960 | tf_op jit(solution)/shard_map/reduce_scatter | solution.py:285
  1079.6 64.2 %reduce-scatter.25.cloned.1.call-done = bf16[144,288]{1,0:T(8,128)(2,1)} async-done(((bf16[1152,288]{1,0:T(8,128)(2,1)}), bf16[144,288]{1,0:T(8,128)(2,1)}) %reduce-scatter.25.cloned.1.call-update) | async-done | bytes 82960 | tf_op jit(solution)/shard_map/reduce_scatter | solution.py:285
  1150.1 66.6 %reduce-scatter.31.cloned.1.call-done = bf16[144,1076]{1,0:T(8,128)(2,1)} async-done(((bf16[1152,1076]{1,0:T(8,128)(2,1)}), bf16[144,1076]{1,0:T(8,128)(2,1)}) %reduce-scatter.31.cloned.1.call-update) | async-done | bytes 309904 | tf_op jit(solution)/shard_map/reduce_scatter | solution.py:279
  1216.7 74.0 %reduce-scatter.29.cloned.1.call-done = bf16[144,1076]{1,0:T(8,128)(2,1)} async-done(((bf16[1152,1076]{1,0:T(8,128)(2,1)}), bf16[144,1076]{1,0:T(8,128)(2,1)}) %reduce-scatter.29.cloned.1.call-update) | async-done | bytes 309904 | tf_op jit(solution)/shard_map/reduce_scatter | solution.py:279
  1293.0 71.0 %reduce-scatter.35.cloned.1.call-done = bf16[144,1076]{1,0:T(8,128)(2,1)} async-done(((bf16[1152,1076]{1,0:T(8,128)(2,1)}), bf16[144,1076]{1,0:T(8,128)(2,1)}) %reduce-scatter.35.cloned.1.call-update) | async-done | bytes 309904 | tf_op jit(solution)/shard_map/reduce_scatter | solution.py:291
  1364.0 74.2 %reduce-scatter.33.cloned.1.call-done = bf16[144,1076]{1,0:T(8,128)(2,1)} async-done(((bf16[1152,1076]{1,0:T(8,128)(2,1)}), bf16[144,1076]{1,0:T(8,128)(2,1)}) %reduce-scatter.33.cloned.1.call-update) | async-done | bytes 309904 | tf_op jit(solution)/shard_map/reduce_scatter | solution.py:291
  1440.4 72.8 %all-reduce.22.cloned.1.call-done = (f32[2,184,1152]{2,1,0:T(8,128)}, f32[2,184,1152]{2,1,0:T(8,128)}) async-done(((f32[2,184,1152]{2,1,0:T(8,128)}, f32[2,184,1152]{2,1,0:T(8,128)}), (f32[2,184,1152]{2,1,0:T(8,128)}, f32[2,184,1152]{2,1,0:T(8,128)})) %all-reduce.22.cloned.1.call-update) | async-done | bytes 3391504 | tf_op jit(solution)/shard_map/psum | solution.py:109
  1516.2 38.9 %all-reduce.1 = (bf16[1,2,1152]{2,1,0:T(2,128)(2,1)S(1)}, bf16[1,2,1152]{2,1,0:T(2,128)(2,1)S(1)}, bf16[1,2,1152]{2,1,0:T(2,128)(2,1)S(1)}, bf16[1,2,1152]{2,1,0...) all-reduce(bf16[1,2,1152]{2,1,0:T(2,128)(2,1)S(1)} %maximum_bitcast, ...), channel_id=1, replica_groups=mesh['fsdp'=2,'ctx'=4,'tp'=4] {'fsdp','ctx'}, use_global_device_ids=true, to_apply=%region_39.40 | all-reduce | flops 17128 | bytes 68512 | tf_op jit(solution)/shard_map/psum | solution.py:299
  1588.1 73.9 %reduce-scatter.21.cloned.1.call-done = bf16[144,3,288]{2,0,1:T(8,128)(2,1)} async-done(((bf16[1152,3,288]{2,0,1:T(8,128)(2,1)}), bf16[144,3,288]{2,0,1:T(8,128)(2,1)}) %reduce-scatter.21.cloned.1.call-update) | async-done | bytes 248848 | tf_op jit(solution)/shard_map/reduce_scatter | solution.py:273
  (368 shorter events, 382.5 us)
Async XLA Ops:
  9.4 175.2 %all-reduce.10.cloned.1.call-start = ((), (), s32[]{:S(2)}) async-start(), calls=%async_computation.12 | async-start | bytes 3391488 | tf_op jit(solution)/shard_map/psum | solution.py:86
  140.7 101.6 %all-gather.19.cloned.1.call-start = ((), (), s32[]{:S(2)}) async-start(), calls=%async_computation.31 | async-start | bytes 2985984 | tf_op jit(solution)/shard_map/all_gather | solution.py:33
  141.6 156.8 %all-gather.21.cloned.1.call-start = ((), (), s32[]{:S(2)}) async-start(), calls=%async_computation.32 | async-start | bytes 2985984 | tf_op jit(solution)/shard_map/all_gather | solution.py:35
  142.6 204.5 %all-reduce.12.cloned.1.call-start = ((), (), s32[]{:S(2)}) async-start(), calls=%async_computation.13 | async-start | bytes 3391488 | tf_op jit(solution)/shard_map/psum | solution.py:109
  303.4 101.4 %all-gather.23.cloned.1.call-start = ((), (), s32[]{:S(2)}) async-start(), calls=%async_computation.33 | async-start | bytes 2985984 | tf_op jit(solution)/shard_map/all_gather | solution.py:32
  304.0 214.0 %all-reduce.14.cloned.1.call-start = ((), (), s32[]{:S(2)}) async-start(), calls=%async_computation.14 | async-start | bytes 3391488 | tf_op jit(solution)/shard_map/psum | solution.py:86
  474.8 100.4 %all-gather.25.cloned.1.call-start = ((), (), s32[]{:S(2)}) async-start(), calls=%async_computation.34 | async-start | bytes 2985984 | tf_op jit(solution)/shard_map/all_gather | solution.py:33
  475.6 155.9 %all-gather.27.cloned.1.call-start = ((), (), s32[]{:S(2)}) async-start(), calls=%async_computation.35 | async-start | bytes 2985984 | tf_op jit(solution)/shard_map/all_gather | solution.py:35
  476.3 208.3 %all-reduce.16.cloned.1.call-start = ((), (), s32[]{:S(2)}) async-start(), calls=%async_computation.15 | async-start | bytes 3391488 | tf_op jit(solution)/shard_map/psum | solution.py:139
  640.9 106.5 %reduce-scatter.15.cloned.1.call-start = ((), (), s32[]{:S(2)}) async-start(), calls=%async_computation.17 | async-start | bytes 2826240 | tf_op jit(solution)/shard_map/reduce_scatter | solution.py:184
  700.7 94.9 %reduce-scatter.13.cloned.1.call-start = ((), (), s32[]{:S(2)}) async-start(), calls=%async_computation.16 | async-start | bytes 2826240 | tf_op jit(solution)/shard_map/reduce_scatter | solution.py:183
  712.4 134.2 %all-reduce.18.cloned.1.call-start = ((), (), s32[]{:S(2)}) async-start(), calls=%async_computation.18 | async-start | bytes 3391488 | tf_op jit(solution)/shard_map/psum | solution.py:201
  802.1 102.9 %all-reduce.20.cloned.1.call-start = ((), (), s32[]{:S(2)}) async-start(), calls=%async_computation.19 | async-start | bytes 3391488 | tf_op jit(solution)/shard_map/psum | solution.py:139
  859.8 107.2 %reduce-scatter.19.cloned.1.call-start = ((), (), s32[]{:S(2)}) async-start(), calls=%async_computation.21 | async-start | bytes 2826240 | tf_op jit(solution)/shard_map/reduce_scatter | solution.py:184
  920.3 94.9 %reduce-scatter.17.cloned.1.call-start = ((), (), s32[]{:S(2)}) async-start(), calls=%async_computation.20 | async-start | bytes 2826240 | tf_op jit(solution)/shard_map/reduce_scatter | solution.py:183
  931.8 147.7 %reduce-scatter.27.cloned.1.call-start = ((), (), s32[]{:S(2)}) async-start(), calls=%async_computation.25 | async-start | bytes 995328 | tf_op jit(solution)/shard_map/reduce_scatter | solution.py:285
  934.9 208.9 %reduce-scatter.25.cloned.1.call-start = ((), (), s32[]{:S(2)}) async-start(), calls=%async_computation.24 | async-start | bytes 995328 | tf_op jit(solution)/shard_map/reduce_scatter | solution.py:285
  938.0 278.8 %reduce-scatter.31.cloned.1.call-start = ((), (), s32[]{:S(2)}) async-start(), calls=%async_computation.27 | async-start | bytes 2985984 | tf_op jit(solution)/shard_map/reduce_scatter | solution.py:279
  943.3 347.5 %reduce-scatter.29.cloned.1.call-start = ((), (), s32[]{:S(2)}) async-start(), calls=%async_computation.26 | async-start | bytes 2985984 | tf_op jit(solution)/shard_map/reduce_scatter | solution.py:279
  948.5 415.5 %reduce-scatter.35.cloned.1.call-start = ((), (), s32[]{:S(2)}) async-start(), calls=%async_computation.29 | async-start | bytes 2985984 | tf_op jit(solution)/shard_map/reduce_scatter | solution.py:291
  954.5 483.7 %reduce-scatter.33.cloned.1.call-start = ((), (), s32[]{:S(2)}) async-start(), calls=%async_computation.28 | async-start | bytes 2985984 | tf_op jit(solution)/shard_map/reduce_scatter | solution.py:291
  960.7 552.5 %all-reduce.22.cloned.1.call-start = ((), (), s32[]{:S(2)}) async-start(), calls=%async_computation.36 | async-start | bytes 6782976 | tf_op jit(solution)/shard_map/psum | solution.py:109
  1020.9 567.2 %reduce-scatter.23.cloned.1.call-start = ((), (), s32[]{:S(2)}) async-start(), calls=%async_computation.23 | async-start | bytes 2985984 | tf_op jit(solution)/shard_map/reduce_scatter | solution.py:273
  1025.4 636.5 %reduce-scatter.21.cloned.1.call-start = ((), (), s32[]{:S(2)}) async-start(), calls=%async_computation.22 | async-start | bytes 2985984 | tf_op jit(solution)/shard_map/reduce_scatter | solution.py:273
  (82 other events, 1630.7 us)
Sparse Core Ops, SparseCore 0:
  10.9 66.5 all-gather.16
  140.7 43.7 all-reduce.9
  187.2 55.0 all-gather.18
  244.8 53.5 all-gather.20
  303.6 43.5 all-reduce.11
  349.8 55.0 all-gather.22
  520.1 55.0 all-gather.24
  577.9 53.5 all-gather.26
  641.0 43.4 all-reduce.15
  700.8 46.5 reduce-scatter.14
  749.7 45.9 reduce-scatter.12
  802.2 44.3 all-reduce.17
  859.9 44.9 all-reduce.19
  920.5 46.5 reduce-scatter.18
  969.3 45.9 reduce-scatter.16
  1019.1 60.4 reduce-scatter.26
  1083.4 60.3 reduce-scatter.24
  1147.4 69.2 reduce-scatter.30
  1220.7 70.0 reduce-scatter.28
  1294.4 69.5 reduce-scatter.34
  1368.1 70.0 reduce-scatter.32
  1441.3 71.8 all-reduce.21
  1516.7 71.3 reduce-scatter.22
  1592.2 69.7 reduce-scatter.20
  (1 shorter events, 43.0 us)
where the time goes:
time: 1680 us; the launch traced here: 1670 us
  waiting for transfers between devices  1210 us (72%)
  blocking collectives  209 us (12%)
  matrix products  130 us (8%)
  local copies, waits for them, and re-layouts  55.1 us (3%)
  other arithmetic  48.3 us (3%)
    reduce_scatter x2, waiting for transfers between devices, per_device(): lax.psum_scatter(large_grads[3].astype(jnp.bfloat16), ('fsdp', 'ctx'), sc...  145 us
    reduce_scatter x2, waiting for transfers between devices, per_device(): lax.psum_scatter(large_grads[1].astype(jnp.bfloat16), ('fsdp', 'ctx'), sc...  141 us
    reduce_scatter x2, waiting for transfers between devices, per_device(): lax.psum_scatter(large_grads[2].astype(jnp.bfloat16), ('fsdp', 'ctx'), sc...  117 us
    all_gather x2, waiting for transfers between devices, fetch_weights(): lax.all_gather(up_rows, ('fsdp', 'ctx'), axis=0, tiled=True)  110 us
    all_gather x2, waiting for transfers between devices, fetch_weights(): lax.all_gather(down_rows, ('fsdp', 'ctx'), axis=0, tiled=True)  103 us
    reduce_scatter x2, waiting for transfers between devices, per_device(): lax.psum_scatter(large_grads[0].astype(jnp.bfloat16), ('fsdp', 'ctx'), sc...  99.1 us
    reduce_scatter x2, waiting for transfers between devices, back_layer(): lax.psum_scatter(key_terms, 'ctx', scatter_dimension=1, tiled=True)  93.6 us
    psum x2, waiting for transfers between devices, back_layer(): second_grad = lax.psum(second_part, 'tp')  88.3 us
  transfers between devices with their start and end apart: 25, of which 24 were waited for; matrix products, arithmetic and copies ran while one was open for 7% of the time, Pallas kernels for 0%

commit v1 on v0

v1 whole, which is shorter than its diff:
```python
import functools

import jax
import jax.numpy as jnp
from jax import lax
from jax.experimental import pallas as pl
from jax.experimental.pallas import tpu as pltpu
from jax.sharding import PartitionSpec as P

HEAD_DIM = 72
norm_eps = 1e-06
gelu_root = 0.7978845608028654
gelu_cubic = 0.044715
masked_score = -1e30

MESH = pl.DeviceIdType.MESH
f32 = jnp.float32
bf16 = jnp.bfloat16
VMEM = pltpu.VMEM
DMA = pltpu.SemaphoreType.DMA


def up_to(value, unit):
    return (value + unit - 1) // unit * unit


def dot(a, b, over):
    return lax.dot_general(a, b, (((over[0],), (over[1],)), ((), ())), preferred_element_type=f32)


class Sizes:
    def __init__(self, mesh, inputs, w_qkv, w_up):
        self.fsdp, self.ctx, self.tp = mesh.shape["fsdp"], mesh.shape["ctx"], mesh.shape["tp"]
        self.images, self.rows, self.d = inputs.shape
        self.layers, self.wrows = w_qkv.shape[0], w_qkv.shape[1]
        self.zl = self.ctx // self.images
        self.chips_y = self.tp // 2
        self.chips = self.zl * self.chips_y
        self.team = self.chips * 2
        self.part = up_to(-(-self.rows // self.tp), 16)
        self.block = self.images * self.part
        self.tile = 2 * self.block
        self.keys = self.chips * self.tile
        self.wide = w_qkv.shape[3] // self.zl
        self.heads = self.wide // HEAD_DIM
        self.ff = w_up.shape[2] // self.zl
        self.ffp = up_to(self.ff, 128)
        self.headp = up_to(self.wide, 128)
        self.qkvp = up_to(3 * self.wide, 128)
        self.attnp = up_to(4 * self.wide, 128)
        self.cols = self.attnp + 2 * self.ffp
        self.wrowsp = up_to(self.wrows, 16)
        self.groups = self.fsdp * self.ctx


class Place:
    def __init__(self, sz):
        self.sz = sz
        self.f, self.c, self.t = lax.axis_index("fsdp"), lax.axis_index("ctx"), lax.axis_index("tp")
        self.zh, self.zl = self.c // sz.zl, self.c % sz.zl
        self.y, self.k = self.t // 2, self.t % 2
        self.chip = self.zl * sz.chips_y + self.y
        self.slot = 2 * self.chip + self.k

    def chip_at(self, step):
        sz = self.sz
        zl = (self.zl + step // sz.chips_y) % sz.zl
        y = (self.y + step % sz.chips_y) % sz.chips_y
        return zl, y

    def chip_back(self, step):
        sz = self.sz
        zl = (self.zl + sz.zl - step // sz.chips_y) % sz.zl
        y = (self.y + sz.chips_y - step % sz.chips_y) % sz.chips_y
        return zl, y

    def index(self, chip):
        return chip[0] * self.sz.chips_y + chip[1]

    def device(self, chip):
        return (self.f, self.zh * self.sz.zl + chip[0], 2 * chip[1] + self.k)

    @property
    def twin(self):
        return (self.f, self.c, self.t + 1 - 2 * self.k)


def greet(others):
    barrier = pltpu.get_barrier_semaphore()
    for other in others:
        pl.semaphore_signal(barrier, inc=1, device_id=other, device_id_type=MESH)
    pl.semaphore_wait(barrier, len(others))


def send(src, dst, send_sem, recv_sem, device):
    return pltpu.make_async_remote_copy(
        src_ref=src, dst_ref=dst, send_sem=send_sem, recv_sem=recv_sem, device_id=device, device_id_type=MESH
    )


def team_peers(pc):
    return [pc.device(pc.chip_at(step)) for step in range(1, pc.sz.chips)] + [pc.twin]


class Gather:
    def __init__(self, pc, buf, sems, at):
        self.pc, self.buf, self.sems, self.at = pc, buf, sems, at

    def far(self, step, slot, device):
        return send(self.buf.at[slot], self.buf.at[slot], self.sems.at[self.at, 0, step],
                    self.sems.at[self.at, 1, step], device)

    def near(self, step, slot):
        return send(self.buf.at[slot], self.buf.at[slot], self.sems.at[self.at, 2, step],
                    self.sems.at[self.at, 3, step], self.pc.twin)

    def start(self):
        pc = self.pc
        for step in range(1, pc.sz.chips):
            self.far(step, pc.slot, pc.device(pc.chip_at(step))).start()
        self.near(0, pc.slot).start()

    def arrive(self, step):
        pc = self.pc
        chip = pc.chip_back(step)
        at = pc.index(chip)

        @pl.when(step > 0)
        def _():
            self.far(step, 2 * at + pc.k, pc.device(chip)).wait_recv()
            self.near(step, 2 * at + pc.k).start()

        self.near(step, 2 * at + 1 - pc.k).wait_recv()
        return at

    def finish(self):
        pc = self.pc
        for step in range(pc.sz.chips):
            if step:
                self.far(step, pc.slot, pc.device(pc.chip_at(step))).wait_send()
            self.near(step, pc.slot).wait_send()


class Scatter:
    def __init__(self, pc, bufs, sems, at):
        self.pc, self.sems, self.at = pc, sems, at
        self.both, self.keep, self.tsend, self.trecv, self.rsend, self.rrecv = bufs

    def near(self, step):
        return send(self.tsend.at[step], self.trecv.at[step], self.sems.at[self.at, 0, step],
                    self.sems.at[self.at, 1, step], self.pc.twin)

    def far(self, step):
        return send(self.rsend.at[step], self.rrecv.at[step], self.sems.at[self.at, 2, step],
                    self.sems.at[self.at, 3, step], self.pc.device(self.pc.chip_back(step)))

    def push(self, step, partial):
        pc, block = self.pc, self.pc.sz.block
        self.both[...] = partial.reshape(2, block, partial.shape[-1])
        self.tsend[step] = self.both[1 - pc.k].astype(bf16)
        self.near(step).start()
        self.keep[step] = self.both[pc.k]

        @pl.when(step > 0)
        def _():
            self.relay(step - 1)

    def relay(self, step):
        self.near(step).wait_recv()
        total = self.keep[step] + self.trecv[step].astype(f32)

        def own():
            self.keep[0] = total

        def other():
            self.rsend[step] = total.astype(bf16)
            self.far(step).start()

        if isinstance(step, int):
            own() if step == 0 else other()
        else:
            pl.when(step == 0)(own)
            pl.when(step > 0)(other)

    def flush(self):
        self.relay(self.pc.sz.chips - 1)

    def finish(self):
        total = self.keep[0]
        for step in range(1, self.pc.sz.chips):
            self.far(step).wait_recv()
            total = total + self.rrecv[step].astype(f32)
        for step in range(self.pc.sz.chips):
            self.near(step).wait_send()
            if step:
                self.far(step).wait_send()
        return total


def team_scratch(sz, gathers, scatters):
    n = sz.chips
    return [
        VMEM((2, sz.block, sz.d), f32),
        VMEM((n, sz.block, sz.d), f32),
        VMEM((n, sz.block, sz.d), bf16),
        VMEM((n, sz.block, sz.d), bf16),
        VMEM((n, sz.block, sz.d), bf16),
        VMEM((n, sz.block, sz.d), bf16),
        DMA((gathers, 4, n)),
        DMA((scatters, 4, n)),
    ]


def normalised(values):
    centre = jnp.mean(values, axis=-1, keepdims=True)
    centred = values - centre
    spread = jnp.mean(centred * centred, axis=-1, keepdims=True)
    inverse = lax.rsqrt(spread + norm_eps)
    return centred * inverse, inverse


def norm_back(values, gain, grad):
    high, inverse = normalised(values)
    scaled = grad * gain
    term = inverse * (
        scaled
        - jnp.mean(scaled, axis=-1, keepdims=True)
        - high * jnp.mean(scaled * high, axis=-1, keepdims=True)
    )
    return term, jnp.sum(grad * high, axis=0, keepdims=True), jnp.sum(grad, axis=0, keepdims=True)


def lanes_of(shape):
    return lax.broadcasted_iota(jnp.int32, shape, len(shape) - 1)


def unpack_out(sz, w_ref, o_ref):
    at = 3 * sz.wide // 128 * 128
    shift = 3 * sz.wide - at

    def step(i, carry):
        rows = pl.ds(pl.multiple_of(i * 128, 128), 128)
        piece = pltpu.roll(w_ref[rows, at:at + sz.headp].astype(f32), sz.headp - shift, 1)
        o_ref[rows, :] = jnp.where(lanes_of(piece.shape) < sz.wide, piece, 0.0).astype(bf16)
        return carry

    lax.fori_loop(0, sz.d // 128, step, 0)


def take(sz, values, kind):
    at = kind * sz.wide // 128 * 128
    shift = kind * sz.wide - at
    piece = values[:, at:at + sz.headp]
    if shift:
        piece = pltpu.roll(piece, sz.headp - shift, 1)
    return jnp.where(lanes_of(piece.shape) < sz.wide, piece, 0.0)


def head_of(values, head):
    lanes = lanes_of(values.shape)
    mine = (lanes >= head * HEAD_DIM) & (lanes < (head + 1) * HEAD_DIM)
    return jnp.where(mine, values, jnp.zeros_like(values))


def probabilities(q_head, keys, valid):
    scores = dot(q_head, keys, (1, 1)) * HEAD_DIM ** (-0.5)
    scores = jnp.where(valid > 0.0, scores, masked_score)
    weights = jnp.exp(scores - jnp.max(scores, axis=-1, keepdims=True))
    return weights / jnp.sum(weights, axis=-1, keepdims=True)


def forward_kernel(
    sz, stream_ref, w_ref, gain_ref, shift_ref, qv_ref, upb_ref, resid_ref, valid_ref,
    out_ref, middle_ref, n1_ref, n2_ref, q_ref, k_ref, v_ref, mixed_ref, pre_ref, hidden_ref,
    o_ref, both, keep, tsend, trecv, rsend, rrecv, gsems, ssems,
):
    pc = Place(sz)
    bufs = (both, keep, tsend, trecv, rsend, rrecv)
    greet(team_peers(pc))
    gather = Gather(pc, n1_ref, gsems, 0)
    high, _ = normalised(stream_ref[...])
    n1_ref[pc.slot] = (high * gain_ref[0:1, :] + shift_ref[0:1, :]).astype(bf16)
    gather.start()
    unpack_out(sz, w_ref, o_ref)

    def project(step, carry):
        at = gather.arrive(step)
        tokens = n1_ref[pl.ds(2 * at, 2)].reshape(sz.tile, sz.d)
        both3 = dot(tokens, w_ref[:, 0:sz.qkvp], (1, 0))
        q_ref[at] = (take(sz, both3, 0) + qv_ref[0:1, :]).astype(bf16)
        k_ref[at] = take(sz, both3, 1).astype(bf16)
        v_ref[at] = (take(sz, both3, 2) + qv_ref[1:2, :]).astype(bf16)
        return carry

    lax.fori_loop(0, sz.chips, project, 0)
    gather.finish()
    scatter = Scatter(pc, bufs, ssems, 0)

    def attend(step, carry):
        at = pc.index(pc.chip_back(step))
        keys = k_ref[...].reshape(sz.keys, sz.headp)
        values = v_ref[...].reshape(sz.keys, sz.headp)
        queries = q_ref[at]
        total = jnp.zeros((sz.tile, sz.headp), f32)
        for head in range(sz.heads):
            probs = probabilities(head_of(queries, head), keys, valid_ref[...])
            total = total + dot(probs.astype(bf16), head_of(values, head), (1, 0))
        mixed = total.astype(bf16)
        mixed_ref[at] = mixed
        scatter.push(step, dot(mixed, o_ref[...], (1, 1)))
        return carry

    lax.fori_loop(0, sz.chips, attend, 0)
    scatter.flush()
    middle = stream_ref[...] + (scatter.finish() + resid_ref[0:1, :])
    middle_ref[...] = middle
    gather = Gather(pc, n2_ref, gsems, 1)
    high, _ = normalised(middle)
    n2_ref[pc.slot] = (high * gain_ref[1:2, :] + shift_ref[1:2, :]).astype(bf16)
    gather.start()
    scatter2 = Scatter(pc, bufs, ssems, 1)

    def feed(step, carry):
        at = gather.arrive(step)
        tokens = n2_ref[pl.ds(2 * at, 2)].reshape(sz.tile, sz.d)
        pre = dot(tokens, w_ref[:, sz.attnp:sz.attnp + sz.ffp], (1, 0)) + upb_ref[...]
        pre_ref[at] = pre
        hidden = (0.5 * pre * (1.0 + jnp.tanh(gelu_root * (pre + gelu_cubic * pre * pre * pre)))).astype(bf16)
        hidden_ref[at] = hidden
        scatter2.push(step, dot(hidden, w_ref[:, sz.attnp + sz.ffp:], (1, 1)))
        return carry

    lax.fori_loop(0, sz.chips, feed, 0)
    scatter2.flush()
    gather.finish()
    out_ref[...] = middle_ref[...] + (scatter2.finish() + resid_ref[1:2, :])


def backward_kernel(
    sz, grad_ref, stream_ref, middle_ref, n1_ref, n2_ref, q_ref, k_ref, v_ref, mixed_ref, pre_ref, hidden_ref,
    w_ref, gain_ref, valid_ref,
    below_ref, dw_ref, vec_ref, dqv_ref, dup_ref,
    o_ref, gl_ref, ml_ref, pg_ref, mg_ref, dk_ref, dv_ref, stack_ref, gmid_ref,
    both, keep, tsend, trecv, rsend, rrecv, gsems, ssems,
):
    pc = Place(sz)
    bufs = (both, keep, tsend, trecv, rsend, rrecv)
    greet(team_peers(pc))
    up_at, down_at = sz.attnp, sz.attnp + sz.ffp
    span = 384 if sz.d % 384 == 0 else 128

    gather = Gather(pc, gl_ref, gsems, 0)
    grad_low = grad_ref[...].astype(bf16)
    gl_ref[pc.slot] = grad_low
    gather.start()
    vec_ref[5:6, :] = jnp.sum(grad_low.astype(f32), axis=0, keepdims=True)
    unpack_out(sz, w_ref, o_ref)
    scatter = Scatter(pc, bufs, ssems, 0)
    dup_ref[...] = jnp.zeros_like(dup_ref)

    def feed(step, carry):
        at = gather.arrive(step)
        grads = gl_ref[pl.ds(2 * at, 2)].reshape(sz.tile, sz.d)
        back = dot(grads, w_ref[:, down_at:], (1, 0))
        pre = pre_ref[at]
        bent = jnp.tanh(gelu_root * (pre + gelu_cubic * pre * pre * pre))
        slope = 0.5 * (1.0 + bent) + 0.5 * pre * (1.0 - bent * bent) * (
            gelu_root * (1.0 + 3.0 * gelu_cubic * pre * pre)
        )
        pre_grad = (back * slope).astype(bf16)
        pg_ref[at] = pre_grad
        dup_ref[...] += jnp.sum(pre_grad.astype(f32), axis=0, keepdims=True)
        scatter.push(step, dot(pre_grad, w_ref[:, up_at:down_at], (1, 1)))
        return carry

    lax.fori_loop(0, sz.chips, feed, 0)
    scatter.flush()

    def grads_ff(i, carry):
        lanes = pl.ds(pl.multiple_of(i * span, 128), span)
        hidden = hidden_ref[...].reshape(sz.keys, sz.ffp)
        dw_ref[lanes, down_at:] = dot(gl_ref[:, :, lanes].reshape(sz.keys, span), hidden, (0, 0)).astype(bf16)
        pre_grad = pg_ref[...].reshape(sz.keys, sz.ffp)
        dw_ref[lanes, up_at:down_at] = dot(n2_ref[:, :, lanes].reshape(sz.keys, span), pre_grad, (0, 0)).astype(bf16)
        return carry

    lax.fori_loop(0, sz.d // span, grads_ff, 0)
    gather.finish()
    second = scatter.finish()
    term, dgain, dshift = norm_back(middle_ref[...], gain_ref[1:2, :], second)
    vec_ref[1:2, :] = dgain
    vec_ref[3:4, :] = dshift
    grad_mid = grad_ref[...] + term
    gmid_ref[...] = grad_mid
    mid_low = grad_mid.astype(bf16)
    gather2 = Gather(pc, ml_ref, gsems, 1)
    ml_ref[pc.slot] = mid_low
    gather2.start()
    vec_ref[4:5, :] = jnp.sum(mid_low.astype(f32), axis=0, keepdims=True)

    def mix(step, carry):
        at = gather2.arrive(step)
        grads = ml_ref[pl.ds(2 * at, 2)].reshape(sz.tile, sz.d)
        mg_ref[at] = dot(grads, o_ref[...], (1, 0)).astype(bf16)
        return carry

    lax.fori_loop(0, sz.chips, mix, 0)
    gather2.finish()
    dk_ref[...] = jnp.zeros_like(dk_ref)
    dv_ref[...] = jnp.zeros_like(dv_ref)
    dqv_ref[...] = jnp.zeros_like(dqv_ref)
    scale = HEAD_DIM ** (-0.5)

    def attend(at, carry):
        keys = k_ref[...].reshape(sz.keys, sz.headp)
        values = v_ref[...].reshape(sz.keys, sz.headp)
        total = jnp.zeros((sz.tile, sz.headp), f32)
        for head in range(sz.heads):
            q_head = head_of(q_ref[at], head)
            g_head = head_of(mg_ref[at], head)
            probs = probabilities(q_head, keys, valid_ref[...])
            dprobs = dot(g_head, values, (1, 1))
            inner = jnp.sum(probs * dprobs, axis=-1, keepdims=True)
            dscores = (probs * (dprobs - inner)).astype(bf16)
            total = total + dot(dscores, head_of(keys, head), (1, 0))
            dk_ref[...] += dot(dscores, q_head, (0, 0))
            dv_ref[...] += dot(probs.astype(bf16), g_head, (0, 0))
        dq = (scale * total).astype(bf16).astype(f32)
        dqv_ref[0:1, :] += jnp.sum(dq, axis=0, keepdims=True)
        stack_ref[at, :, 0:sz.headp] = dq.astype(bf16)
        return carry

    lax.fori_loop(0, sz.chips, attend, 0)
    scatter2 = Scatter(pc, bufs, ssems, 1)

    def back_project(step, carry):
        at = pc.index(pc.chip_back(step))
        rows = pl.ds(pl.multiple_of(at * sz.tile, sz.tile), sz.tile)
        dk = (scale * dk_ref[rows, :]).astype(bf16).astype(f32)
        dv = dv_ref[rows, :].astype(bf16).astype(f32)
        dqv_ref[1:2, :] += jnp.sum(dv, axis=0, keepdims=True)
        dq = stack_ref[at, :, 0:sz.headp].astype(f32)
        total = jnp.pad(dq, ((0, 0), (0, sz.qkvp - sz.headp)))
        for kind, piece in ((1, dk), (2, dv)):
            start = kind * sz.wide // 128 * 128
            shift = kind * sz.wide - start
            moved = pltpu.roll(piece, shift, 1) if shift else piece
            total = total + jnp.pad(moved, ((0, 0), (start, sz.qkvp - start - sz.headp)))
        stacked = total.astype(bf16)
        stack_ref[at] = stacked
        scatter2.push(step, dot(stacked, w_ref[:, 0:sz.qkvp], (1, 1)))
        return carry

    lax.fori_loop(0, sz.chips, back_project, 0)
    scatter2.flush()
    o_at = 3 * sz.wide // 128 * 128
    o_shift = 3 * sz.wide - o_at

    def grads_attn(i, carry):
        lanes = pl.ds(pl.multiple_of(i * span, 128), span)
        stacked = stack_ref[...].reshape(sz.keys, sz.qkvp)
        dqkv = dot(n1_ref[:, :, lanes].reshape(sz.keys, span), stacked, (0, 0))
        mixed = mixed_ref[...].reshape(sz.keys, sz.headp)
        dout = dot(ml_ref[:, :, lanes].reshape(sz.keys, span), mixed, (0, 0))
        if o_shift:
            dout = pltpu.roll(dout, o_shift, 1)
        total = jnp.pad(dqkv, ((0, 0), (0, sz.attnp - sz.qkvp))) + jnp.pad(
            dout, ((0, 0), (o_at, sz.attnp - o_at - sz.headp))
        )
        dw_ref[lanes, 0:sz.attnp] = total.astype(bf16)
        return carry

    lax.fori_loop(0, sz.d // span, grads_attn, 0)
    first = scatter2.finish()
    term, dgain, dshift = norm_back(stream_ref[...], gain_ref[0:1, :], first)
    vec_ref[0:1, :] = dgain
    vec_ref[2:3, :] = dshift
    vec_ref[6:8, :] = jnp.zeros_like(vec_ref[6:8, :])
    below_ref[...] = gmid_ref[...] + term


def whole(ref_count):
    return [pl.BlockSpec(memory_space=pltpu.VMEM)] * ref_count


def params(collective_id):
    return pltpu.CompilerParams(
        collective_id=collective_id, has_side_effects=True, vmem_limit_bytes=60 * 1024 * 1024
    )


def forward(sz, stream, w, gains, shifts, qv, upb, resid, valid):
    shapes = [
        ((sz.block, sz.d), f32), ((sz.block, sz.d), f32),
        ((sz.team, sz.block, sz.d), bf16), ((sz.team, sz.block, sz.d), bf16),
        ((sz.chips, sz.tile, sz.headp), bf16), ((sz.chips, sz.tile, sz.headp), bf16),
        ((sz.chips, sz.tile, sz.headp), bf16), ((sz.chips, sz.tile, sz.headp), bf16),
        ((sz.chips, sz.tile, sz.ffp), f32), ((sz.chips, sz.tile, sz.ffp), bf16),
    ]
    return pl.pallas_call(
        functools.partial(forward_kernel, sz),
        out_shape=[jax.ShapeDtypeStruct(*s) for s in shapes],
        in_specs=whole(8),
        out_specs=whole(len(shapes)),
        scratch_shapes=[VMEM((sz.d, sz.headp), bf16)] + team_scratch(sz, 2, 2),
        compiler_params=params(1),
        name="layer_forward",
    )(stream, w, gains, shifts, qv, upb, resid, valid)


def backward(sz, grad, stream, saved, w, gains, valid):
    shapes = [
        ((sz.block, sz.d), f32), ((sz.d, sz.cols), bf16), ((8, sz.d), f32),
        ((2, sz.headp), f32), ((1, sz.ffp), f32),
    ]
    return pl.pallas_call(
        functools.partial(backward_kernel, sz),
        out_shape=[jax.ShapeDtypeStruct(*s) for s in shapes],
        in_specs=whole(14),
        out_specs=whole(len(shapes)),
        scratch_shapes=[
            VMEM((sz.d, sz.headp), bf16),
            VMEM((sz.team, sz.block, sz.d), bf16),
            VMEM((sz.team, sz.block, sz.d), bf16),
            VMEM((sz.chips, sz.tile, sz.ffp), bf16),
            VMEM((sz.chips, sz.tile, sz.headp), bf16),
            VMEM((sz.keys, sz.headp), f32),
            VMEM((sz.keys, sz.headp), f32),
            VMEM((sz.chips, sz.tile, sz.qkvp), bf16),
            VMEM((sz.block, sz.d), f32),
        ]
        + team_scratch(sz, 2, 2),
        compiler_params=params(2),
        name="layer_backward",
    )(grad, stream, *saved, w, gains, valid)


class Weights:
    def __init__(self, pc, own_ref, all_ref, sems):
        self.pc, self.own, self.all, self.sems = pc, own_ref, all_ref, sems

    def along_ctx(self, step):
        pc, sz = self.pc, self.pc.sz
        c = (pc.c + step) % sz.ctx
        return send(self.own.at[c % sz.zl], self.all.at[pc.f * sz.ctx + pc.c], self.sems.at[0, 0, step],
                    self.sems.at[0, 1, step], (pc.f, c, pc.t))

    def own_copy(self):
        pc, sz = self.pc, self.pc.sz
        return pltpu.make_async_copy(self.own.at[pc.zl], self.all.at[pc.f * sz.ctx + pc.c], self.sems.at[0, 0, 0])

    def along_fsdp(self, jump, step):
        pc, sz = self.pc, self.pc.sz
        at = pc.f * sz.ctx + (pc.c + sz.ctx - step) % sz.ctx
        return send(self.all.at[at], self.all.at[at], self.sems.at[jump, 0, step], self.sems.at[jump, 1, step],
                    ((pc.f + jump) % sz.fsdp, pc.c, pc.t))

    def start(self):
        for step in range(1, self.pc.sz.ctx):
            self.along_ctx(step).start()
        self.own_copy().start()

    def forward(self):
        sz = self.pc.sz
        for step in range(sz.ctx):
            if step:
                self.along_ctx(step).wait_recv()
            else:
                self.own_copy().wait()
            for jump in range(1, sz.fsdp):
                self.along_fsdp(jump, step).start()

    def finish(self):
        sz = self.pc.sz
        for step in range(sz.ctx):
            if step:
                self.along_ctx(step).wait_send()
            for jump in range(1, sz.fsdp):
                self.along_fsdp(jump, step).wait()


def weight_peers(pc):
    sz = pc.sz
    return [(pc.f, (pc.c + step) % sz.ctx, pc.t) for step in range(1, sz.ctx)] + [
        ((pc.f + jump) % sz.fsdp, pc.c, pc.t) for jump in range(1, sz.fsdp)
    ]


def fetch_kernel(sz, *refs):
    own_refs, tokens_ref = refs[:sz.layers], refs[sz.layers]
    all_refs, mine_ref = refs[sz.layers + 1:2 * sz.layers + 1], refs[2 * sz.layers + 1]
    wsems, tsems = refs[2 * sz.layers + 2:]
    pc = Place(sz)
    greet(weight_peers(pc))

    def swap(step):
        zh = (pc.zh + step) % sz.images
        return send(tokens_ref.at[zh], mine_ref.at[pc.zh], tsems.at[0, step], tsems.at[1, step],
                    (pc.f, zh * sz.zl + pc.zl, pc.t))

    for step in range(1, sz.images):
        swap(step).start()
    moves = [Weights(pc, own_refs[l], all_refs[l], wsems.at[l]) for l in range(sz.layers)]
    for move in moves:
        move.start()
    mine_ref[pc.zh] = tokens_ref[pc.zh]
    for move in moves:
        move.forward()
    for move in moves:
        move.finish()
    for step in range(1, sz.images):
        swap(step).wait()


def fetch(sz, packs, tokens):
    shapes = [((sz.groups, sz.wrowsp, sz.cols), bf16)] * sz.layers + [(tokens.shape, bf16)]
    return pl.pallas_call(
        functools.partial(fetch_kernel, sz),
        out_shape=[jax.ShapeDtypeStruct(*s) for s in shapes],
        in_specs=whole(sz.layers + 1),
        out_specs=whole(len(shapes)),
        scratch_shapes=[DMA((sz.layers, sz.fsdp, 2, sz.ctx)), DMA((2, sz.images))],
        compiler_params=params(3),
        name="fetch_weights",
    )(*packs, tokens)


class Reduce:
    def __init__(self, pc, dw_ref, out_ref, got, total, recv, sems):
        self.pc, self.dw, self.out = pc, dw_ref, out_ref
        self.got, self.total, self.recv, self.sems = got, total, recv, sems

    def along_fsdp(self, jump, step):
        pc, sz = self.pc, self.pc.sz
        f = (pc.f + jump) % sz.fsdp
        return send(self.dw.at[f * sz.ctx + (pc.c + step) % sz.ctx], self.got.at[jump - 1, step],
                    self.sems.at[jump, 0, step], self.sems.at[jump, 1, step], (f, pc.c, pc.t))

    def along_ctx(self, step):
        pc, sz = self.pc, self.pc.sz
        c = (pc.c + step) % sz.ctx
        return send(self.total.at[step], self.recv.at[step], self.sems.at[0, 0, step], self.sems.at[0, 1, step],
                    (pc.f, c, pc.t))

    def order(self):
        return list(range(1, self.pc.sz.ctx)) + [0]

    def start(self):
        for step in self.order():
            for jump in range(1, self.pc.sz.fsdp):
                self.along_fsdp(jump, step).start()

    def forward(self):
        pc, sz = self.pc, self.pc.sz
        for step in self.order():
            for jump in range(1, sz.fsdp):
                self.along_fsdp(jump, step).wait_recv()
            at = pc.f * sz.ctx + (pc.c + step) % sz.ctx
            total = self.dw[at].astype(f32)
            for jump in range(1, sz.fsdp):
                total = total + self.got[jump - 1, step].astype(f32)
            self.total[step] = total.astype(bf16)
            if step:
                self.along_ctx(step).start()

    def finish(self):
        pc, sz = self.pc, self.pc.sz
        for step in range(1, sz.ctx):
            self.along_ctx(step).wait_recv()
        for j in range(sz.zl):
            total = None
            for zh in range(sz.images):
                step = (pc.c + sz.ctx - (zh * sz.zl + j)) % sz.ctx
                piece = self.recv[step].astype(f32)
                total = piece if total is None else total + piece
            self.out[j] = total
        for step in range(sz.ctx):
            if step:
                self.along_ctx(step).wait_send()
            for jump in range(1, sz.fsdp):
                self.along_fsdp(jump, step).wait_send()


def give_kernel(sz, *refs):
    n = sz.layers
    dw_refs, ends_ref, small_ref, share_ref = refs[:n], refs[n], refs[n + 1], refs[n + 2]
    out_refs, whole_ref, small_out, share_out = refs[n + 3:2 * n + 3], *refs[2 * n + 3:2 * n + 6]
    got, total, recv, rsems, esems, ysems, ssems, from_tp, from_ctx, from_fsdp, sum_tp, sum_ctx = refs[2 * n + 6:]
    pc = Place(sz)
    peers = [(pc.f, (pc.c + s) % sz.ctx, pc.t) for s in range(1, sz.ctx)]
    peers += [((pc.f + s) % sz.fsdp, pc.c, pc.t) for s in range(1, sz.fsdp)]
    peers += [(pc.f, pc.c, (pc.t + s) % sz.tp) for s in range(1, sz.tp)]
    greet(peers)
    moves = [Reduce(pc, dw_refs[l], out_refs[l], got.at[l], total.at[l], recv.at[l], rsems.at[l]) for l in range(n)]

    def swap(step):
        zh = (pc.zh + step) % sz.images
        return send(ends_ref.at[zh], whole_ref.at[pc.t, pc.zh], esems.at[0, step], esems.at[1, step],
                    (pc.f, zh * sz.zl + pc.zl, pc.t))

    def spread(step):
        return send(whole_ref.at[pc.t], whole_ref.at[pc.t], ysems.at[0, step], ysems.at[1, step],
                    (pc.f, pc.c, (pc.t + step) % sz.tp))

    def spread_wait(step):
        back = (pc.t + sz.tp - step) % sz.tp
        return send(whole_ref.at[back], whole_ref.at[back], ysems.at[0, step], ysems.at[1, step],
                    (pc.f, pc.c, back))

    for step in range(1, sz.images):
        swap(step).start()
    whole_ref[pc.t, pc.zh] = ends_ref[pc.zh]
    for move in moves:
        move.start()
    for step in range(1, sz.images):
        swap(step).wait()
    for step in range(1, sz.tp):
        spread(step).start()

    def over_tp(step):
        return send(small_ref, from_tp.at[step], ssems.at[0, 0, step], ssems.at[0, 1, step],
                    (pc.f, pc.c, (pc.t + step) % sz.tp))

    def over_ctx(step):
        return send(sum_tp, from_ctx.at[step], ssems.at[1, 0, step], ssems.at[1, 1, step],
                    (pc.f, (pc.c + step) % sz.ctx, pc.t))

    def over_fsdp(step):
        return send(sum_ctx, from_fsdp.at[step], ssems.at[2, 0, step], ssems.at[2, 1, step],
                    ((pc.f + step) % sz.fsdp, pc.c, pc.t))

    rows = small_ref.shape[0]
    for step in range(1, sz.tp):
        over_tp(step).start()
    for move in moves:
        move.forward()
    value = small_ref[...]
    for step in range(1, sz.tp):
        over_tp(step).wait()
        value = value + from_tp[step]
    sum_tp[0:rows, :] = value
    sum_tp[rows:, :] = share_ref[...]
    for step in range(1, sz.ctx):
        over_ctx(step).start()
    value = sum_tp[...]
    for step in range(1, sz.ctx):
        over_ctx(step).wait()
        value = value + from_ctx[step]
    sum_ctx[...] = value
    for step in range(1, sz.fsdp):
        over_fsdp(step).start()
    for step in range(1, sz.fsdp):
        over_fsdp(step).wait()
        value = value + from_fsdp[step]
    small_out[...] = value[0:rows, :]
    share_out[...] = value[rows:, :]
    for step in range(1, sz.tp):
        spread_wait(step).wait_recv()
        spread(step).wait_send()
    for move in moves:
        move.recv[0] = move.total[0]
        move.finish()


def give(sz, dws, ends, small, share):
    rows = small.shape[0] + share.shape[0]
    shapes = [((sz.zl, sz.wrowsp, sz.cols), f32)] * sz.layers + [
        ((sz.tp,) + ends.shape, bf16), (small.shape, f32), (share.shape, f32),
    ]
    n, far = sz.layers, max(sz.tp, sz.ctx, sz.fsdp)
    return pl.pallas_call(
        functools.partial(give_kernel, sz),
        out_shape=[jax.ShapeDtypeStruct(*s) for s in shapes],
        in_specs=whole(n + 3),
        out_specs=whole(len(shapes)),
        scratch_shapes=[
            VMEM((n, max(sz.fsdp - 1, 1), sz.ctx, sz.wrowsp, sz.cols), bf16),
            VMEM((n, sz.ctx, sz.wrowsp, sz.cols), bf16),
            VMEM((n, sz.ctx, sz.wrowsp, sz.cols), bf16),
            DMA((n, sz.fsdp, 2, sz.ctx)),
            DMA((2, sz.images)),
            DMA((2, sz.tp)),
            DMA((3, 2, far)),
            VMEM((sz.tp,) + small.shape, f32),
            VMEM((sz.ctx, rows, sz.d), f32),
            VMEM((sz.fsdp, rows, sz.d), f32),
            VMEM((rows, sz.d), f32),
            VMEM((rows, sz.d), f32),
        ],
        compiler_params=params(4),
        name="give_gradients",
    )(*dws, ends, small, share)


def pack_weights(sz, w_qkv, w_out, w_up, w_down):
    def split(a, to):
        a = a.reshape(sz.wrows, -1, sz.zl, a.shape[-1] // sz.zl)
        a = jnp.moveaxis(a, 2, 0).reshape(sz.zl, sz.wrows, -1)
        return jnp.pad(a, ((0, 0), (0, sz.wrowsp - sz.wrows), (0, to - a.shape[2])))

    attn = jnp.concatenate([w_qkv, w_out[:, None]], axis=1)
    return jnp.concatenate([split(attn, sz.attnp), split(w_up, sz.ffp), split(w_down, sz.ffp)], axis=2)


def unpack_grads(sz, sums):
    sums = sums[:, :sz.wrows]

    def join(a, kinds):
        a = a.reshape(sz.zl, sz.wrows, kinds, -1)
        return jnp.moveaxis(a, 0, 2).reshape(sz.wrows, kinds, -1)

    attn = join(sums[:, :, :4 * sz.wide], 4)
    up = join(sums[:, :, sz.attnp:sz.attnp + sz.ff], 1)[:, 0]
    down = join(sums[:, :, sz.attnp + sz.ffp:sz.attnp + sz.ffp + sz.ff], 1)[:, 0]
    return attn[:, :3], attn[:, 3], up, down


def per_device(mesh, inputs, cotangent, valid_count, norm_gain, norm_bias, w_qkv, bias_qv, w_out, w_up, bias_up,
               w_down, bias_resid):
    sz = Sizes(mesh, inputs, w_qkv, w_up)
    c, t = lax.axis_index("ctx"), lax.axis_index("tp")
    zh, zl = c // sz.zl, c % sz.zl
    slot = zl * sz.tp + t

    def pieces(a):
        a = jnp.pad(a, ((0, 0), (0, sz.tp * sz.part - sz.rows), (0, 0)))
        return lax.dynamic_slice_in_dim(a, t * sz.part, sz.part, axis=1)

    tokens = jnp.stack([pieces(inputs), pieces(cotangent)], axis=1)

    row = jnp.arange(sz.keys, dtype=jnp.int32)
    of_slot, within = row // sz.block, row % sz.block
    token = (of_slot % sz.tp) * sz.part + within % sz.part
    source = (within // sz.part) * sz.zl + of_slot // sz.tp
    position = source * sz.rows + token
    count = lax.dynamic_index_in_dim(valid_count, zh, keepdims=False)
    valid = ((token < sz.rows) & (position < count)).astype(f32)
    own_valid = lax.dynamic_slice_in_dim(valid, slot * sz.block, sz.block)

    packs = [pack_weights(sz, w_qkv[l], w_out[l], w_up[l], w_down[l]) for l in range(sz.layers)]
    *fetched, mine = fetch(sz, packs, tokens)
    weights = [w[:, :sz.wrows].reshape(sz.d, sz.cols) for w in fetched]
    valid = valid[None, :]

    def half(a, to):
        a = lax.dynamic_index_in_dim(a.reshape(a.shape[0], sz.zl, -1), zl, axis=1, keepdims=False)
        return jnp.pad(a, ((0, 0), (0, to - a.shape[1])))

    stream = mine[:, 0].reshape(sz.block, sz.d).astype(f32)
    streams, kept = [], []
    for l in range(sz.layers):
        streams.append(stream)
        stream, *saved = forward(
            sz, stream, weights[l], norm_gain[l], norm_bias[l], half(bias_qv[l], sz.headp),
            half(bias_up[l][None], sz.ffp), bias_resid[l], valid,
        )
        kept.append(saved)
    output = stream.astype(bf16)

    grad = mine[:, 1].reshape(sz.block, sz.d).astype(f32) * own_valid[:, None]
    dws, vecs, dqvs, dups = [[None] * sz.layers for _ in range(4)]
    for l in reversed(range(sz.layers)):
        grad, dws[l], vecs[l], dqvs[l], dups[l] = backward(
            sz, grad, streams[l], kept[l], weights[l], norm_gain[l], valid
        )
    ends = jnp.stack(
        [output.reshape(sz.images, sz.part, sz.d), grad.astype(bf16).reshape(sz.images, sz.part, sz.d)], axis=1
    )
    blocks = [
        jnp.pad(dw.reshape(sz.groups, sz.wrows, sz.cols), ((0, 0), (0, sz.wrowsp - sz.wrows), (0, 0))) for dw in dws
    ]
    small = jnp.concatenate(vecs, axis=0)
    mine_now = (jnp.arange(sz.zl) == zl).astype(f32)[:, None, None]

    def wide(a):
        return jnp.pad(a, ((0, 0), (0, sz.d - a.shape[1])))

    share = jnp.concatenate([jnp.concatenate([wide(dqvs[l]), wide(dups[l])], axis=0) for l in range(sz.layers)], axis=0)
    share = (share[None] * mine_now).reshape(-1, sz.d)
    share = jnp.pad(share, ((0, up_to(share.shape[0], 8) - share.shape[0]), (0, 0)))
    *sums, ends, small, share = give(sz, blocks, ends, small, share)

    ends = jnp.moveaxis(ends, (2, 1), (0, 1))
    ends = ends.reshape(2, sz.images, sz.tp * sz.part, sz.d)[:, :, :sz.rows]
    small = small.reshape(sz.layers, 8, sz.d)
    share = share[:sz.zl * sz.layers * 3].reshape(sz.zl, sz.layers, 3, sz.d)
    grad_qv = jnp.moveaxis(share[:, :, 0:2, :sz.wide], 0, 2).reshape(sz.layers, 2, -1)
    grad_up_bias = jnp.moveaxis(share[:, :, 2, :sz.ff], 0, 1).reshape(sz.layers, -1)
    large = [unpack_grads(sz, s) for s in sums]
    stack = lambda i: jnp.stack([g[i] for g in large])
    return (
        ends[0], ends[1].astype(f32), small[:, 0:2], small[:, 2:4], stack(0), grad_qv, stack(1), stack(2),
        grad_up_bias, stack(3), small[:, 4:6],
    )


def solution(mesh):
    tokens, rows = P("fsdp", "ctx", None), P(None, ("fsdp", "ctx"), "tp")
    qkv = P(None, ("fsdp", "ctx"), None, "tp")
    qv, up = P(None, None, "tp"), P(None, "tp")
    return jax.shard_map(
        functools.partial(per_device, mesh),
        mesh=mesh,
        in_specs=(tokens, tokens, P("fsdp"), P(), P(), qkv, qv, rows, rows, up, rows, P()),
        out_specs=(tokens, tokens, P(), P(), qkv, qv, rows, rows, up, rows, P()),
        check_vma=False,
    )
```

time: 1680 us -> 666 us (0.40)
  waiting for transfers between devices: 1210 us -> 0 us
  Pallas kernels: 0 us -> 588 us
  blocking collectives: 209 us -> 0 us
  matrix products: 130 us -> 0 us
  other arithmetic: 48.3 us -> 20.1 us
    reduce_scatter x12 -> x0, waiting for transfers between devices: 625 us -> none  [the longest x2 145 us: per_device(): lax.psum_scatter(large_grads[3].astype(jnp.bfloat16), ('fsdp', 'ctx'), sc...]
    pallas_call x0 -> x6, Pallas kernels: none -> 588 us  [the longest x1 156 us: give(): pl.pallas_call(functools.partial(give_kernel, sz), out_shape=[jax.ShapeDt...]
    psum x7 -> x0, waiting for transfers between devices: 294 us -> none  [the longest x2 88.3 us: back_layer(): second_grad = lax.psum(second_part, 'tp')]
    all_gather x6 -> x0, waiting for transfers between devices: 290 us -> none  [the longest x2 110 us: fetch_weights(): lax.all_gather(up_rows, ('fsdp', 'ctx'), axis=0, tiled=True)]
    all_gather x6 -> x0, blocking collectives: 171 us -> none  [the longest x2 79 us: fetch_weights(): lax.all_gather(out_rows, ('fsdp', 'ctx'), axis=0, tiled=True)]
    dot_general x34 -> x0, matrix products: 120 us -> none  [the longest x2 10.1 us: run_layer(): jnp.einsum('bcf,df->bcd', hidden, down_full, preferred_element_type=jnp.f...]
    psum x1 -> x0, blocking collectives: 38.9 us -> none  [per_device(): lax.psum(small_grads[0].astype(jnp.bfloat16), ('fsdp', 'ctx'))]
    reduce_sum x21 -> x0, other arithmetic: 20.2 us -> none  [the longest x6 10.5 us: layer_norm(): return centred * lax.rsqrt(spread + norm_eps) * scale_vec + shift_vec]
  transfers between devices with their start and end apart: 25 -> 0, of which waited for: 24 -> 0; matrix products, arithmetic and copies ran while one was open for 7% -> 0% of each run, Pallas kernels for 0% -> 0%
where the time goes in v1:
time: 666 us; the launch traced here: 659 us
  Pallas kernels  588 us (88%)
  local copies, waits for them, and re-layouts  48.9 us (7%)
  other arithmetic  20.1 us (3%)
    pallas_call x1, Pallas kernels, give(): pl.pallas_call(functools.partial(give_kernel, sz), out_shape=[jax.ShapeDt...  156 us
    pallas_call x1, Pallas kernels, fetch(): pl.pallas_call(functools.partial(fetch_kernel, sz), out_shape=[jax.ShapeD...  154 us
    pallas_call x2, Pallas kernels, backward(): pl.pallas_call(functools.partial(backward_kernel, sz), out_shape=[jax.Sha...  147 us
    pallas_call x2, Pallas kernels, forward(): pl.pallas_call(functools.partial(forward_kernel, sz), out_shape=[jax.Shap...  131 us

profile of v1, /device:TPU:0, one launch (start us, length us, event | category | flops | bytes accessed | tf_op | source)
XLA Modules:
  0.0 659.0 jit_solution(14628912990099765878)
XLA Ops:
  0.7 1.4 dynamic_slice.29
  9.7 1.4 slice_bitcast_fusion.10
  21.1 153.8 %fetch_weights.1 = (bf16[8,144,1920]{2,1,0:T(8,128)(2,1)}, bf16[8,144,1920]{2,1,0:T(8,128)(2,1)}, bf16[2,2,48,1152]{3,2,1,0:T(8,128)(2,1)}) custom-call(bf16[2,144,1920]{2,1,0:T(8,128)(2,1)} %fusion.8.refs_0_, bf16[2,144,1920]{2,1,0:T(8,128)(2,1)} %fusion.10.refs_1_, bf16[2,2,48,1152]{3,2,1,0:T(8,128)(2,1)} %pad_maximum_fusion.3.refs_2_), custom_call_target="tpu_custom_call" | custom-call | tf_op jit(solution)/shard_map/fetch_weights/pallas_call | solution.py:617
  177.6 65.4 %layer_forward.2 = (f32[96,1152]{1,0:T(8,128)}, f32[96,1152]{1,0:T(8,128)}, bf16[8,96,1152]{2,1,0:T(8,128)(2,1)}, bf16[8,96,1152]{2,1,0:T(8,128)(2,1)}, bf16[4,1...) custom-call(f32[96,1152]{1,0:T(8,128)} %bitcast_convert_fusion.strea, ...), custom_call_target="tpu_custom_call" | custom-call | tf_op jit(solution)/shard_map/layer_forward/pallas_call | solution.py:500
  243.1 65.9 %layer_forward.3 = (f32[96,1152]{1,0:T(8,128)}, f32[96,1152]{1,0:T(8,128)}, bf16[8,96,1152]{2,1,0:T(8,128)(2,1)}, bf16[8,96,1152]{2,1,0:T(8,128)(2,1)}, bf16[4,1...) custom-call(f32[96,1152]{1,0:T(8,128)} %get-tuple-element.51.stream_, ...), custom_call_target="tpu_custom_call" | custom-call | tf_op jit(solution)/shard_map/layer_forward/pallas_call | solution.py:500
  309.0 74.0 %layer_backward.2 = (f32[96,1152]{1,0:T(8,128)}, bf16[1152,1920]{1,0:T(8,128)(2,1)}, f32[8,1152]{1,0:T(8,128)}, f32[2,256]{1,0:T(2,128)}, f32[1,640]{1,0:T(1,128)}) custom-call(f32[96,1152]{1,0:T(8,128)} %convert_multiply_fusion.grad_ref, f32[96,1152]{1,0:T(8,128)} %get-tuple-element.51.stream_ref, f32[96,1152]{1,0:T(8,128)} %get-tuple-element.53.middle_ref, ...), custom_call_target="tpu_custom_call" | custom-call | tf_op jit(solution)/shard_map/layer_backward/pallas_call | solution.py:516
  383.0 72.8 %layer_backward.3 = (f32[96,1152]{1,0:T(8,128)}, bf16[1152,1920]{1,0:T(8,128)(2,1)}, f32[8,1152]{1,0:T(8,128)}, f32[2,256]{1,0:T(2,128)}, f32[1,640]{1,0:T(1,128)}) custom-call(f32[96,1152]{1,0:T(8,128)} %get-tuple-element.62.grad_ref, f32[96,1152]{1,0:T(8,128)} %bitcast_convert_fusion.stream_ref, f32[96,1152]{1,0:T(8,128)} %get-tuple-element.63.middle_ref, ...), custom_call_target="tpu_custom_call" | custom-call | tf_op jit(solution)/shard_map/layer_backward/pallas_call | solution.py:516
  457.3 1.4 pad_maximum_fusion.6.refs_3_
  460.6 156.4 %give_gradients.1 = (f32[2,144,1920]{2,1,0:T(8,128)}, f32[2,144,1920]{2,1,0:T(8,128)}, bf16[4,2,2,48,1152]{4,3,2,1,0:T(8,128)(2,1)}, f32[16,1152]{1,0:T(8,128)}, f32[16,1152]{1,0:T(8,128)}) custom-call(bf16[8,144,1920]{2,1,0:T(8,128)(2,1)} %bitcast.132, bf16[8,144,1920]{2,1,0:T(8,128)(2,1)} %bitcast.131, bf16[2,2,48,1152]{3,2,1,0:T(8,128)(2,1)} %pad_maximum_fusion.4.refs_2_, ...), custom_call_target="tpu_custom_call" | custom-call | tf_op jit(solution)/shard_map/give_gradients/pallas_call | solution.py:771
  617.1 1.7 copy.60
  620.9 2.0 slice.143
  622.9 2.3 slice_bitcast_fusion.3
  625.6 1.3 stack_squeeze_reshape.14
  626.9 1.9 reshape.305
  628.9 1.9 copy.61
  630.8 2.3 reshape.306
  636.5 2.0 slice.145
  638.5 2.3 slice_bitcast_fusion.2
  642.5 2.2 pad_maximum_fusion.2
  644.7 1.9 reshape.307
  646.7 1.9 copy.62
  648.6 2.3 reshape.308
  654.7 2.2 pad_maximum_fusion.1
  657.0 1.6 fusion.11
  (113 shorter events, 34.7 us)
Async XLA Ops:
  0.6 12.1 %copy-start.7 = (bf16[2,184,1152]{2,1,0:T(8,128)(2,1)S(1)}, bf16[2,184,1152]{2,1,0:T(8,128)(2,1)}, u32[]{:S(2)}) copy-start(bf16[2,184,1152]{2,1,0:T(8,128)(2,1)} %param.13) | copy-start | bytes 2543620
  0.7 12.1 %copy-start.6 = (bf16[2,184,1152]{2,1,0:T(8,128)(2,1)S(1)}, bf16[2,184,1152]{2,1,0:T(8,128)(2,1)}, u32[]{:S(2)}) copy-start(bf16[2,184,1152]{2,1,0:T(8,128)(2,1)} %param.12) | copy-start | bytes 2543620
  12.5 1.1 copy-start.8
  15.6 1.5 copy-start.9
  16.6 1.2 copy-start.10
  383.0 72.8 %copy-start.15 = (f32[1,640]{1,0:T(1,128)S(1)}, f32[1,640]{1,0:T(1,128)}, u32[]{:S(2)}) copy-start(f32[1,640]{1,0:T(1,128)} %get-tuple-element.81) | copy-start | bytes 7684
  383.0 72.8 %copy-start.16 = (f32[2,256]{1,0:T(2,128)S(1)}, f32[2,256]{1,0:T(2,128)}, u32[]{:S(2)}) copy-start(f32[2,256]{1,0:T(2,128)} %get-tuple-element.80) | copy-start | bytes 6148
  383.0 74.3 %copy-start.14 = (f32[8,1152]{1,0:T(8,128)S(1)}, f32[8,1152]{1,0:T(8,128)}, u32[]{:S(2)}) copy-start(f32[8,1152]{1,0:T(8,128)} %get-tuple-element.77) | copy-start | bytes 110596
  455.8 4.0 copy-start.11
  617.1 1.7 copy-start.13
  617.1 2.3 copy-start.12
  630.8 3.9 copy-start.1
  640.8 1.7 copy-start.4
  648.6 2.4 copy-start.3
  651.0 1.2 copy-start.5
  651.1 2.0 copy-start
  652.2 2.5 copy-start.2

commit v2 on v1

v2 whole, which is shorter than its diff:
```python
import functools

import jax
import jax.numpy as jnp
from jax import lax
from jax.experimental import pallas as pl
from jax.experimental.pallas import tpu as pltpu
from jax.sharding import PartitionSpec as P

HEAD_DIM = 72
norm_eps = 1e-06
gelu_root = 0.7978845608028654
gelu_cubic = 0.044715
masked_score = -1e30

MESH = pl.DeviceIdType.MESH
f32 = jnp.float32
bf16 = jnp.bfloat16
VMEM = pltpu.VMEM
DMA = pltpu.SemaphoreType.DMA


def up_to(value, unit):
    return (value + unit - 1) // unit * unit


def dot(a, b, over):
    return lax.dot_general(a, b, (((over[0],), (over[1],)), ((), ())), preferred_element_type=f32)


class Sizes:
    def __init__(self, mesh, inputs, w_qkv, w_up):
        self.fsdp, self.ctx, self.tp = mesh.shape["fsdp"], mesh.shape["ctx"], mesh.shape["tp"]
        self.images, self.rows, self.d = inputs.shape
        self.layers, self.wrows = w_qkv.shape[0], w_qkv.shape[1]
        self.zl = self.ctx // self.images
        self.chips_y = self.tp // 2
        self.chips = self.zl * self.chips_y
        self.team = self.chips * 2
        self.part = up_to(-(-self.rows // self.tp), 16)
        self.block = self.images * self.part
        self.tile = 2 * self.block
        self.keys = self.chips * self.tile
        self.wide = w_qkv.shape[3] // self.zl
        self.heads = self.wide // HEAD_DIM
        self.ff = w_up.shape[2] // self.zl
        self.ffw = up_to(2 * self.ff, 128)
        self.down_at = self.ff // 128 * 128
        self.down_shift = self.ff - self.down_at
        self.ffp = self.ffw - self.down_at
        self.headp = up_to(self.wide, 128)
        self.qkvp = up_to(3 * self.wide, 128)
        self.attnp = up_to(4 * self.wide, 128)
        self.wrowsp = up_to(self.wrows, 16)
        self.groups = self.fsdp * self.ctx


class Place:
    def __init__(self, sz):
        self.sz = sz
        self.f, self.c, self.t = lax.axis_index("fsdp"), lax.axis_index("ctx"), lax.axis_index("tp")
        self.zh, self.zl = self.c // sz.zl, self.c % sz.zl
        self.y, self.k = self.t // 2, self.t % 2
        self.chip = self.zl * sz.chips_y + self.y
        self.slot = 2 * self.chip + self.k

    def chip_at(self, step):
        sz = self.sz
        zl = (self.zl + step // sz.chips_y) % sz.zl
        y = (self.y + step % sz.chips_y) % sz.chips_y
        return zl, y

    def chip_back(self, step):
        sz = self.sz
        zl = (self.zl + sz.zl - step // sz.chips_y) % sz.zl
        y = (self.y + sz.chips_y - step % sz.chips_y) % sz.chips_y
        return zl, y

    def index(self, chip):
        return chip[0] * self.sz.chips_y + chip[1]

    def device(self, chip):
        return (self.f, self.zh * self.sz.zl + chip[0], 2 * chip[1] + self.k)

    @property
    def twin(self):
        return (self.f, self.c, self.t + 1 - 2 * self.k)


    def ctx_ahead(self, step):
        sz = self.sz
        return (self.zh + step // sz.zl) % sz.images * sz.zl + (self.zl + step % sz.zl) % sz.zl

    def ctx_back(self, step):
        sz = self.sz
        zh = (self.zh + sz.images - step // sz.zl) % sz.images
        return zh * sz.zl + (self.zl + sz.zl - step % sz.zl) % sz.zl


def greet(others):
    barrier = pltpu.get_barrier_semaphore()
    for other in others:
        pl.semaphore_signal(barrier, inc=1, device_id=other, device_id_type=MESH)
    pl.semaphore_wait(barrier, len(others))


def send(src, dst, send_sem, recv_sem, device):
    return pltpu.make_async_remote_copy(
        src_ref=src, dst_ref=dst, send_sem=send_sem, recv_sem=recv_sem, device_id=device, device_id_type=MESH
    )


def team_peers(pc):
    return [pc.device(pc.chip_at(step)) for step in range(1, pc.sz.chips)] + [pc.twin]


def weight_peers(pc, team=False):
    sz = pc.sz
    first = sz.zl if team else 1
    return [(pc.f, pc.ctx_ahead(step), pc.t) for step in range(first, sz.ctx)] + [
        ((pc.f + jump) % sz.fsdp, pc.c, pc.t) for jump in range(1, sz.fsdp)
    ]


class Gather:
    def __init__(self, pc, buf, sems, at):
        self.pc, self.buf, self.sems, self.at = pc, buf, sems, at

    def far(self, step, slot, device):
        return send(self.buf.at[slot], self.buf.at[slot], self.sems.at[self.at, 0, step],
                    self.sems.at[self.at, 1, step], device)

    def near(self, step, slot):
        return send(self.buf.at[slot], self.buf.at[slot], self.sems.at[self.at, 2, step],
                    self.sems.at[self.at, 3, step], self.pc.twin)

    def start(self):
        pc = self.pc
        for step in range(1, pc.sz.chips):
            self.far(step, pc.slot, pc.device(pc.chip_at(step))).start()
        self.near(0, pc.slot).start()

    def arrive(self, step):
        pc = self.pc
        chip = pc.chip_back(step)
        at = pc.index(chip)

        @pl.when(step > 0)
        def _():
            self.far(step, 2 * at + pc.k, pc.device(chip)).wait_recv()
            self.near(step, 2 * at + pc.k).start()

        self.near(step, 2 * at + 1 - pc.k).wait_recv()
        return at

    def finish(self):
        pc = self.pc
        for step in range(pc.sz.chips):
            if step:
                self.far(step, pc.slot, pc.device(pc.chip_at(step))).wait_send()
            self.near(step, pc.slot).wait_send()


class Scatter:
    def __init__(self, pc, bufs, sems, at):
        self.pc, self.sems, self.at = pc, sems, at
        self.both, self.keep, self.tsend, self.trecv, self.rsend, self.rrecv = bufs

    def near(self, step):
        return send(self.tsend.at[step], self.trecv.at[step], self.sems.at[self.at, 0, step],
                    self.sems.at[self.at, 1, step], self.pc.twin)

    def far(self, step):
        return send(self.rsend.at[step], self.rrecv.at[step], self.sems.at[self.at, 2, step],
                    self.sems.at[self.at, 3, step], self.pc.device(self.pc.chip_back(step)))

    def push(self, step, partial):
        pc, block = self.pc, self.pc.sz.block
        self.both[...] = partial.reshape(2, block, partial.shape[-1])
        self.tsend[step] = self.both[1 - pc.k].astype(bf16)
        self.near(step).start()
        self.keep[step] = self.both[pc.k]

        @pl.when(step > 0)
        def _():
            self.relay(step - 1)

    def relay(self, step):
        self.near(step).wait_recv()
        total = self.keep[step] + self.trecv[step].astype(f32)

        def own():
            self.keep[0] = total

        def other():
            self.rsend[step] = total.astype(bf16)
            self.far(step).start()

        if isinstance(step, int):
            own() if step == 0 else other()
        else:
            pl.when(step == 0)(own)
            pl.when(step > 0)(other)

    def flush(self):
        self.relay(self.pc.sz.chips - 1)

    def finish(self):
        total = self.keep[0]
        for step in range(1, self.pc.sz.chips):
            self.far(step).wait_recv()
            total = total + self.rrecv[step].astype(f32)
        for step in range(self.pc.sz.chips):
            self.near(step).wait_send()
            if step:
                self.far(step).wait_send()
        return total


def team_scratch(sz, gathers, scatters):
    n = sz.chips
    return [
        VMEM((2, sz.block, sz.d), f32),
        VMEM((n, sz.block, sz.d), f32),
        VMEM((n, sz.block, sz.d), bf16),
        VMEM((n, sz.block, sz.d), bf16),
        VMEM((n, sz.block, sz.d), bf16),
        VMEM((n, sz.block, sz.d), bf16),
        DMA((gathers, 4, n)),
        DMA((scatters, 4, n)),
    ]


def normalised(values):
    centre = jnp.mean(values, axis=-1, keepdims=True)
    centred = values - centre
    spread = jnp.mean(centred * centred, axis=-1, keepdims=True)
    inverse = lax.rsqrt(spread + norm_eps)
    return centred * inverse, inverse


def norm_back(values, gain, grad):
    high, inverse = normalised(values)
    scaled = grad * gain
    term = inverse * (
        scaled
        - jnp.mean(scaled, axis=-1, keepdims=True)
        - high * jnp.mean(scaled * high, axis=-1, keepdims=True)
    )
    return term, jnp.sum(grad * high, axis=0, keepdims=True), jnp.sum(grad, axis=0, keepdims=True)


def lanes_of(shape):
    return lax.broadcasted_iota(jnp.int32, shape, len(shape) - 1)


def unpack_out(sz, w_ref, o_ref):
    at = 3 * sz.wide // 128 * 128
    shift = 3 * sz.wide - at

    def step(i, carry):
        rows = pl.ds(pl.multiple_of(i * 128, 128), 128)
        piece = pltpu.roll(w_ref[rows, at:at + sz.headp].astype(f32), sz.headp - shift, 1)
        o_ref[rows, :] = jnp.where(lanes_of(piece.shape) < sz.wide, piece, 0.0).astype(bf16)
        return carry

    lax.fori_loop(0, sz.d // 128, step, 0)


def take(sz, values, kind):
    at = kind * sz.wide // 128 * 128
    shift = kind * sz.wide - at
    piece = values[:, at:at + sz.headp]
    if shift:
        piece = pltpu.roll(piece, sz.headp - shift, 1)
    return jnp.where(lanes_of(piece.shape) < sz.wide, piece, 0.0)


def head_of(values, head):
    lanes = lanes_of(values.shape)
    mine = (lanes >= head * HEAD_DIM) & (lanes < (head + 1) * HEAD_DIM)
    return jnp.where(mine, values, jnp.zeros_like(values))


def probabilities(q_head, keys, valid):
    scores = dot(q_head, keys, (1, 1)) * HEAD_DIM ** (-0.5)
    scores = jnp.where(valid > 0.0, scores, masked_score)
    weights = jnp.exp(scores - jnp.max(scores, axis=-1, keepdims=True))
    return weights / jnp.sum(weights, axis=-1, keepdims=True)


class Fetch:
    def __init__(self, pc, own, everything, sems):
        self.pc, self.own, self.all, self.sems = pc, own, everything, sems
        self.parts = [self.start, self.pass_own] + [
            functools.partial(self.pass_on, step) for step in range(1, pc.sz.ctx)
        ]

    def along_ctx(self, step):
        pc = self.pc
        c = pc.ctx_ahead(step)
        return send(self.own.at[c % pc.sz.zl], self.all.at[pc.f * pc.sz.ctx + pc.c], self.sems.at[0, 0, step],
                    self.sems.at[0, 1, step], (pc.f, c, pc.t))

    def own_copy(self):
        pc = self.pc
        return pltpu.make_async_copy(self.own.at[pc.zl], self.all.at[pc.f * pc.sz.ctx + pc.c], self.sems.at[0, 0, 0])

    def along_fsdp(self, jump, step):
        pc, sz = self.pc, self.pc.sz
        at = pc.f * sz.ctx + pc.ctx_back(step)
        return send(self.all.at[at], self.all.at[at], self.sems.at[jump, 0, step], self.sems.at[jump, 1, step],
                    ((pc.f + jump) % sz.fsdp, pc.c, pc.t))

    def start(self):
        self.own_copy().start()
        for step in range(1, self.pc.sz.ctx):
            self.along_ctx(step).start()

    def pass_own(self):
        self.own_copy().wait()
        for jump in range(1, self.pc.sz.fsdp):
            self.along_fsdp(jump, 0).start()

    def pass_on(self, step):
        self.along_ctx(step).wait_recv()
        for jump in range(1, self.pc.sz.fsdp):
            self.along_fsdp(jump, step).start()

    def finish(self):
        sz = self.pc.sz
        for step in range(sz.ctx):
            if step:
                self.along_ctx(step).wait_send()
            for jump in range(1, sz.fsdp):
                self.along_fsdp(jump, step).wait()

    @staticmethod
    def result(sz, cols):
        return [((sz.groups, sz.wrowsp, cols), bf16)]

    @staticmethod
    def scratch(sz, cols):
        return [DMA((sz.fsdp, 2, sz.ctx))]


class Give:
    def __init__(self, pc, dw, out, got, total, recv, sems):
        self.pc, self.dw, self.out = pc, dw, out
        self.got, self.total, self.recv, self.sems = got, total, recv, sems
        self.order = list(range(pc.sz.ctx - 1, -1, -1))
        self.parts = [self.start] + [functools.partial(self.pass_on, step) for step in self.order]

    def along_fsdp(self, jump, step):
        pc, sz = self.pc, self.pc.sz
        f = (pc.f + jump) % sz.fsdp
        return send(self.dw.at[f * sz.ctx + pc.ctx_ahead(step)], self.got.at[jump - 1, step],
                    self.sems.at[jump, 0, step], self.sems.at[jump, 1, step], (f, pc.c, pc.t))

    def along_ctx(self, step):
        pc = self.pc
        return send(self.total.at[step], self.recv.at[pc.c], self.sems.at[0, 0, step], self.sems.at[0, 1, step],
                    (pc.f, pc.ctx_ahead(step), pc.t))

    def from_ctx(self, step):
        pc = self.pc
        return send(self.total.at[step], self.recv.at[pc.ctx_back(step)], self.sems.at[0, 0, step],
                    self.sems.at[0, 1, step], (pc.f, pc.ctx_back(step), pc.t))

    def start(self):
        for step in self.order:
            for jump in range(1, self.pc.sz.fsdp):
                self.along_fsdp(jump, step).start()

    def pass_on(self, step):
        pc, sz = self.pc, self.pc.sz
        for jump in range(1, sz.fsdp):
            self.along_fsdp(jump, step).wait_recv()
        total = self.dw[pc.f * sz.ctx + pc.ctx_ahead(step)].astype(f32)
        for jump in range(1, sz.fsdp):
            total = total + self.got[jump - 1, step].astype(f32)
        if step:
            self.total[step] = total.astype(bf16)
            self.along_ctx(step).start()
        else:
            self.recv[pc.c] = total.astype(bf16)

    def finish(self):
        pc, sz = self.pc, self.pc.sz
        for step in range(1, sz.ctx):
            self.from_ctx(step).wait_recv()
        for j in range(sz.zl):
            total = self.recv[j].astype(f32)
            for zh in range(1, sz.images):
                total = total + self.recv[zh * sz.zl + j].astype(f32)
            self.out[j] = total
        for step in range(sz.ctx):
            if step:
                self.along_ctx(step).wait_send()
            for jump in range(1, sz.fsdp):
                self.along_fsdp(jump, step).wait_send()

    @staticmethod
    def result(sz, cols):
        return [((sz.zl, sz.wrowsp, cols), f32)]

    @staticmethod
    def scratch(sz, cols):
        return [
            VMEM((max(sz.fsdp - 1, 1), sz.ctx, sz.wrowsp, cols), bf16),
            VMEM((sz.ctx, sz.wrowsp, cols), bf16),
            VMEM((sz.ctx, sz.wrowsp, cols), bf16),
            DMA((sz.fsdp, 2, sz.ctx)),
        ]


class Beside:
    def __init__(self, pc, mover, refs):
        self.mover = mover(pc, *refs) if mover else None

    def part(self, index):
        if self.mover:
            self.mover.parts[index]()

    def rest(self, first):
        if self.mover:
            for part in self.mover.parts[first:]:
                part()

    def at(self, step, places):
        if self.mover:
            for when, index in places.items():
                pl.when(step == when)(functools.partial(self.part, index))

    def finish(self):
        if self.mover:
            self.mover.finish()


def split_refs(refs, *counts):
    out, at = [], 0
    for count in counts:
        out.append(refs[at:at + count])
        at += count
    assert at == len(refs)
    return out


def layer_kernel(body, ins, outs, scratch, gathers, scatters, mover, sz, *refs):
    m = 1 if mover else 0
    own, team = len(scratch), 8
    rest = len(refs) - ins - m - outs - m - own - team
    a, ma, b, mb, s, t, ms = split_refs(refs, ins, m, outs, m, own, team, rest)
    pc = Place(sz)
    greet(team_peers(pc) + (weight_peers(pc, True) if mover else []))
    body(sz, pc, Beside(pc, mover, (*ma, *mb, *ms)), *a, *b, *s, t[:6], t[6], t[7])


def layer_call(sz, name, ident, body, operands, shapes, scratch, gathers, scatters, mover=None, extra=None):
    cols = extra.shape[-1] if mover else 0
    results = list(shapes) + (mover.result(sz, cols) if mover else [])
    n_in = len(operands) + (1 if mover else 0)
    return pl.pallas_call(
        functools.partial(layer_kernel, body, len(operands), len(shapes), scratch, gathers, scatters, mover, sz),
        out_shape=[jax.ShapeDtypeStruct(*s) for s in results],
        in_specs=whole(n_in),
        out_specs=whole(len(results)),
        scratch_shapes=scratch + team_scratch(sz, gathers, scatters) + (mover.scratch(sz, cols) if mover else []),
        compiler_params=params(ident),
        name=name,
    )(*operands, *([extra] if mover else []))


def whole(ref_count):
    return [pl.BlockSpec(memory_space=pltpu.VMEM)] * ref_count


def params(collective_id):
    return pltpu.CompilerParams(
        collective_id=collective_id, has_side_effects=True, vmem_limit_bytes=60 * 1024 * 1024
    )


def attn_forward(sz, pc, beside, stream_ref, w_ref, gain_ref, shift_ref, qv_ref, resid_ref, valid_ref,
                 middle_ref, n1_ref, q_ref, k_ref, v_ref, mixed_ref, o_ref, bufs, gsems, ssems):
    gather = Gather(pc, n1_ref, gsems, 0)
    high, _ = normalised(stream_ref[...])
    n1_ref[pc.slot] = (high * gain_ref[0:1, :] + shift_ref[0:1, :]).astype(bf16)
    gather.start()
    beside.part(0)
    unpack_out(sz, w_ref, o_ref)
    beside.part(1)

    def project(step, carry):
        at = gather.arrive(step)
        tokens = n1_ref[pl.ds(2 * at, 2)].reshape(sz.tile, sz.d)
        both3 = dot(tokens, w_ref[:, 0:sz.qkvp], (1, 0))
        q_ref[at] = (take(sz, both3, 0) + qv_ref[0:1, :]).astype(bf16)
        k_ref[at] = take(sz, both3, 1).astype(bf16)
        v_ref[at] = (take(sz, both3, 2) + qv_ref[1:2, :]).astype(bf16)
        return carry

    lax.fori_loop(0, sz.chips, project, 0)
    gather.finish()
    scatter = Scatter(pc, bufs, ssems, 0)

    def attend(step, carry):
        at = pc.index(pc.chip_back(step))
        keys = k_ref[...].reshape(sz.keys, sz.headp)
        values = v_ref[...].reshape(sz.keys, sz.headp)
        queries = q_ref[at]
        total = jnp.zeros((sz.tile, sz.headp), f32)
        for head in range(sz.heads):
            probs = probabilities(head_of(queries, head), keys, valid_ref[...])
            total = total + dot(probs.astype(bf16), head_of(values, head), (1, 0))
        mixed = total.astype(bf16)
        mixed_ref[at] = mixed
        scatter.push(step, dot(mixed, o_ref[...], (1, 1)))
        beside.at(step, {sz.chips - 1: 2})
        return carry

    lax.fori_loop(0, sz.chips, attend, 0)
    scatter.flush()
    beside.rest(3)
    middle_ref[...] = stream_ref[...] + (scatter.finish() + resid_ref[0:1, :])
    beside.finish()


def ff_forward(sz, pc, beside, middle_ref, w_ref, gain_ref, shift_ref, upb_ref, resid_ref,
               out_ref, n2_ref, pre_ref, hidden_ref, bufs, gsems, ssems):
    gather = Gather(pc, n2_ref, gsems, 0)
    high, _ = normalised(middle_ref[...])
    n2_ref[pc.slot] = (high * gain_ref[1:2, :] + shift_ref[1:2, :]).astype(bf16)
    gather.start()
    beside.part(0)
    beside.part(1)
    scatter = Scatter(pc, bufs, ssems, 0)

    def feed(step, carry):
        at = gather.arrive(step)
        tokens = n2_ref[pl.ds(2 * at, 2)].reshape(sz.tile, sz.d)
        pre = dot(tokens, w_ref[:, 0:sz.ffp], (1, 0)) + upb_ref[...]
        pre_ref[at] = pre
        hidden = 0.5 * pre * (1.0 + jnp.tanh(gelu_root * (pre + gelu_cubic * pre * pre * pre)))
        hidden = jnp.where(lanes_of(hidden.shape) < sz.ff, hidden, 0.0)
        if sz.down_shift:
            hidden = pltpu.roll(hidden, sz.down_shift, 1)
        hidden = hidden.astype(bf16)
        hidden_ref[at] = hidden
        scatter.push(step, dot(hidden, w_ref[:, sz.down_at:], (1, 1)))
        beside.at(step, {sz.chips - 1: 2})
        return carry

    lax.fori_loop(0, sz.chips, feed, 0)
    scatter.flush()
    gather.finish()
    beside.rest(3)
    out_ref[...] = middle_ref[...] + (scatter.finish() + resid_ref[1:2, :])
    beside.finish()


def ff_backward(sz, pc, beside, grad_ref, middle_ref, n2_ref, pre_ref, hidden_ref, w_ref, gain_ref,
                gmid_ref, dw_ref, vec_ref, dup_ref, gl_ref, pg_ref, bufs, gsems, ssems):
    span = 384 if sz.d % 384 == 0 else 128
    gather = Gather(pc, gl_ref, gsems, 0)
    grad_low = grad_ref[...].astype(bf16)
    gl_ref[pc.slot] = grad_low
    gather.start()
    beside.part(0)
    vec_ref[...] = jnp.zeros_like(vec_ref)
    vec_ref[2:3, :] = jnp.sum(grad_low.astype(f32), axis=0, keepdims=True)
    scatter = Scatter(pc, bufs, ssems, 0)
    dup_ref[...] = jnp.zeros_like(dup_ref)

    def feed(step, carry):
        at = gather.arrive(step)
        grads = gl_ref[pl.ds(2 * at, 2)].reshape(sz.tile, sz.d)
        back = dot(grads, w_ref[:, sz.down_at:], (1, 0))
        if sz.down_shift:
            back = pltpu.roll(back, sz.ffp - sz.down_shift, 1)
        pre = pre_ref[at]
        bent = jnp.tanh(gelu_root * (pre + gelu_cubic * pre * pre * pre))
        slope = 0.5 * (1.0 + bent) + 0.5 * pre * (1.0 - bent * bent) * (
            gelu_root * (1.0 + 3.0 * gelu_cubic * pre * pre)
        )
        pre_grad = jnp.where(lanes_of(back.shape) < sz.ff, back * slope, 0.0).astype(bf16)
        pg_ref[at] = pre_grad
        dup_ref[...] += jnp.sum(pre_grad.astype(f32), axis=0, keepdims=True)
        scatter.push(step, dot(pre_grad, w_ref[:, 0:sz.ffp], (1, 1)))
        beside.at(step, {sz.chips - 2: 1, sz.chips - 1: 2})
        return carry

    lax.fori_loop(0, sz.chips, feed, 0)
    scatter.flush()
    beside.rest(3)

    def grads_ff(i, carry):
        lanes = pl.ds(pl.multiple_of(i * span, 128), span)
        hidden = hidden_ref[...].reshape(sz.keys, sz.ffp)
        down = dot(gl_ref[:, :, lanes].reshape(sz.keys, span), hidden, (0, 0))
        pre_grad = pg_ref[...].reshape(sz.keys, sz.ffp)
        up = dot(n2_ref[:, :, lanes].reshape(sz.keys, span), pre_grad, (0, 0))
        dw_ref[lanes, 0:sz.down_at] = up[:, 0:sz.down_at].astype(bf16)
        over = sz.ffp - sz.down_at
        if over:
            dw_ref[lanes, sz.down_at:sz.ffp] = (up[:, sz.down_at:] + down[:, 0:over]).astype(bf16)
        dw_ref[lanes, sz.ffp:] = down[:, over:].astype(bf16)
        return carry

    lax.fori_loop(0, sz.d // span, grads_ff, 0)
    gather.finish()
    second = scatter.finish()
    term, dgain, dshift = norm_back(middle_ref[...], gain_ref[1:2, :], second)
    vec_ref[0:1, :] = dgain
    vec_ref[1:2, :] = dshift
    gmid_ref[...] = grad_ref[...] + term
    beside.finish()


def attn_backward(sz, pc, beside, gmid_ref, stream_ref, n1_ref, q_ref, k_ref, v_ref, mixed_ref, w_ref, gain_ref,
                  valid_ref, below_ref, dw_ref, vec_ref, dqv_ref,
                  o_ref, ml_ref, mg_ref, dk_ref, dv_ref, stack_ref, bufs, gsems, ssems):
    span = 384 if sz.d % 384 == 0 else 128
    gather = Gather(pc, ml_ref, gsems, 0)
    mid_low = gmid_ref[...].astype(bf16)
    ml_ref[pc.slot] = mid_low
    gather.start()
    beside.part(0)
    vec_ref[...] = jnp.zeros_like(vec_ref)
    vec_ref[2:3, :] = jnp.sum(mid_low.astype(f32), axis=0, keepdims=True)
    unpack_out(sz, w_ref, o_ref)

    def mix(step, carry):
        at = gather.arrive(step)
        grads = ml_ref[pl.ds(2 * at, 2)].reshape(sz.tile, sz.d)
        mg_ref[at] = dot(grads, o_ref[...], (1, 0)).astype(bf16)
        return carry

    lax.fori_loop(0, sz.chips, mix, 0)
    gather.finish()
    beside.part(1)
    dk_ref[...] = jnp.zeros_like(dk_ref)
    dv_ref[...] = jnp.zeros_like(dv_ref)
    dqv_ref[...] = jnp.zeros_like(dqv_ref)
    scale = HEAD_DIM ** (-0.5)

    def attend(at, carry):
        keys = k_ref[...].reshape(sz.keys, sz.headp)
        values = v_ref[...].reshape(sz.keys, sz.headp)
        total = jnp.zeros((sz.tile, sz.headp), f32)
        for head in range(sz.heads):
            q_head = head_of(q_ref[at], head)
            g_head = head_of(mg_ref[at], head)
            probs = probabilities(q_head, keys, valid_ref[...])
            dprobs = dot(g_head, values, (1, 1))
            inner = jnp.sum(probs * dprobs, axis=-1, keepdims=True)
            dscores = (probs * (dprobs - inner)).astype(bf16)
            total = total + dot(dscores, head_of(keys, head), (1, 0))
            dk_ref[...] += dot(dscores, q_head, (0, 0))
            dv_ref[...] += dot(probs.astype(bf16), g_head, (0, 0))
        dq = (scale * total).astype(bf16).astype(f32)
        dqv_ref[0:1, :] += jnp.sum(dq, axis=0, keepdims=True)
        stack_ref[at, :, 0:sz.headp] = dq.astype(bf16)
        beside.at(at, {1: 2, 3: 3})
        return carry

    lax.fori_loop(0, sz.chips, attend, 0)
    beside.rest(4)
    scatter = Scatter(pc, bufs, ssems, 0)

    def back_project(step, carry):
        at = pc.index(pc.chip_back(step))
        rows = pl.ds(pl.multiple_of(at * sz.tile, sz.tile), sz.tile)
        dk = (scale * dk_ref[rows, :]).astype(bf16).astype(f32)
        dv = dv_ref[rows, :].astype(bf16).astype(f32)
        dqv_ref[1:2, :] += jnp.sum(dv, axis=0, keepdims=True)
        dq = stack_ref[at, :, 0:sz.headp].astype(f32)
        total = jnp.pad(dq, ((0, 0), (0, sz.qkvp - sz.headp)))
        for kind, piece in ((1, dk), (2, dv)):
            start = kind * sz.wide // 128 * 128
            shift = kind * sz.wide - start
            moved = pltpu.roll(piece, shift, 1) if shift else piece
            total = total + jnp.pad(moved, ((0, 0), (start, sz.qkvp - start - sz.headp)))
        stacked = total.astype(bf16)
        stack_ref[at] = stacked
        scatter.push(step, dot(stacked, w_ref[:, 0:sz.qkvp], (1, 1)))
        return carry

    lax.fori_loop(0, sz.chips, back_project, 0)
    scatter.flush()
    o_at = 3 * sz.wide // 128 * 128
    o_shift = 3 * sz.wide - o_at

    def grads_attn(i, carry):
        lanes = pl.ds(pl.multiple_of(i * span, 128), span)
        stacked = stack_ref[...].reshape(sz.keys, sz.qkvp)
        dqkv = dot(n1_ref[:, :, lanes].reshape(sz.keys, span), stacked, (0, 0))
        mixed = mixed_ref[...].reshape(sz.keys, sz.headp)
        dout = dot(ml_ref[:, :, lanes].reshape(sz.keys, span), mixed, (0, 0))
        if o_shift:
            dout = pltpu.roll(dout, o_shift, 1)
        total = jnp.pad(dqkv, ((0, 0), (0, sz.attnp - sz.qkvp))) + jnp.pad(
            dout, ((0, 0), (o_at, sz.attnp - o_at - sz.headp))
        )
        dw_ref[lanes, 0:sz.attnp] = total.astype(bf16)
        return carry

    lax.fori_loop(0, sz.d // span, grads_attn, 0)
    first = scatter.finish()
    term, dgain, dshift = norm_back(stream_ref[...], gain_ref[0:1, :], first)
    vec_ref[0:1, :] = dgain
    vec_ref[1:2, :] = dshift
    below_ref[...] = gmid_ref[...] + term
    beside.finish()


def shift_lanes(values, start, count, at, width):
    have = values.shape[-1]
    first, last = start // 128 * 128, up_to(start + count, 128)
    to = at // 128 * 128
    span = max(last - first, up_to(at + count, 128) - to)
    piece = values[:, first:min(last, have)].astype(f32)
    if piece.shape[-1] < span:
        piece = jnp.pad(piece, ((0, 0), (0, span - piece.shape[-1])))
    turn = ((at - to) - (start - first)) % span
    if turn:
        piece = pltpu.roll(piece, turn, 1)
    lanes = lanes_of(piece.shape)
    piece = jnp.where((lanes >= at - to) & (lanes < at - to + count), piece, 0.0)
    piece = piece[:, 0:min(span, width - to)]
    return jnp.pad(piece, ((0, 0), (to, width - to - piece.shape[-1])))


def open_kernel(sz, wqkv_ref, wout_ref, wup_ref, wdown_ref, tokens_ref, valid_ref, *refs):
    n = sz.layers
    everything, attn_refs, ff_refs, (stream_ref, grad_ref), (attn0_ref, mine_ref, tsems, wsems) = split_refs(
        refs, 1, n - 1, n, 2, 4
    )
    attn_refs = [attn0_ref] + list(attn_refs)
    pc = Place(sz)
    greet(weight_peers(pc))

    def swap(step):
        zh = (pc.zh + step) % sz.images
        return send(tokens_ref.at[zh], mine_ref.at[pc.zh], tsems.at[0, step], tsems.at[1, step],
                    (pc.f, zh * sz.zl + pc.zl, pc.t))

    def pack(ref, half, pieces):
        total = None
        for values, start, count, at in pieces:
            piece = shift_lanes(values, start, count, at, ref.shape[-1])
            total = piece if total is None else total + piece
        ref[half, 0:sz.wrows, :] = total.astype(bf16)
        if sz.wrowsp > sz.wrows:
            ref[half, sz.wrows:, :] = jnp.zeros((sz.wrowsp - sz.wrows, ref.shape[-1]), bf16)

    def pack_attn(layer):
        full = sz.wide * sz.zl
        for half in range(sz.zl):
            pieces = [(wqkv_ref[layer], kind * full + half * sz.wide, sz.wide, kind * sz.wide) for kind in range(3)]
            pack(attn_refs[layer], half, pieces + [(wout_ref[layer], half * sz.wide, sz.wide, 3 * sz.wide)])

    pack_attn(0)
    move = Fetch(pc, attn0_ref, everything[0], wsems)
    move.parts[0]()
    for step in range(1, sz.images):
        swap(step).start()
    move.parts[1]()
    mine_ref[pc.zh] = tokens_ref[pc.zh]
    for layer in range(n):
        if layer:
            pack_attn(layer)
        for half in range(sz.zl):
            pack(ff_refs[layer], half, [(wup_ref[layer], half * sz.ff, sz.ff, 0),
                                        (wdown_ref[layer], half * sz.ff, sz.ff, sz.ff)])
    for step in range(1, sz.images):
        swap(step).wait()
    stream_ref[...] = mine_ref[:, 0].reshape(sz.block, sz.d).astype(f32)
    grad_ref[...] = mine_ref[:, 1].reshape(sz.block, sz.d).astype(f32) * valid_ref[...]
    for part in move.parts[2:]:
        part()
    move.finish()


def open_call(sz, w_qkv, w_out, w_up, w_down, tokens, own_valid):
    attn, ff = ((sz.zl, sz.wrowsp, sz.attnp), bf16), ((sz.zl, sz.wrowsp, sz.ffw), bf16)
    own = ((sz.block, sz.d), f32)
    shapes = Fetch.result(sz, sz.attnp) + [attn] * (sz.layers - 1) + [ff] * sz.layers + [own, own]
    operands = (w_qkv.reshape(sz.layers, sz.wrows, -1), w_out, w_up, w_down, tokens, own_valid)
    return pl.pallas_call(
        functools.partial(open_kernel, sz),
        out_shape=[jax.ShapeDtypeStruct(*s) for s in shapes],
        in_specs=whole(len(operands)),
        out_specs=whole(len(shapes)),
        scratch_shapes=[VMEM(*attn), VMEM(tokens.shape, bf16), DMA((2, sz.images))] + Fetch.scratch(sz, 0),
        compiler_params=params(9),
        name="open",
    )(*operands)


def give_kernel(sz, dw_ref, stream_ref, grad_ref, *refs):
    n = sz.layers
    ff_vecs, attn_vecs, dqvs, dups, (sum_ref, whole_ref, small_ref), own, give_refs = split_refs(
        refs, n, n, n, n, 3, 10, 4
    )
    ends_ref, esems, ysems, ssems, first, from_tp, from_ctx, from_fsdp, sum_tp, sum_ctx = own
    pc = Place(sz)
    greet(weight_peers(pc) + [(pc.f, pc.c, (pc.t + s) % sz.tp) for s in range(1, sz.tp)])
    move = Give(pc, dw_ref, sum_ref, *give_refs)
    move.parts[0]()

    def swap(step):
        zh = (pc.zh + step) % sz.images
        return send(ends_ref.at[zh], whole_ref.at[pc.t, pc.zh], esems.at[0, step], esems.at[1, step],
                    (pc.f, zh * sz.zl + pc.zl, pc.t))

    def spread(step):
        return send(whole_ref.at[pc.t], whole_ref.at[pc.t], ysems.at[0, step], ysems.at[1, step],
                    (pc.f, pc.c, (pc.t + step) % sz.tp))

    def spread_wait(step):
        back = (pc.t + sz.tp - step) % sz.tp
        return send(whole_ref.at[back], whole_ref.at[back], ysems.at[0, step], ysems.at[1, step],
                    (pc.f, pc.c, back))

    for kind, ref in enumerate((stream_ref, grad_ref)):
        ends_ref[:, kind] = ref[...].reshape(sz.images, sz.part, sz.d).astype(bf16)
    for step in range(1, sz.images):
        swap(step).start()
    whole_ref[pc.t, pc.zh] = ends_ref[pc.zh]

    def over_tp(step):
        return send(first, from_tp.at[step], ssems.at[0, 0, step], ssems.at[0, 1, step],
                    (pc.f, pc.c, (pc.t + step) % sz.tp))

    def over_ctx(step):
        return send(sum_tp, from_ctx.at[step], ssems.at[1, 0, step], ssems.at[1, 1, step],
                    (pc.f, pc.ctx_ahead(step), pc.t))

    def over_fsdp(step):
        return send(sum_ctx, from_fsdp.at[step], ssems.at[2, 0, step], ssems.at[2, 1, step],
                    ((pc.f + step) % sz.fsdp, pc.c, pc.t))

    sum_tp[...] = jnp.zeros_like(sum_tp)
    for layer in range(n):
        first[layer] = jnp.zeros_like(first[layer])
        for kind in range(3):
            first[layer, 2 * kind:2 * kind + 1, :] = attn_vecs[layer][kind:kind + 1, :]
            first[layer, 2 * kind + 1:2 * kind + 2, :] = ff_vecs[layer][kind:kind + 1, :]
        sum_tp[n + pc.zl, 3 * layer:3 * layer + 2, 0:sz.headp] = dqvs[layer][...]
        sum_tp[n + pc.zl, 3 * layer + 2:3 * layer + 3, 0:sz.ffp] = dups[layer][...]
    for step in range(1, sz.tp):
        over_tp(step).start()
    for step in range(1, sz.images):
        swap(step).wait()
    for step in range(1, sz.tp):
        spread(step).start()
    move.parts[1]()
    value = first[...]
    for step in range(1, sz.tp):
        over_tp(step).wait()
        value = value + from_tp[step]
    sum_tp[0:n] = value
    for step in range(1, sz.ctx):
        over_ctx(step).start()
    move.parts[2]()
    value = sum_tp[...]
    for step in range(1, sz.ctx):
        over_ctx(step).wait()
        value = value + from_ctx[step]
    sum_ctx[...] = value
    for step in range(1, sz.fsdp):
        over_fsdp(step).start()
    for part in move.parts[3:]:
        part()
    value = sum_ctx[...]
    for step in range(1, sz.fsdp):
        over_fsdp(step).wait()
        value = value + from_fsdp[step]
    small_ref[...] = value
    for step in range(1, sz.tp):
        spread_wait(step).wait_recv()
        spread(step).wait_send()
    move.finish()


def give_call(sz, dw, stream, grad, ff_vecs, attn_vecs, dqvs, dups):
    n, far = sz.layers, max(sz.tp, sz.ctx, sz.fsdp)
    deep = up_to(max(6, 3 * n), 8)
    small = (n + sz.zl, deep, sz.d)
    ends = (sz.images, 2, sz.part, sz.d)
    shapes = Give.result(sz, sz.attnp) + [((sz.tp,) + ends, bf16), (small, f32)]
    operands = (dw, stream, grad, *ff_vecs, *attn_vecs, *dqvs, *dups)
    return pl.pallas_call(
        functools.partial(give_kernel, sz),
        out_shape=[jax.ShapeDtypeStruct(*s) for s in shapes],
        in_specs=whole(len(operands)),
        out_specs=whole(len(shapes)),
        scratch_shapes=[
            VMEM(ends, bf16), DMA((2, sz.images)), DMA((2, sz.tp)), DMA((3, 2, far)),
            VMEM((n, deep, sz.d), f32),
            VMEM((sz.tp, n, deep, sz.d), f32),
            VMEM((sz.ctx,) + small, f32),
            VMEM((sz.fsdp,) + small, f32),
            VMEM(small, f32),
            VMEM(small, f32),
        ]
        + Give.scratch(sz, sz.attnp),
        compiler_params=params(10),
        name="give_rest",
    )(*operands)


def close_kernel(sz, *refs):
    n = sz.layers
    attn_refs, ff_refs, (whole_ref, small_ref), outs = split_refs(refs, n, n, 2, 11)
    out_ref, gin_ref, gain_ref, bias_ref, qkv_ref, qv_ref, wout_ref, up_ref, upb_ref, down_ref, resid_ref = outs
    full, ff = sz.wide * sz.zl, sz.ff * sz.zl

    def join(ref, start, count, width):
        total = None
        for half in range(sz.zl):
            piece = shift_lanes(ref[half], start, count, half * count, up_to(width, 128))
            total = piece if total is None else total + piece
        return total[0:sz.wrows, 0:width]

    for layer in range(n):
        for kind in range(3):
            at = kind * full
            qkv_ref[layer, :, at:at + full] = join(attn_refs[layer], kind * sz.wide, sz.wide, full)
        wout_ref[layer] = join(attn_refs[layer], 3 * sz.wide, sz.wide, full)
        up_ref[layer] = join(ff_refs[layer], 0, sz.ff, ff)
        down_ref[layer] = join(ff_refs[layer], sz.ff, sz.ff, ff)
        values = small_ref[layer]
        gain_ref[layer] = values[0:2]
        bias_ref[layer] = values[2:4]
        resid_ref[layer] = values[4:6]
        total_qv, total_up = None, None
        for half in range(sz.zl):
            values = small_ref[n + half]
            qv = shift_lanes(values, 0, sz.wide, half * sz.wide, up_to(full, 128))
            up = shift_lanes(values, 0, sz.ff, half * sz.ff, up_to(ff, 128))
            total_qv = qv if total_qv is None else total_qv + qv
            total_up = up if total_up is None else total_up + up
        qv_ref[layer] = total_qv[3 * layer:3 * layer + 2, 0:full]
        upb_ref[layer:layer + 1, :] = total_up[3 * layer + 2:3 * layer + 3, 0:ff]
    for image in range(sz.images):
        rows = whole_ref[:, image, 0].reshape(sz.tp * sz.part, sz.d)
        out_ref[image] = rows[0:sz.rows]
        rows = whole_ref[:, image, 1].reshape(sz.tp * sz.part, sz.d)
        gin_ref[image] = rows.astype(f32)[0:sz.rows]


def close_call(sz, attn_sums, ff_sums, ends, small):
    n, full, ff = sz.layers, sz.wide * sz.zl, sz.ff * sz.zl
    tokens = (sz.images, sz.rows, sz.d)
    vec, up = ((n, 2, sz.d), f32), ((n, sz.wrows, ff), f32)
    shapes = [
        (tokens, bf16), (tokens, f32), vec, vec, ((n, sz.wrows, 3 * full), f32), ((n, 2, full), f32),
        ((n, sz.wrows, full), f32), up, ((n, ff), f32), up, vec,
    ]
    results = pl.pallas_call(
        functools.partial(close_kernel, sz),
        out_shape=[jax.ShapeDtypeStruct(*s) for s in shapes],
        in_specs=whole(2 * n + 2),
        out_specs=whole(len(shapes)),
        compiler_params=pltpu.CompilerParams(vmem_limit_bytes=60 * 1024 * 1024),
        name="close",
    )(*attn_sums, *ff_sums, ends, small)
    results = list(results)
    results[4] = results[4].reshape(n, sz.wrows, 3, full)
    return tuple(results)


def per_device(mesh, inputs, cotangent, valid_count, norm_gain, norm_bias, w_qkv, bias_qv, w_out, w_up, bias_up,
               w_down, bias_resid):
    sz = Sizes(mesh, inputs, w_qkv, w_up)
    n = sz.layers
    c, t = lax.axis_index("ctx"), lax.axis_index("tp")
    zh, zl = c // sz.zl, c % sz.zl
    slot = zl * sz.tp + t

    def pieces(a):
        a = jnp.pad(a, ((0, 0), (0, sz.tp * sz.part - sz.rows), (0, 0)))
        return lax.dynamic_slice_in_dim(a, t * sz.part, sz.part, axis=1)

    tokens = jnp.stack([pieces(inputs), pieces(cotangent)], axis=1)

    row = jnp.arange(sz.keys, dtype=jnp.int32)
    of_slot, within = row // sz.block, row % sz.block
    token = (of_slot % sz.tp) * sz.part + within % sz.part
    source = (within // sz.part) * sz.zl + of_slot // sz.tp
    position = source * sz.rows + token
    count = lax.dynamic_index_in_dim(valid_count, zh, keepdims=False)
    valid = ((token < sz.rows) & (position < count)).astype(f32)
    own_valid = lax.dynamic_slice_in_dim(valid, slot * sz.block, sz.block)[:, None]
    valid = valid[None, :]

    attn0, *rest = open_call(sz, w_qkv, w_out, w_up, w_down, tokens, own_valid)
    own_attn, own_ff, (stream, grad) = split_refs(rest, n - 1, n, 2)
    own_attn = [None] + list(own_attn)

    def half(a, to):
        a = lax.dynamic_index_in_dim(a.reshape(a.shape[0], sz.zl, -1), zl, axis=1, keepdims=False)
        return jnp.pad(a, ((0, 0), (0, to - a.shape[1])))

    def joined(w):
        return w[:, :sz.wrows].reshape(sz.d, w.shape[-1])

    def blocks(dw):
        dw = dw.reshape(sz.groups, sz.wrows, dw.shape[-1])
        return jnp.pad(dw, ((0, 0), (0, sz.wrowsp - sz.wrows), (0, 0)))

    own = ((sz.block, sz.d), f32)
    team = ((sz.team, sz.block, sz.d), bf16)
    head = ((sz.chips, sz.tile, sz.headp), bf16)
    hidden = (sz.chips, sz.tile, sz.ffp)
    vec = ((8, sz.d), f32)
    o_scratch = VMEM((sz.d, sz.headp), bf16)

    w_attn, w_ff = [joined(attn0)] + [None] * (n - 1), [None] * n
    streams, attn_kept, ff_kept, middles = [], [], [], []
    for l in range(n):
        streams.append(stream)
        middle, *kept, fetched = layer_call(
            sz, "attn_forward", 1, attn_forward,
            (stream, w_attn[l], norm_gain[l], norm_bias[l], half(bias_qv[l], sz.headp), bias_resid[l], valid),
            [own, team] + [head] * 4, [o_scratch], 1, 1, Fetch, own_ff[l],
        )
        w_ff[l] = joined(fetched)
        middles.append(middle)
        attn_kept.append(kept)
        last = l == n - 1
        stream, *kept = layer_call(
            sz, "ff_forward_last" if last else "ff_forward", 3 if last else 2, ff_forward,
            (middle, w_ff[l], norm_gain[l], norm_bias[l], half(bias_up[l][None], sz.ffp), bias_resid[l]),
            [own, team, (hidden, f32), (hidden, bf16)], [], 1, 1,
            *(() if last else (Fetch, own_attn[l + 1])),
        )
        if not last:
            w_attn[l + 1] = joined(kept.pop())
        ff_kept.append(kept)

    attn_sums, ff_sums, ff_vecs, attn_vecs, dqvs, dups = [[None] * n for _ in range(6)]
    pending = None
    for l in reversed(range(n)):
        last = l == n - 1
        gmid, dw_ff, ff_vecs[l], dups[l], *summed = layer_call(
            sz, "ff_backward_last" if last else "ff_backward", 5 if last else 4, ff_backward,
            (grad, middles[l], *ff_kept[l], w_ff[l], norm_gain[l]),
            [own, ((sz.d, sz.ffw), bf16), vec, ((1, sz.ffp), f32)],
            [VMEM(*team), VMEM(hidden, bf16)], 1, 1, *(() if last else (Give, blocks(pending))),
        )
        if not last:
            attn_sums[l + 1] = summed[0]
        grad, pending, attn_vecs[l], dqvs[l], ff_sums[l] = layer_call(
            sz, "attn_backward", 6, attn_backward,
            (gmid, streams[l], *attn_kept[l], w_attn[l], norm_gain[l], valid),
            [own, ((sz.d, sz.attnp), bf16), vec, ((2, sz.headp), f32)],
            [o_scratch, VMEM(*team), VMEM(*head), VMEM((sz.keys, sz.headp), f32), VMEM((sz.keys, sz.headp), f32),
             VMEM((sz.chips, sz.tile, sz.qkvp), bf16)],
            1, 1, Give, blocks(dw_ff),
        )
    attn_sums[0], ends, small = give_call(sz, blocks(pending), stream, grad, ff_vecs, attn_vecs, dqvs, dups)
    return close_call(sz, attn_sums, ff_sums, ends, small)


def solution(mesh):
    tokens, rows = P("fsdp", "ctx", None), P(None, ("fsdp", "ctx"), "tp")
    qkv = P(None, ("fsdp", "ctx"), None, "tp")
    qv, up = P(None, None, "tp"), P(None, "tp")
    return jax.shard_map(
        functools.partial(per_device, mesh),
        mesh=mesh,
        in_specs=(tokens, tokens, P("fsdp"), P(), P(), qkv, qv, rows, rows, up, rows, P()),
        out_specs=(tokens, tokens, P(), P(), qkv, qv, rows, rows, up, rows, P()),
        check_vma=False,
    )
```

time: 666 us -> 509 us (0.76)
  Pallas kernels: 588 us -> 490 us
  local copies, waits for them, and re-layouts: 48.9 us -> 15.3 us
  other arithmetic: 20.1 us -> 2.77 us
    pallas_call x6 -> x11, Pallas kernels: 588 us -> 490 us  [the longest x8 386 us: layer_call(): pl.pallas_call(functools.partial(layer_kernel, body, len(operands), len(s...]
    transpose x12 -> x0, local copies, waits for them, and re-layouts: 11.6 us -> none  [the longest x8 9.96 us: join(): return jnp.moveaxis(a, 0, 2).reshape(sz.wrows, kinds, -1)]
    another operation x12 -> x0, local copies, waits for them, and re-layouts: 8.48 us -> none  [the longest x8 6.95 us: per_device(): stack = lambda i: jnp.stack([g[i] for g in large])]
    another operation x5 -> x0, other arithmetic: 7.23 us -> none  [the longest x4 6.42 us: per_device(): stack = lambda i: jnp.stack([g[i] for g in large])]
    reshape x11 -> x2, local copies, waits for them, and re-layouts: 10.9 us -> 3.7 us  [the longest x1 2.44 us: close_call(): results[4] = results[4].reshape(n, sz.wrows, 3, full)]
    slice x9 -> x0, local copies, waits for them, and re-layouts: 6.93 us -> none  [the longest x2 4.05 us: unpack_grads(): attn = join(sums[:, :, :4 * sz.wide], 4)]
where the time goes in v2:
time: 509 us; the launch traced here: 508 us
  Pallas kernels  490 us (96%)
  local copies, waits for them, and re-layouts  15.3 us (3%)
    pallas_call x8, Pallas kernels, layer_call(): pl.pallas_call(functools.partial(layer_kernel, body, len(operands), len(s...  386 us
    pallas_call x1, Pallas kernels, open_call(): pl.pallas_call(functools.partial(open_kernel, sz), out_shape=[jax.ShapeDt...  48.9 us
    pallas_call x1, Pallas kernels, give_call(): pl.pallas_call(functools.partial(give_kernel, sz), out_shape=[jax.ShapeDt...  47.4 us

profile of v2, /device:TPU:0, one launch (start us, length us, event | category | flops | bytes accessed | tf_op | source)
XLA Modules:
  0.0 508.4 jit_solution(519655519031831587)
XLA Ops:
  0.7 1.3 dynamic_slice.29
  2.0 1.3 and_convert_fusion.refs_6_.refs_9_
  3.3 0.7 and_convert_fusion.1
  4.0 0.7 fusion.27
  6.1 0.8 slice_reduce_fusion
  8.3 1.3 slice_bitcast_fusion.2
  9.6 1.4 slice_bitcast_fusion
  10.9 0.7 copy.29.valid_ref
  11.7 1.1 fusion
  12.7 0.8 pad_maximum_fusion.tokens_ref
  13.9 1.3 reshape.228.wqkv_ref
  15.2 48.9 %open.1 = (bf16[8,144,640]{2,1,0:T(8,128)(2,1)}, bf16[2,144,640]{2,1,0:T(8,128)(2,1)}, bf16[2,144,1152]{2,1,0:T(8,128)(2,1)}, bf16[2,144,1152]{2,1,0:T(8,128)(2,...) custom-call(bf16[2,144,864]{2,1,0:T(8,128)(2,1)} %reshape.228.wqkv_ref, bf16[2,144,288]{2,1,0:T(8,128)(2,1)} %wout_ref.1, ...), custom_call_target="tpu_custom_call" | custom-call | tf_op jit(solution)/shard_map/open/pallas_call | solution.py:790
  64.1 55.9 %attn_forward.2 = (f32[96,1152]{1,0:T(8,128)}, bf16[8,96,1152]{2,1,0:T(8,128)(2,1)}, bf16[4,192,256]{2,1,0:T(8,128)(2,1)}, bf16[4,192,256]{2,1,0:T(8,128)(2,1)},...) custom-call(f32[96,1152]{1,0:T(8,128)} %get-tuple-element.74.refs_0_.refs_1_, ...), custom_call_target="tpu_custom_call" | custom-call | tf_op jit(solution)/shard_map/attn_forward/pallas_call | solution.py:463
  120.0 40.6 %ff_forward.1 = (f32[96,1152]{1,0:T(8,128)}, bf16[8,96,1152]{2,1,0:T(8,128)(2,1)}, f32[4,192,640]{2,1,0:T(8,128)}, bf16[4,192,640]{2,1,0:T(8,128)(2,1)}, bf16[8,144,640]{2,1,0:T(8,128)(2,1)}) custom-call(f32[96,1152]{1,0:T(8,128)} %get-tuple-element.77.refs_0_.refs_1_, bf16[1152,1152]{1,0:T(8,128)(2,1)} %bitcast.39, ...), custom_call_target="tpu_custom_call" | custom-call | tf_op jit(solution)/shard_map/ff_forward/pallas_call | solution.py:463
  160.6 57.4 %attn_forward.3 = (f32[96,1152]{1,0:T(8,128)}, bf16[8,96,1152]{2,1,0:T(8,128)(2,1)}, bf16[4,192,256]{2,1,0:T(8,128)(2,1)}, bf16[4,192,256]{2,1,0:T(8,128)(2,1)},...) custom-call(f32[96,1152]{1,0:T(8,128)} %get-tuple-element.80.refs_0_.refs_1_, ...), custom_call_target="tpu_custom_call" | custom-call | tf_op jit(solution)/shard_map/attn_forward/pallas_call | solution.py:463
  217.9 32.6 %ff_forward_last.1 = (f32[96,1152]{1,0:T(8,128)}, bf16[8,96,1152]{2,1,0:T(8,128)(2,1)}, f32[4,192,640]{2,1,0:T(8,128)}, bf16[4,192,640]{2,1,0:T(8,128)(2,1)}) custom-call(f32[96,1152]{1,0:T(8,128)} %get-tuple-element.83.refs_0_.refs_1_, bf16[1152,1152]{1,0:T(8,128)(2,1)} %bitcast.37, f32[2,1152]{1,0:T(2,128)} %get-tuple-element.163.refs_2_.refs_6_.refs_8_, ...), custom_call_target="tpu_custom_call" | custom-call | tf_op jit(solution)/shard_map/ff_forward_last/pallas_call | solution.py:463
  250.5 34.0 %ff_backward_last.1 = (f32[96,1152]{1,0:T(8,128)}, bf16[1152,1152]{1,0:T(8,128)(2,1)}, f32[8,1152]{1,0:T(8,128)}, f32[1,640]{1,0:T(1,128)}) custom-call(f32[96,1152]{1,0:T(8,128)} %get-tuple-element.73.refs_0_, f32[96,1152]{1,0:T(8,128)} %get-tuple-element.83.refs_0_.refs_1_, bf16[8,96,1152]{2,1,0:T(8,128)(2,1)} %get-tuple-element.85.refs_2_, ...), custom_call_target="tpu_custom_call" | custom-call | tf_op jit(solution)/shard_map/ff_backward_last/pallas_call | solution.py:463
  284.5 60.4 %attn_backward.2 = (f32[96,1152]{1,0:T(8,128)}, bf16[1152,640]{1,0:T(8,128)(2,1)}, f32[8,1152]{1,0:T(8,128)}, f32[2,256]{1,0:T(2,128)}, f32[2,144,1152]{2,1,0:T(8,128)}) custom-call(f32[96,1152]{1,0:T(8,128)} %get-tuple-element.88.refs_0_, f32[96,1152]{1,0:T(8,128)} %get-tuple-element.80.refs_0_.refs_1_, bf16[8,96,1152]{2,1,0:T(8,128)(2,1)} %get-tuple-element.89.refs_2_, ...), custom_call_target="tpu_custom_call" | custom-call | tf_op jit(solution)/shard_map/attn_backward/pallas_call | solution.py:463
  344.9 44.4 %ff_backward.1 = (f32[96,1152]{1,0:T(8,128)}, bf16[1152,1152]{1,0:T(8,128)(2,1)}, f32[8,1152]{1,0:T(8,128)}, f32[1,640]{1,0:T(1,128)}, f32[2,144,640]{2,1,0:T(8,128)}) custom-call(f32[96,1152]{1,0:T(8,128)} %get-tuple-element.95.refs_0_, f32[96,1152]{1,0:T(8,128)} %get-tuple-element.77.refs_0_.refs_1_, bf16[8,96,1152]{2,1,0:T(8,128)(2,1)} %get-tuple-element.96.refs_2_, ...), custom_call_target="tpu_custom_call" | custom-call | tf_op jit(solution)/shard_map/ff_backward/pallas_call | solution.py:463
  389.3 61.1 %attn_backward.3 = (f32[96,1152]{1,0:T(8,128)}, bf16[1152,640]{1,0:T(8,128)(2,1)}, f32[8,1152]{1,0:T(8,128)}, f32[2,256]{1,0:T(2,128)}, f32[2,144,1152]{2,1,0:T(8,128)}) custom-call(f32[96,1152]{1,0:T(8,128)} %get-tuple-element.100.refs_0_, f32[96,1152]{1,0:T(8,128)} %get-tuple-element.74.refs_0_.refs_1_, bf16[8,96,1152]{2,1,0:T(8,128)(2,1)} %get-tuple-element.101.refs_2_, ...), custom_call_target="tpu_custom_call" | custom-call | tf_op jit(solution)/shard_map/attn_backward/pallas_call | solution.py:463
  450.4 47.4 %give_rest.1 = (f32[2,144,640]{2,1,0:T(8,128)}, bf16[4,2,2,48,1152]{4,3,2,1,0:T(8,128)(2,1)}, f32[4,8,1152]{2,1,0:T(8,128)}) custom-call(bf16[8,144,640]{2,1,0:T(8,128)(2,1)} %bitcast.47, f32[96,1152]{1,0:T(8,128)} %get-tuple-element.108.stream_ref, f32[96,1152]{1,0:T(8,128)} %get-tuple-element.109.grad_ref, f32[8,1152]{1,0:T(8,128)} %get-tuple-element.110.refs_0_, ...), custom_call_target="tpu_custom_call" | custom-call | tf_op jit(solution)/shard_map/give_rest/pallas_call | solution.py:894
  497.8 6.9 %close.1 = (bf16[2,184,1152]{2,1,0:T(8,128)(2,1)}, f32[2,184,1152]{2,1,0:T(8,128)}, f32[2,2,1152]{2,1,0:T(2,128)}, f32[2,2,1152]{2,1,0:T(2,128)}, f32[2,144,864]...) custom-call(f32[2,144,640]{2,1,0:T(8,128)} %get-tuple-element.118.re, ...), custom_call_target="tpu_custom_call" | custom-call | tf_op jit(solution)/shard_map/close/pallas_call | solution.py:962
  504.8 2.4 reshape.237
  507.2 1.1 copy.32
  (16 shorter events, 3.1 us)
Async XLA Ops:
  0.6 12.9 %copy-start = (bf16[2,144,3,288]{3,1,2,0:T(8,128)(2,1)S(1)}, bf16[2,144,3,288]{3,1,2,0:T(8,128)(2,1)}, u32[]{:S(2)}) copy-start(bf16[2,144,3,288]{3,1,2,0:T(8,128)(2,1)} %param.17) | copy-start | bytes 1492996

commit v3 on v2

--- a/solution.py
+++ b/solution.py
@@ -39,8 +39,9 @@
         self.team = self.chips * 2
         self.part = up_to(-(-self.rows // self.tp), 16)
         self.block = self.images * self.part
-        self.tile = 2 * self.block
-        self.keys = self.chips * self.tile
+        self.units = self.chips * self.images
+        self.tile = 2 * self.part
+        self.keys = self.units * self.tile
         self.wide = w_qkv.shape[3] // self.zl
         self.heads = self.wide // HEAD_DIM
         self.ff = w_up.shape[2] // self.zl
@@ -97,11 +98,19 @@
         return zh * sz.zl + (self.zl + sz.zl - step % sz.zl) % sz.zl
 
 
+class Greeting:
+    def __init__(self, others):
+        self.count = len(others)
+        self.barrier = pltpu.get_barrier_semaphore()
+        for other in others:
+            pl.semaphore_signal(self.barrier, inc=1, device_id=other, device_id_type=MESH)
+
+    def wait(self):
+        pl.semaphore_wait(self.barrier, self.count)
+
+
 def greet(others):
-    barrier = pltpu.get_barrier_semaphore()
-    for other in others:
-        pl.semaphore_signal(barrier, inc=1, device_id=other, device_id_type=MESH)
-    pl.semaphore_wait(barrier, len(others))
+    Greeting(others).wait()
 
 
 def send(src, dst, send_sem, recv_sem, device):
@@ -122,112 +131,206 @@
     ]
 
 
+def pick(step, values):
+    if isinstance(step, int):
+        return values[step]
+    out = jnp.int32(values[0])
+    for i in range(1, len(values)):
+        out = jnp.where(step == i, jnp.int32(values[i]), out)
+    return out
+
+
+def when(condition, run):
+    if isinstance(condition, (bool, int)):
+        if condition:
+            run()
+    else:
+        pl.when(condition)(run)
+
+
+class Routes:
+    def __init__(self, sz):
+        self.sz = sz
+        pieces = range(sz.images)
+        z = [dz * sz.chips_y for dz in range(1, sz.zl)]
+        y = list(range(1, sz.chips_y))
+        self.straight = z + y
+        self.turned = [dz + dy for dz in z for dy in y]
+        own = [(0, p) for p in pieces]
+        near = [(b, p) for p in pieces for b in self.straight]
+        far = [(b, p) for p in pieces for b in self.turned]
+        self.arriving = own + near + far
+        self.leaving = far + [(b, p) for b in z for p in pieces] + [(b, p) for b in y for p in pieces] + own
+
+
+def backs(order):
+    return [b for b, _ in order]
+
+
+def pieces_of(order):
+    return [p for _, p in order]
+
+
 class Gather:
-    def __init__(self, pc, buf, sems, at):
-        self.pc, self.buf, self.sems, self.at = pc, buf, sems, at
-
-    def far(self, step, slot, device):
-        return send(self.buf.at[slot], self.buf.at[slot], self.sems.at[self.at, 0, step],
-                    self.sems.at[self.at, 1, step], device)
-
-    def near(self, step, slot):
-        return send(self.buf.at[slot], self.buf.at[slot], self.sems.at[self.at, 2, step],
-                    self.sems.at[self.at, 3, step], self.pc.twin)
+    def __init__(self, pc, buf, sems, turn_z=()):
+        self.pc, self.buf, self.sems = pc, buf, sems
+        self.routes = Routes(pc.sz)
+        self.order = self.routes.arriving
+        self.turn_z = turn_z
+
+    def move(self, kind, back, piece, slot, device):
+        return send(self.buf.at[slot, piece], self.buf.at[slot, piece], self.sems.at[kind, back, piece],
+                    self.sems.at[kind + 1, back, piece], device)
+
+    def near(self, back, piece, slot):
+        return self.move(2, back, piece, slot, self.pc.twin)
 
     def start(self):
         pc = self.pc
-        for step in range(1, pc.sz.chips):
-            self.far(step, pc.slot, pc.device(pc.chip_at(step))).start()
-        self.near(0, pc.slot).start()
-
-    def arrive(self, step):
+        for piece in range(pc.sz.images):
+            for step in self.routes.straight:
+                self.move(0, step, piece, pc.slot, pc.device(pc.chip_at(step))).start()
+            self.near(0, piece, pc.slot).start()
+
+    def relays(self, back, piece):
+        sz = self.pc.sz
+        if back == 0 or back in self.routes.turned:
+            return []
+        if back % sz.chips_y == 0:
+            return [] if piece in self.turn_z else [(back + dy, dy) for dy in range(1, sz.chips_y)]
+        return [(back + dz * sz.chips_y, dz * sz.chips_y) for dz in range(1, sz.zl)] if piece in self.turn_z else []
+
+    def forward(self, step):
+        pc, order = self.pc, self.order
+        back, piece = pick(step, backs(order)), pick(step, pieces_of(order))
+        slot = 2 * pc.index(pc.chip_back(back)) + pc.k
+
+        def other():
+            self.move(0, back, piece, slot, pc.twin).wait_recv()
+            self.near(back, piece, slot).start()
+
+        when(back > 0, other)
+        for at, (b, p) in enumerate(order):
+            for seen, ahead in self.relays(b, p):
+                when(step == at, self.move(0, seen, p, slot, pc.device(pc.chip_at(ahead))).start)
+
+    def ready(self, step):
         pc = self.pc
-        chip = pc.chip_back(step)
-        at = pc.index(chip)
-
-        @pl.when(step > 0)
-        def _():
-            self.far(step, 2 * at + pc.k, pc.device(chip)).wait_recv()
-            self.near(step, 2 * at + pc.k).start()
-
-        self.near(step, 2 * at + 1 - pc.k).wait_recv()
-        return at
+        back, piece = pick(step, backs(self.order)), pick(step, pieces_of(self.order))
+        at = pc.index(pc.chip_back(back))
+        self.near(back, piece, 2 * at + 1 - pc.k).wait_recv()
+        return at * pc.sz.images + piece, at, piece
+
+    def ahead(self, step):
+        if isinstance(step, int):
+            if step + 1 < len(self.order):
+                self.forward(step + 1)
+        else:
+            pl.when(step + 1 < len(self.order))(lambda: self.forward(step + 1))
+
+    def tokens(self, at, piece):
+        sz = self.pc.sz
+        return self.buf[pl.ds(2 * at, 2), piece].reshape(sz.tile, sz.d)
 
     def finish(self):
         pc = self.pc
-        for step in range(pc.sz.chips):
-            if step:
-                self.far(step, pc.slot, pc.device(pc.chip_at(step))).wait_send()
-            self.near(step, pc.slot).wait_send()
+        for b, p in self.order:
+            if b:
+                self.move(0, b, p, pc.slot, pc.twin).wait_send()
+            self.near(b, p, pc.slot).wait_send()
 
 
 class Scatter:
-    def __init__(self, pc, bufs, sems, at):
-        self.pc, self.sems, self.at = pc, sems, at
+    def __init__(self, pc, bufs, sems, turn):
+        self.pc, self.sems, self.turn = pc, sems, turn
         self.both, self.keep, self.tsend, self.trecv, self.rsend, self.rrecv = bufs
-
-    def near(self, step):
-        return send(self.tsend.at[step], self.trecv.at[step], self.sems.at[self.at, 0, step],
-                    self.sems.at[self.at, 1, step], self.pc.twin)
-
-    def far(self, step):
-        return send(self.rsend.at[step], self.rrecv.at[step], self.sems.at[self.at, 2, step],
-                    self.sems.at[self.at, 3, step], self.pc.device(self.pc.chip_back(step)))
+        self.routes = Routes(pc.sz)
+        self.order = self.routes.leaving if turn else self.routes.arriving
+
+    def near(self, back, piece):
+        return send(self.tsend.at[back, piece], self.trecv.at[back, piece], self.sems.at[0, back, piece],
+                    self.sems.at[1, back, piece], self.pc.twin)
+
+    def far(self, back, piece):
+        pc, sz = self.pc, self.pc.sz
+        to = back
+        if self.turn:
+            if isinstance(back, int):
+                to = back % sz.chips_y or back
+            else:
+                dy = lax.rem(back, jnp.int32(sz.chips_y))
+                to = jnp.where(dy > 0, dy, back)
+        return send(self.rsend.at[back, piece], self.rrecv.at[back, piece], self.sems.at[2, back, piece],
+                    self.sems.at[3, back, piece], pc.device(pc.chip_back(to)))
+
+    def at(self, step):
+        return pick(step, backs(self.order)), pick(step, pieces_of(self.order))
+
+    def unit(self, step):
+        back, piece = self.at(step)
+        return self.pc.index(self.pc.chip_back(back)) * self.pc.sz.images + piece
 
     def push(self, step, partial):
-        pc, block = self.pc, self.pc.sz.block
-        self.both[...] = partial.reshape(2, block, partial.shape[-1])
-        self.tsend[step] = self.both[1 - pc.k].astype(bf16)
-        self.near(step).start()
-        self.keep[step] = self.both[pc.k]
-
-        @pl.when(step > 0)
-        def _():
-            self.relay(step - 1)
+        pc = self.pc
+        back, piece = self.at(step)
+        self.both[...] = partial.reshape(2, pc.sz.part, partial.shape[-1])
+        self.tsend[back, piece] = self.both[1 - pc.k].astype(bf16)
+        self.near(back, piece).start()
+        self.keep[back, piece] = self.both[pc.k]
+        pl.when(step > 0)(lambda: self.relay(step - 1))
 
     def relay(self, step):
-        self.near(step).wait_recv()
-        total = self.keep[step] + self.trecv[step].astype(f32)
-
-        def own():
-            self.keep[0] = total
-
-        def other():
-            self.rsend[step] = total.astype(bf16)
-            self.far(step).start()
-
-        if isinstance(step, int):
-            own() if step == 0 else other()
-        else:
-            pl.when(step == 0)(own)
-            pl.when(step > 0)(other)
+        sz = self.pc.sz
+        back, piece = self.at(step)
+        self.near(back, piece).wait_recv()
+        self.keep[back, piece] += self.trecv[back, piece].astype(f32)
+        if self.turn:
+            for at, (b, p) in enumerate(self.order):
+                if b and b % sz.chips_y == 0:
+
+                    def extra(b=b, p=p):
+                        for dy in range(1, sz.chips_y):
+                            self.far(b + dy, p).wait_recv()
+                            self.keep[b, p] += self.rrecv[b + dy, p].astype(f32)
+
+                    when(step == at, extra)
+
+        def leave():
+            self.rsend[back, piece] = self.keep[back, piece].astype(bf16)
+            self.far(back, piece).start()
+
+        when(back > 0, leave)
 
     def flush(self):
-        self.relay(self.pc.sz.chips - 1)
+        self.relay(self.pc.sz.units - 1)
 
     def finish(self):
+        sz = self.pc.sz
         total = self.keep[0]
-        for step in range(1, self.pc.sz.chips):
-            self.far(step).wait_recv()
-            total = total + self.rrecv[step].astype(f32)
-        for step in range(self.pc.sz.chips):
-            self.near(step).wait_send()
-            if step:
-                self.far(step).wait_send()
-        return total
-
-
-def team_scratch(sz, gathers, scatters):
-    n = sz.chips
+        for back in range(1, sz.chips):
+            if self.turn and back in self.routes.turned:
+                continue
+            for piece in range(sz.images):
+                self.far(back, piece).wait_recv()
+            total = total + self.rrecv[back].astype(f32)
+        for back, piece in self.order:
+            self.near(back, piece).wait_send()
+            if back:
+                self.far(back, piece).wait_send()
+        return total.reshape(sz.block, sz.d)
+
+
+def team_scratch(sz):
+    n = (sz.chips, sz.images)
     return [
-        VMEM((2, sz.block, sz.d), f32),
-        VMEM((n, sz.block, sz.d), f32),
-        VMEM((n, sz.block, sz.d), bf16),
-        VMEM((n, sz.block, sz.d), bf16),
-        VMEM((n, sz.block, sz.d), bf16),
-        VMEM((n, sz.block, sz.d), bf16),
-        DMA((gathers, 4, n)),
-        DMA((scatters, 4, n)),
+        VMEM((2, sz.part, sz.d), f32),
+        VMEM(n + (sz.part, sz.d), f32),
+        VMEM(n + (sz.part, sz.d), bf16),
+        VMEM(n + (sz.part, sz.d), bf16),
+        VMEM(n + (sz.part, sz.d), bf16),
+        VMEM(n + (sz.part, sz.d), bf16),
+        DMA((4,) + n),
+        DMA((4,) + n),
     ]
 
 
@@ -289,6 +392,8 @@
     return weights / jnp.sum(weights, axis=-1, keepdims=True)
 
 
+FF_TURN = (1,)
+
 class Fetch:
     def __init__(self, pc, own, everything, sems):
         self.pc, self.own, self.all, self.sems = pc, own, everything, sems
@@ -314,7 +419,7 @@
 
     def start(self):
         self.own_copy().start()
-        for step in range(1, self.pc.sz.ctx):
+        for step in range(1, min(3, self.pc.sz.ctx)):
             self.along_ctx(step).start()
 
     def pass_own(self):
@@ -324,6 +429,8 @@
 
     def pass_on(self, step):
         self.along_ctx(step).wait_recv()
+        if step + 2 < self.pc.sz.ctx:
+            self.along_ctx(step + 2).start()
         for jump in range(1, self.pc.sz.fsdp):
             self.along_fsdp(jump, step).start()
 
@@ -368,7 +475,7 @@
                     self.sems.at[0, 1, step], (pc.f, pc.ctx_back(step), pc.t))
 
     def start(self):
-        for step in self.order:
+        for step in self.order[:2]:
             for jump in range(1, self.pc.sz.fsdp):
                 self.along_fsdp(jump, step).start()
 
@@ -376,6 +483,8 @@
         pc, sz = self.pc, self.pc.sz
         for jump in range(1, sz.fsdp):
             self.along_fsdp(jump, step).wait_recv()
+            if step >= 2:
+                self.along_fsdp(jump, step - 2).start()
         total = self.dw[pc.f * sz.ctx + pc.ctx_ahead(step)].astype(f32)
         for jump in range(1, sz.fsdp):
             total = total + self.got[jump - 1, step].astype(f32)
@@ -437,6 +546,20 @@
             self.mover.finish()
 
 
+def by_unit(sz, values):
+    values = values.reshape(sz.chips, 2, sz.images, sz.part, values.shape[-1])
+    return jnp.swapaxes(values, 1, 2).reshape(sz.keys, values.shape[-1])
+
+
+def gather_norm(pc, greeting, gather, values, gain, shift):
+    high, _ = normalised(values)
+    low = (high * gain + shift).astype(bf16)
+    gather.buf[pc.slot] = low.reshape(pc.sz.images, pc.sz.part, pc.sz.d)
+    if greeting:
+        greeting.wait()
+    gather.start()
+
+
 def split_refs(refs, *counts):
     out, at = [], 0
     for count in counts:
@@ -446,26 +569,26 @@
     return out
 
 
-def layer_kernel(body, ins, outs, scratch, gathers, scatters, mover, sz, *refs):
+def layer_kernel(body, ins, outs, scratch, mover, sz, *refs):
     m = 1 if mover else 0
     own, team = len(scratch), 8
     rest = len(refs) - ins - m - outs - m - own - team
     a, ma, b, mb, s, t, ms = split_refs(refs, ins, m, outs, m, own, team, rest)
     pc = Place(sz)
-    greet(team_peers(pc) + (weight_peers(pc, True) if mover else []))
-    body(sz, pc, Beside(pc, mover, (*ma, *mb, *ms)), *a, *b, *s, t[:6], t[6], t[7])
-
-
-def layer_call(sz, name, ident, body, operands, shapes, scratch, gathers, scatters, mover=None, extra=None):
+    greeting = Greeting(team_peers(pc) + (weight_peers(pc, True) if mover else []))
+    body(sz, pc, greeting, Beside(pc, mover, (*ma, *mb, *ms)), *a, *b, *s, t[:6], t[6], t[7])
+
+
+def layer_call(sz, name, ident, body, operands, shapes, scratch, mover=None, extra=None):
     cols = extra.shape[-1] if mover else 0
     results = list(shapes) + (mover.result(sz, cols) if mover else [])
     n_in = len(operands) + (1 if mover else 0)
     return pl.pallas_call(
-        functools.partial(layer_kernel, body, len(operands), len(shapes), scratch, gathers, scatters, mover, sz),
+        functools.partial(layer_kernel, body, len(operands), len(shapes), scratch, mover, sz),
         out_shape=[jax.ShapeDtypeStruct(*s) for s in results],
         in_specs=whole(n_in),
         out_specs=whole(len(results)),
-        scratch_shapes=scratch + team_scratch(sz, gathers, scatters) + (mover.scratch(sz, cols) if mover else []),
+        scratch_shapes=scratch + team_scratch(sz) + (mover.scratch(sz, cols) if mover else []),
         compiler_params=params(ident),
         name=name,
     )(*operands, *([extra] if mover else []))
@@ -481,125 +604,133 @@
     )
 
 
-def attn_forward(sz, pc, beside, stream_ref, w_ref, gain_ref, shift_ref, qv_ref, resid_ref, valid_ref,
-                 middle_ref, n1_ref, q_ref, k_ref, v_ref, mixed_ref, o_ref, bufs, gsems, ssems):
-    gather = Gather(pc, n1_ref, gsems, 0)
-    high, _ = normalised(stream_ref[...])
-    n1_ref[pc.slot] = (high * gain_ref[0:1, :] + shift_ref[0:1, :]).astype(bf16)
-    gather.start()
+def attn_forward(first, sz, pc, greeting, beside, stream_ref, w_ref, gain_ref, shift_ref, qv_ref, resid_ref, valid_ref, *refs):
+    given, (middle_ref,), made, (q_ref, k_ref, v_ref, mixed_ref, o_ref, bufs, gsems, ssems) = split_refs(
+        refs, 1 if first else 0, 1, 0 if first else 1, 8
+    )
+    gather = Gather(pc, given[0] if first else made[0], gsems)
+    if first:
+        greeting.wait()
+    else:
+        gather_norm(pc, greeting, gather, stream_ref[...], gain_ref[0:1, :], shift_ref[0:1, :])
     beside.part(0)
     unpack_out(sz, w_ref, o_ref)
     beside.part(1)
 
     def project(step, carry):
-        at = gather.arrive(step)
-        tokens = n1_ref[pl.ds(2 * at, 2)].reshape(sz.tile, sz.d)
-        both3 = dot(tokens, w_ref[:, 0:sz.qkvp], (1, 0))
-        q_ref[at] = (take(sz, both3, 0) + qv_ref[0:1, :]).astype(bf16)
-        k_ref[at] = take(sz, both3, 1).astype(bf16)
-        v_ref[at] = (take(sz, both3, 2) + qv_ref[1:2, :]).astype(bf16)
+        if first:
+            at, piece = lax.div(step, sz.images), lax.rem(step, sz.images)
+            unit = step
+        else:
+            unit, at, piece = gather.ready(step)
+        both3 = dot(gather.tokens(at, piece), w_ref[:, 0:sz.qkvp], (1, 0))
+        if not first:
+            gather.ahead(step)
+        q_ref[unit] = (take(sz, both3, 0) + qv_ref[0:1, :]).astype(bf16)
+        k_ref[unit] = take(sz, both3, 1).astype(bf16)
+        v_ref[unit] = (take(sz, both3, 2) + qv_ref[1:2, :]).astype(bf16)
         return carry
 
-    lax.fori_loop(0, sz.chips, project, 0)
-    gather.finish()
-    scatter = Scatter(pc, bufs, ssems, 0)
+    lax.fori_loop(0, sz.units, project, 0)
+    if not first:
+        gather.finish()
+    scatter = Scatter(pc, bufs, ssems, True)
 
     def attend(step, carry):
-        at = pc.index(pc.chip_back(step))
+        unit = scatter.unit(step)
         keys = k_ref[...].reshape(sz.keys, sz.headp)
         values = v_ref[...].reshape(sz.keys, sz.headp)
-        queries = q_ref[at]
+        queries = q_ref[unit]
         total = jnp.zeros((sz.tile, sz.headp), f32)
         for head in range(sz.heads):
             probs = probabilities(head_of(queries, head), keys, valid_ref[...])
             total = total + dot(probs.astype(bf16), head_of(values, head), (1, 0))
         mixed = total.astype(bf16)
-        mixed_ref[at] = mixed
+        mixed_ref[unit] = mixed
         scatter.push(step, dot(mixed, o_ref[...], (1, 1)))
-        beside.at(step, {sz.chips - 1: 2})
+        beside.at(step, {1: 2, 3: 3})
         return carry
 
-    lax.fori_loop(0, sz.chips, attend, 0)
+    lax.fori_loop(0, sz.units, attend, 0)
     scatter.flush()
-    beside.rest(3)
+    beside.rest(4)
     middle_ref[...] = stream_ref[...] + (scatter.finish() + resid_ref[0:1, :])
     beside.finish()
 
 
-def ff_forward(sz, pc, beside, middle_ref, w_ref, gain_ref, shift_ref, upb_ref, resid_ref,
+def ff_forward(sz, pc, greeting, beside, middle_ref, w_ref, gain_ref, shift_ref, upb_ref, resid_ref,
                out_ref, n2_ref, pre_ref, hidden_ref, bufs, gsems, ssems):
-    gather = Gather(pc, n2_ref, gsems, 0)
-    high, _ = normalised(middle_ref[...])
-    n2_ref[pc.slot] = (high * gain_ref[1:2, :] + shift_ref[1:2, :]).astype(bf16)
-    gather.start()
+    gather = Gather(pc, n2_ref, gsems, FF_TURN)
+    gather_norm(pc, greeting, gather, middle_ref[...], gain_ref[1:2, :], shift_ref[1:2, :])
     beside.part(0)
     beside.part(1)
-    scatter = Scatter(pc, bufs, ssems, 0)
+    scatter = Scatter(pc, bufs, ssems, False)
 
     def feed(step, carry):
-        at = gather.arrive(step)
-        tokens = n2_ref[pl.ds(2 * at, 2)].reshape(sz.tile, sz.d)
-        pre = dot(tokens, w_ref[:, 0:sz.ffp], (1, 0)) + upb_ref[...]
-        pre_ref[at] = pre
+        unit, at, piece = gather.ready(step)
+        pre = dot(gather.tokens(at, piece), w_ref[:, 0:sz.ffp], (1, 0)) + upb_ref[...]
+        gather.ahead(step)
+        pre_ref[unit] = pre
         hidden = 0.5 * pre * (1.0 + jnp.tanh(gelu_root * (pre + gelu_cubic * pre * pre * pre)))
         hidden = jnp.where(lanes_of(hidden.shape) < sz.ff, hidden, 0.0)
         if sz.down_shift:
             hidden = pltpu.roll(hidden, sz.down_shift, 1)
         hidden = hidden.astype(bf16)
-        hidden_ref[at] = hidden
+        hidden_ref[unit] = hidden
         scatter.push(step, dot(hidden, w_ref[:, sz.down_at:], (1, 1)))
-        beside.at(step, {sz.chips - 1: 2})
+        beside.at(step, {4: 2, 6: 3})
         return carry
 
-    lax.fori_loop(0, sz.chips, feed, 0)
+    lax.fori_loop(0, sz.units, feed, 0)
     scatter.flush()
     gather.finish()
-    beside.rest(3)
+    beside.rest(4)
     out_ref[...] = middle_ref[...] + (scatter.finish() + resid_ref[1:2, :])
     beside.finish()
 
 
-def ff_backward(sz, pc, beside, grad_ref, middle_ref, n2_ref, pre_ref, hidden_ref, w_ref, gain_ref,
+def ff_backward(sz, pc, greeting, beside, grad_ref, middle_ref, n2_ref, pre_ref, hidden_ref, w_ref, gain_ref,
                 gmid_ref, dw_ref, vec_ref, dup_ref, gl_ref, pg_ref, bufs, gsems, ssems):
     span = 384 if sz.d % 384 == 0 else 128
-    gather = Gather(pc, gl_ref, gsems, 0)
+    gather = Gather(pc, gl_ref, gsems, FF_TURN)
     grad_low = grad_ref[...].astype(bf16)
-    gl_ref[pc.slot] = grad_low
+    gl_ref[pc.slot] = grad_low.reshape(sz.images, sz.part, sz.d)
+    greeting.wait()
     gather.start()
     beside.part(0)
     vec_ref[...] = jnp.zeros_like(vec_ref)
     vec_ref[2:3, :] = jnp.sum(grad_low.astype(f32), axis=0, keepdims=True)
-    scatter = Scatter(pc, bufs, ssems, 0)
+    scatter = Scatter(pc, bufs, ssems, False)
     dup_ref[...] = jnp.zeros_like(dup_ref)
 
     def feed(step, carry):
-        at = gather.arrive(step)
-        grads = gl_ref[pl.ds(2 * at, 2)].reshape(sz.tile, sz.d)
-        back = dot(grads, w_ref[:, sz.down_at:], (1, 0))
+        unit, at, piece = gather.ready(step)
+        back = dot(gather.tokens(at, piece), w_ref[:, sz.down_at:], (1, 0))
+        gather.ahead(step)
         if sz.down_shift:
             back = pltpu.roll(back, sz.ffp - sz.down_shift, 1)
-        pre = pre_ref[at]
+        pre = pre_ref[unit]
         bent = jnp.tanh(gelu_root * (pre + gelu_cubic * pre * pre * pre))
         slope = 0.5 * (1.0 + bent) + 0.5 * pre * (1.0 - bent * bent) * (
             gelu_root * (1.0 + 3.0 * gelu_cubic * pre * pre)
         )
         pre_grad = jnp.where(lanes_of(back.shape) < sz.ff, back * slope, 0.0).astype(bf16)
-        pg_ref[at] = pre_grad
+        pg_ref[unit] = pre_grad
         dup_ref[...] += jnp.sum(pre_grad.astype(f32), axis=0, keepdims=True)
         scatter.push(step, dot(pre_grad, w_ref[:, 0:sz.ffp], (1, 1)))
-        beside.at(step, {sz.chips - 2: 1, sz.chips - 1: 2})
+        beside.at(step, {3: 1, 5: 2, 7: 3})
         return carry
 
-    lax.fori_loop(0, sz.chips, feed, 0)
+    lax.fori_loop(0, sz.units, feed, 0)
     scatter.flush()
-    beside.rest(3)
+    beside.rest(4)
 
     def grads_ff(i, carry):
         lanes = pl.ds(pl.multiple_of(i * span, 128), span)
         hidden = hidden_ref[...].reshape(sz.keys, sz.ffp)
-        down = dot(gl_ref[:, :, lanes].reshape(sz.keys, span), hidden, (0, 0))
+        down = dot(by_unit(sz, gl_ref[:, :, :, lanes]), hidden, (0, 0))
         pre_grad = pg_ref[...].reshape(sz.keys, sz.ffp)
-        up = dot(n2_ref[:, :, lanes].reshape(sz.keys, span), pre_grad, (0, 0))
+        up = dot(by_unit(sz, n2_ref[:, :, :, lanes]), pre_grad, (0, 0))
         dw_ref[lanes, 0:sz.down_at] = up[:, 0:sz.down_at].astype(bf16)
         over = sz.ffp - sz.down_at
         if over:
@@ -617,40 +748,34 @@
     beside.finish()
 
 
-def attn_backward(sz, pc, beside, gmid_ref, stream_ref, n1_ref, q_ref, k_ref, v_ref, mixed_ref, w_ref, gain_ref,
+def attn_backward(sz, pc, greeting, beside, gmid_ref, stream_ref, n1_ref, q_ref, k_ref, v_ref, mixed_ref, w_ref, gain_ref,
                   valid_ref, below_ref, dw_ref, vec_ref, dqv_ref,
-                  o_ref, ml_ref, mg_ref, dk_ref, dv_ref, stack_ref, bufs, gsems, ssems):
+                  o_ref, ml_ref, dk_ref, dv_ref, stack_ref, bufs, gsems, ssems):
     span = 384 if sz.d % 384 == 0 else 128
-    gather = Gather(pc, ml_ref, gsems, 0)
+    gather = Gather(pc, ml_ref, gsems)
     mid_low = gmid_ref[...].astype(bf16)
-    ml_ref[pc.slot] = mid_low
+    ml_ref[pc.slot] = mid_low.reshape(sz.images, sz.part, sz.d)
+    greeting.wait()
     gather.start()
     beside.part(0)
     vec_ref[...] = jnp.zeros_like(vec_ref)
     vec_ref[2:3, :] = jnp.sum(mid_low.astype(f32), axis=0, keepdims=True)
     unpack_out(sz, w_ref, o_ref)
-
-    def mix(step, carry):
-        at = gather.arrive(step)
-        grads = ml_ref[pl.ds(2 * at, 2)].reshape(sz.tile, sz.d)
-        mg_ref[at] = dot(grads, o_ref[...], (1, 0)).astype(bf16)
-        return carry
-
-    lax.fori_loop(0, sz.chips, mix, 0)
-    gather.finish()
-    beside.part(1)
     dk_ref[...] = jnp.zeros_like(dk_ref)
     dv_ref[...] = jnp.zeros_like(dv_ref)
     dqv_ref[...] = jnp.zeros_like(dqv_ref)
     scale = HEAD_DIM ** (-0.5)
 
-    def attend(at, carry):
+    def attend(step, carry):
+        unit, at, piece = gather.ready(step)
+        mixed_grad = dot(gather.tokens(at, piece), o_ref[...], (1, 0)).astype(bf16)
+        gather.ahead(step)
         keys = k_ref[...].reshape(sz.keys, sz.headp)
         values = v_ref[...].reshape(sz.keys, sz.headp)
         total = jnp.zeros((sz.tile, sz.headp), f32)
         for head in range(sz.heads):
-            q_head = head_of(q_ref[at], head)
-            g_head = head_of(mg_ref[at], head)
+            q_head = head_of(q_ref[unit], head)
+            g_head = head_of(mixed_grad, head)
             probs = probabilities(q_head, keys, valid_ref[...])
             dprobs = dot(g_head, values, (1, 1))
             inner = jnp.sum(probs * dprobs, axis=-1, keepdims=True)
@@ -660,21 +785,22 @@
             dv_ref[...] += dot(probs.astype(bf16), g_head, (0, 0))
         dq = (scale * total).astype(bf16).astype(f32)
         dqv_ref[0:1, :] += jnp.sum(dq, axis=0, keepdims=True)
-        stack_ref[at, :, 0:sz.headp] = dq.astype(bf16)
-        beside.at(at, {1: 2, 3: 3})
+        stack_ref[unit, :, 0:sz.headp] = dq.astype(bf16)
+        beside.at(step, {2: 1, 4: 2, 6: 3})
         return carry
 
-    lax.fori_loop(0, sz.chips, attend, 0)
+    lax.fori_loop(0, sz.units, attend, 0)
+    gather.finish()
     beside.rest(4)
-    scatter = Scatter(pc, bufs, ssems, 0)
+    scatter = Scatter(pc, bufs, ssems, True)
 
     def back_project(step, carry):
-        at = pc.index(pc.chip_back(step))
-        rows = pl.ds(pl.multiple_of(at * sz.tile, sz.tile), sz.tile)
+        unit = scatter.unit(step)
+        rows = pl.ds(pl.multiple_of(unit * sz.tile, sz.tile), sz.tile)
         dk = (scale * dk_ref[rows, :]).astype(bf16).astype(f32)
         dv = dv_ref[rows, :].astype(bf16).astype(f32)
         dqv_ref[1:2, :] += jnp.sum(dv, axis=0, keepdims=True)
-        dq = stack_ref[at, :, 0:sz.headp].astype(f32)
+        dq = stack_ref[unit, :, 0:sz.headp].astype(f32)
         total = jnp.pad(dq, ((0, 0), (0, sz.qkvp - sz.headp)))
         for kind, piece in ((1, dk), (2, dv)):
             start = kind * sz.wide // 128 * 128
@@ -682,11 +808,11 @@
             moved = pltpu.roll(piece, shift, 1) if shift else piece
             total = total + jnp.pad(moved, ((0, 0), (start, sz.qkvp - start - sz.headp)))
         stacked = total.astype(bf16)
-        stack_ref[at] = stacked
+        stack_ref[unit] = stacked
         scatter.push(step, dot(stacked, w_ref[:, 0:sz.qkvp], (1, 1)))
         return carry
 
-    lax.fori_loop(0, sz.chips, back_project, 0)
+    lax.fori_loop(0, sz.units, back_project, 0)
     scatter.flush()
     o_at = 3 * sz.wide // 128 * 128
     o_shift = 3 * sz.wide - o_at
@@ -694,9 +820,9 @@
     def grads_attn(i, carry):
         lanes = pl.ds(pl.multiple_of(i * span, 128), span)
         stacked = stack_ref[...].reshape(sz.keys, sz.qkvp)
-        dqkv = dot(n1_ref[:, :, lanes].reshape(sz.keys, span), stacked, (0, 0))
+        dqkv = dot(by_unit(sz, n1_ref[:, :, :, lanes]), stacked, (0, 0))
         mixed = mixed_ref[...].reshape(sz.keys, sz.headp)
-        dout = dot(ml_ref[:, :, lanes].reshape(sz.keys, span), mixed, (0, 0))
+        dout = dot(by_unit(sz, ml_ref[:, :, :, lanes]), mixed, (0, 0))
         if o_shift:
             dout = pltpu.roll(dout, o_shift, 1)
         total = jnp.pad(dqkv, ((0, 0), (0, sz.attnp - sz.qkvp))) + jnp.pad(
@@ -731,14 +857,13 @@
     return jnp.pad(piece, ((0, 0), (to, width - to - piece.shape[-1])))
 
 
-def open_kernel(sz, wqkv_ref, wout_ref, wup_ref, wdown_ref, tokens_ref, valid_ref, *refs):
+def open_kernel(sz, wqkv_ref, wout_ref, wup_ref, wdown_ref, tokens_ref, valid_ref, gain_ref, shift_ref, *refs):
     n = sz.layers
-    everything, attn_refs, ff_refs, (stream_ref, grad_ref), (attn0_ref, mine_ref, tsems, wsems) = split_refs(
-        refs, 1, n - 1, n, 2, 4
-    )
+    everything, attn_refs, ff_refs, (stream_ref, grad_ref, n1_ref), own = split_refs(refs, 1, n - 1, n, 3, 5)
+    attn0_ref, mine_ref, tsems, gsems, wsems = own
     attn_refs = [attn0_ref] + list(attn_refs)
     pc = Place(sz)
-    greet(weight_peers(pc))
+    greet(team_peers(pc) + weight_peers(pc, True))
 
     def swap(step):
         zh = (pc.zh + step) % sz.images
@@ -760,39 +885,50 @@
             pieces = [(wqkv_ref[layer], kind * full + half * sz.wide, sz.wide, kind * sz.wide) for kind in range(3)]
             pack(attn_refs[layer], half, pieces + [(wout_ref[layer], half * sz.wide, sz.wide, 3 * sz.wide)])
 
+    for step in range(1, sz.images):
+        swap(step).start()
     pack_attn(0)
     move = Fetch(pc, attn0_ref, everything[0], wsems)
     move.parts[0]()
+    mine_ref[pc.zh] = tokens_ref[pc.zh]
     for step in range(1, sz.images):
-        swap(step).start()
+        swap(step).wait()
     move.parts[1]()
-    mine_ref[pc.zh] = tokens_ref[pc.zh]
+    stream = mine_ref[:, 0].reshape(sz.block, sz.d).astype(f32)
+    stream_ref[...] = stream
+    gather = Gather(pc, n1_ref, gsems, FF_TURN)
+    gather_norm(pc, None, gather, stream, gain_ref[0:1, :], shift_ref[0:1, :])
+    grad_ref[...] = mine_ref[:, 1].reshape(sz.block, sz.d).astype(f32) * valid_ref[...]
+    move.parts[2]()
+    for layer in range(1, n):
+        pack_attn(layer)
+    move.parts[3]()
     for layer in range(n):
-        if layer:
-            pack_attn(layer)
         for half in range(sz.zl):
             pack(ff_refs[layer], half, [(wup_ref[layer], half * sz.ff, sz.ff, 0),
                                         (wdown_ref[layer], half * sz.ff, sz.ff, sz.ff)])
-    for step in range(1, sz.images):
-        swap(step).wait()
-    stream_ref[...] = mine_ref[:, 0].reshape(sz.block, sz.d).astype(f32)
-    grad_ref[...] = mine_ref[:, 1].reshape(sz.block, sz.d).astype(f32) * valid_ref[...]
-    for part in move.parts[2:]:
+    for step in range(sz.units):
+        gather.forward(step)
+        gather.ready(step)
+    for part in move.parts[4:]:
         part()
+    gather.finish()
     move.finish()
 
 
-def open_call(sz, w_qkv, w_out, w_up, w_down, tokens, own_valid):
+def open_call(sz, w_qkv, w_out, w_up, w_down, tokens, own_valid, gains, shifts):
     attn, ff = ((sz.zl, sz.wrowsp, sz.attnp), bf16), ((sz.zl, sz.wrowsp, sz.ffw), bf16)
     own = ((sz.block, sz.d), f32)
-    shapes = Fetch.result(sz, sz.attnp) + [attn] * (sz.layers - 1) + [ff] * sz.layers + [own, own]
-    operands = (w_qkv.reshape(sz.layers, sz.wrows, -1), w_out, w_up, w_down, tokens, own_valid)
+    team = ((sz.team, sz.images, sz.part, sz.d), bf16)
+    shapes = Fetch.result(sz, sz.attnp) + [attn] * (sz.layers - 1) + [ff] * sz.layers + [own, own, team]
+    operands = (w_qkv.reshape(sz.layers, sz.wrows, -1), w_out, w_up, w_down, tokens, own_valid, gains, shifts)
     return pl.pallas_call(
         functools.partial(open_kernel, sz),
         out_shape=[jax.ShapeDtypeStruct(*s) for s in shapes],
         in_specs=whole(len(operands)),
         out_specs=whole(len(shapes)),
-        scratch_shapes=[VMEM(*attn), VMEM(tokens.shape, bf16), DMA((2, sz.images))] + Fetch.scratch(sz, 0),
+        scratch_shapes=[VMEM(*attn), VMEM(tokens.shape, bf16), DMA((2, sz.images)), DMA((4, sz.chips, sz.images))]
+        + Fetch.scratch(sz, 0),
         compiler_params=params(9),
         name="open",
     )(*operands)
@@ -987,17 +1123,21 @@
     tokens = jnp.stack([pieces(inputs), pieces(cotangent)], axis=1)
 
     row = jnp.arange(sz.keys, dtype=jnp.int32)
-    of_slot, within = row // sz.block, row % sz.block
-    token = (of_slot % sz.tp) * sz.part + within % sz.part
-    source = (within // sz.part) * sz.zl + of_slot // sz.tp
-    position = source * sz.rows + token
+    unit, within = row // sz.tile, row % sz.tile
+    of_slot = unit // sz.images * 2 + within // sz.part
     count = lax.dynamic_index_in_dim(valid_count, zh, keepdims=False)
-    valid = ((token < sz.rows) & (position < count)).astype(f32)
-    own_valid = lax.dynamic_slice_in_dim(valid, slot * sz.block, sz.block)[:, None]
-    valid = valid[None, :]
-
-    attn0, *rest = open_call(sz, w_qkv, w_out, w_up, w_down, tokens, own_valid)
-    own_attn, own_ff, (stream, grad) = split_refs(rest, n - 1, n, 2)
+
+    def valid_at(slots, piece, place):
+        token = slots % sz.tp * sz.part + place
+        position = (piece * sz.zl + slots // sz.tp) * sz.rows + token
+        return ((token < sz.rows) & (position < count)).astype(f32)
+
+    valid = valid_at(of_slot, unit % sz.images, within % sz.part)[None, :]
+    mine = jnp.arange(sz.block, dtype=jnp.int32)
+    own_valid = valid_at(slot, mine // sz.part, mine % sz.part)[:, None]
+
+    attn0, *rest = open_call(sz, w_qkv, w_out, w_up, w_down, tokens, own_valid, norm_gain[0], norm_bias[0])
+    own_attn, own_ff, (stream, grad, normed) = split_refs(rest, n - 1, n, 3)
     own_attn = [None] + list(own_attn)
 
     def half(a, to):
@@ -1012,9 +1152,9 @@
         return jnp.pad(dw, ((0, 0), (0, sz.wrowsp - sz.wrows), (0, 0)))
 
     own = ((sz.block, sz.d), f32)
-    team = ((sz.team, sz.block, sz.d), bf16)
-    head = ((sz.chips, sz.tile, sz.headp), bf16)
-    hidden = (sz.chips, sz.tile, sz.ffp)
+    team = ((sz.team, sz.images, sz.part, sz.d), bf16)
+    head = ((sz.units, sz.tile, sz.headp), bf16)
+    hidden = (sz.units, sz.tile, sz.ffp)
     vec = ((8, sz.d), f32)
     o_scratch = VMEM((sz.d, sz.headp), bf16)
 
@@ -1022,11 +1162,18 @@
     streams, attn_kept, ff_kept, middles = [], [], [], []
     for l in range(n):
         streams.append(stream)
-        middle, *kept, fetched = layer_call(
-            sz, "attn_forward", 1, attn_forward,
-            (stream, w_attn[l], norm_gain[l], norm_bias[l], half(bias_qv[l], sz.headp), bias_resid[l], valid),
-            [own, team] + [head] * 4, [o_scratch], 1, 1, Fetch, own_ff[l],
-        )
+        operands = (stream, w_attn[l], norm_gain[l], norm_bias[l], half(bias_qv[l], sz.headp), bias_resid[l], valid)
+        if l == 0:
+            middle, *kept, fetched = layer_call(
+                sz, "attn_forward_first", 7, functools.partial(attn_forward, True), operands + (normed,),
+                [own] + [head] * 4, [o_scratch], Fetch, own_ff[l],
+            )
+            kept = [normed] + kept
+        else:
+            middle, *kept, fetched = layer_call(
+                sz, "attn_forward", 1, functools.partial(attn_forward, False), operands,
+                [own, team] + [head] * 4, [o_scratch], Fetch, own_ff[l],
+            )
         w_ff[l] = joined(fetched)
         middles.append(middle)
         attn_kept.append(kept)
@@ -1034,7 +1181,7 @@
         stream, *kept = layer_call(
             sz, "ff_forward_last" if last else "ff_forward", 3 if last else 2, ff_forward,
             (middle, w_ff[l], norm_gain[l], norm_bias[l], half(bias_up[l][None], sz.ffp), bias_resid[l]),
-            [own, team, (hidden, f32), (hidden, bf16)], [], 1, 1,
+            [own, team, (hidden, f32), (hidden, bf16)], [],
             *(() if last else (Fetch, own_attn[l + 1])),
         )
         if not last:
@@ -1049,7 +1196,7 @@
             sz, "ff_backward_last" if last else "ff_backward", 5 if last else 4, ff_backward,
             (grad, middles[l], *ff_kept[l], w_ff[l], norm_gain[l]),
             [own, ((sz.d, sz.ffw), bf16), vec, ((1, sz.ffp), f32)],
-            [VMEM(*team), VMEM(hidden, bf16)], 1, 1, *(() if last else (Give, blocks(pending))),
+            [VMEM(*team), VMEM(hidden, bf16)], *(() if last else (Give, blocks(pending))),
         )
         if not last:
             attn_sums[l + 1] = summed[0]
@@ -1057,9 +1204,9 @@
             sz, "attn_backward", 6, attn_backward,
             (gmid, streams[l], *attn_kept[l], w_attn[l], norm_gain[l], valid),
             [own, ((sz.d, sz.attnp), bf16), vec, ((2, sz.headp), f32)],
-            [o_scratch, VMEM(*team), VMEM(*head), VMEM((sz.keys, sz.headp), f32), VMEM((sz.keys, sz.headp), f32),
-             VMEM((sz.chips, sz.tile, sz.qkvp), bf16)],
-            1, 1, Give, blocks(dw_ff),
+            [o_scratch, VMEM(*team), VMEM((sz.keys, sz.headp), f32), VMEM((sz.keys, sz.headp), f32),
+             VMEM((sz.units, sz.tile, sz.qkvp), bf16)],
+            Give, blocks(dw_ff),
         )
     attn_sums[0], ends, small = give_call(sz, blocks(pending), stream, grad, ff_vecs, attn_vecs, dqvs, dups)
     return close_call(sz, attn_sums, ff_sums, ends, small)

time: 509 us -> 477 us (0.937)
  Pallas kernels: 490 us -> 458 us
    pallas_call x8, Pallas kernels: 386 us -> 356 us  [layer_call(): pl.pallas_call(functools.partial(layer_kernel, body, len(operands), len(s...]
where the time goes in v3:
time: 477 us
  Pallas kernels  458 us (96%)
  local copies, waits for them, and re-layouts  14.5 us (3%)
    pallas_call x8, Pallas kernels, layer_call(): pl.pallas_call(functools.partial(layer_kernel, body, len(operands), len(s...  356 us
    pallas_call x1, Pallas kernels, give_call(): pl.pallas_call(functools.partial(give_kernel, sz), out_shape=[jax.ShapeDt...  48.5 us
    pallas_call x1, Pallas kernels, open_call(): pl.pallas_call(functools.partial(open_kernel, sz), out_shape=[jax.ShapeDt...  46.2 us

profile of v3, /device:TPU:0, one launch (start us, length us, event | category | flops | bytes accessed | tf_op | source)
XLA Modules:
  0.0 476.8 jit_solution(1713901551945423458)
XLA Ops:
  0.7 1.3 dynamic_slice.26
  2.0 1.3 and_convert_fusion.refs_6_.refs_9_
  3.3 0.7 fusion.21
  4.2 0.6 pad.25.refs_4_
  5.4 0.8 slice_reduce_fusion
  7.5 1.3 slice_bitcast_fusion
  8.9 1.4 slice_bitcast_fusion.1
  10.2 1.3 fusion.15.valid_ref
  11.5 1.1 fusion
  12.6 0.8 pad_maximum_fusion.tokens_ref
  13.8 1.3 reshape.371.wqkv_ref
  15.0 46.2 %open.1 = (bf16[8,144,640]{2,1,0:T(8,128)(2,1)}, bf16[2,144,640]{2,1,0:T(8,128)(2,1)}, bf16[2,144,1152]{2,1,0:T(8,128)(2,1)}, bf16[2,144,1152]{2,1,0:T(8,128)(2,...) custom-call(bf16[2,144,864]{2,1,0:T(8,128)(2,1)} %reshape.371.wqkv_ref, ...), custom_call_target="tpu_custom_call" | custom-call | tf_op jit(solution)/shard_map/open/pallas_call | solution.py:925
  61.3 47.1 %attn_forward_first.1 = (f32[96,1152]{1,0:T(8,128)}, bf16[8,96,256]{2,1,0:T(8,128)(2,1)}, bf16[8,96,256]{2,1,0:T(8,128)(2,1)}, bf16[8,96,256]{2,1,0:T(8,128)(2,1...) custom-call(f32[96,1152]{1,0:T(8,128)} %get-tuple-element.74.refs_0_.refs_1_, bf16[1152,640]{1,0:T(8,128)(2,1)} %bitcast.41, ...), custom_call_target="tpu_custom_call" | custom-call | tf_op jit(solution)/shard_map/attn_forward_first/pallas_call | solution.py:586
  108.3 36.4 %ff_forward.1 = (f32[96,1152]{1,0:T(8,128)}, bf16[8,2,48,1152]{3,2,1,0:T(8,128)(2,1)}, f32[8,96,640]{2,1,0:T(8,128)}, bf16[8,96,640]{2,1,0:T(8,128)(2,1)}, bf16[8,144,640]{2,1,0:T(8,128)(2,1)}) custom-call(f32[96,1152]{1,0:T(8,128)} %get-tuple-element.78.refs_0_.refs_1_, bf16[1152,1152]{1,0:T(8,128)(2,1)} %bitcast.37, ...), custom_call_target="tpu_custom_call" | custom-call | tf_op jit(solution)/shard_map/ff_forward/pallas_call | solution.py:586
  144.8 54.9 %attn_forward.1 = (f32[96,1152]{1,0:T(8,128)}, bf16[8,2,48,1152]{3,2,1,0:T(8,128)(2,1)}, bf16[8,96,256]{2,1,0:T(8,128)(2,1)}, bf16[8,96,256]{2,1,0:T(8,128)(2,1)...) custom-call(f32[96,1152]{1,0:T(8,128)} %get-tuple-element.81.refs_0_.refs_1_, ...), custom_call_target="tpu_custom_call" | custom-call | tf_op jit(solution)/shard_map/attn_forward/pallas_call | solution.py:586
  199.7 31.5 %ff_forward_last.1 = (f32[96,1152]{1,0:T(8,128)}, bf16[8,2,48,1152]{3,2,1,0:T(8,128)(2,1)}, f32[8,96,640]{2,1,0:T(8,128)}, bf16[8,96,640]{2,1,0:T(8,128)(2,1)}) custom-call(f32[96,1152]{1,0:T(8,128)} %get-tuple-element.84.refs_0_.refs_1_, bf16[1152,1152]{1,0:T(8,128)(2,1)} %bitcast.35, f32[2,1152]{1,0:T(2,128)} %get-tuple-element.181.refs_2_.refs_6_.refs_8_, ...), custom_call_target="tpu_custom_call" | custom-call | tf_op jit(solution)/shard_map/ff_forward_last/pallas_call | solution.py:586
  231.2 32.6 %ff_backward_last.1 = (f32[96,1152]{1,0:T(8,128)}, bf16[1152,1152]{1,0:T(8,128)(2,1)}, f32[8,1152]{1,0:T(8,128)}, f32[1,640]{1,0:T(1,128)}) custom-call(f32[96,1152]{1,0:T(8,128)} %get-tuple-element.73.refs_0_, f32[96,1152]{1,0:T(8,128)} %get-tuple-element.84.refs_0_.refs_1_, bf16[8,2,48,1152]{3,2,1,0:T(8,128)(2,1)} %get-tuple-element.86.refs_2_, ...), custom_call_target="tpu_custom_call" | custom-call | tf_op jit(solution)/shard_map/ff_backward_last/pallas_call | solution.py:586
  263.9 54.9 %attn_backward.2 = (f32[96,1152]{1,0:T(8,128)}, bf16[1152,640]{1,0:T(8,128)(2,1)}, f32[8,1152]{1,0:T(8,128)}, f32[2,256]{1,0:T(2,128)}, f32[2,144,1152]{2,1,0:T(8,128)}) custom-call(f32[96,1152]{1,0:T(8,128)} %get-tuple-element.89.refs_0_, f32[96,1152]{1,0:T(8,128)} %get-tuple-element.81.refs_0_.refs_1_, bf16[8,2,48,1152]{3,2,1,0:T(8,128)(2,1)} %get-tuple-element.90.refs_2_, ...), custom_call_target="tpu_custom_call" | custom-call | tf_op jit(solution)/shard_map/attn_backward/pallas_call | solution.py:586
  318.8 43.4 %ff_backward.1 = (f32[96,1152]{1,0:T(8,128)}, bf16[1152,1152]{1,0:T(8,128)(2,1)}, f32[8,1152]{1,0:T(8,128)}, f32[1,640]{1,0:T(1,128)}, f32[2,144,640]{2,1,0:T(8,128)}) custom-call(f32[96,1152]{1,0:T(8,128)} %get-tuple-element.96.refs_0_, f32[96,1152]{1,0:T(8,128)} %get-tuple-element.78.refs_0_.refs_1_, bf16[8,2,48,1152]{3,2,1,0:T(8,128)(2,1)} %get-tuple-element.97.refs_2_, ...), custom_call_target="tpu_custom_call" | custom-call | tf_op jit(solution)/shard_map/ff_backward/pallas_call | solution.py:586
  362.2 55.6 %attn_backward.3 = (f32[96,1152]{1,0:T(8,128)}, bf16[1152,640]{1,0:T(8,128)(2,1)}, f32[8,1152]{1,0:T(8,128)}, f32[2,256]{1,0:T(2,128)}, f32[2,144,1152]{2,1,0:T(8,128)}) custom-call(f32[96,1152]{1,0:T(8,128)} %get-tuple-element.101.refs_0_, f32[96,1152]{1,0:T(8,128)} %get-tuple-element.74.refs_0_.refs_1_, ...), custom_call_target="tpu_custom_call" | custom-call | tf_op jit(solution)/shard_map/attn_backward/pallas_call | solution.py:586
  417.8 48.5 %give_rest.1 = (f32[2,144,640]{2,1,0:T(8,128)}, bf16[4,2,2,48,1152]{4,3,2,1,0:T(8,128)(2,1)}, f32[4,8,1152]{2,1,0:T(8,128)}) custom-call(bf16[8,144,640]{2,1,0:T(8,128)(2,1)} %bitcast.45, f32[96,1152]{1,0:T(8,128)} %get-tuple-element.108.stream_ref, f32[96,1152]{1,0:T(8,128)} %get-tuple-element.109.grad_ref, f32[8,1152]{1,0:T(8,128)} %get-tuple-element.110.refs_0_, ...), custom_call_target="tpu_custom_call" | custom-call | tf_op jit(solution)/shard_map/give_rest/pallas_call | solution.py:1030
  466.3 6.9 %close.1 = (bf16[2,184,1152]{2,1,0:T(8,128)(2,1)}, f32[2,184,1152]{2,1,0:T(8,128)}, f32[2,2,1152]{2,1,0:T(2,128)}, f32[2,2,1152]{2,1,0:T(2,128)}, f32[2,144,864]...) custom-call(f32[2,144,640]{2,1,0:T(8,128)} %get-tuple-element.118.re, ...), custom_call_target="tpu_custom_call" | custom-call | tf_op jit(solution)/shard_map/close/pallas_call | solution.py:1098
  473.2 2.4 reshape.380
  475.7 1.1 copy.35
  (14 shorter events, 2.4 us)
Async XLA Ops:
  0.6 12.8 %copy-start = (bf16[2,144,3,288]{3,1,2,0:T(8,128)(2,1)S(1)}, bf16[2,144,3,288]{3,1,2,0:T(8,128)(2,1)}, u32[]{:S(2)}) copy-start(bf16[2,144,3,288]{3,1,2,0:T(8,128)(2,1)} %param.17) | copy-start | bytes 1492996

commit v4 on v3

v4 whole, which is shorter than its diff:
```python
import functools

import jax
import jax.numpy as jnp
from jax import lax
from jax.experimental import pallas as pl
from jax.experimental.pallas import tpu as pltpu
from jax.sharding import PartitionSpec as P

HEAD_DIM = 72
norm_eps = 1e-06
gelu_root = 0.7978845608028654
gelu_cubic = 0.044715
masked_score = -1e30

MESH = pl.DeviceIdType.MESH
f32 = jnp.float32
bf16 = jnp.bfloat16
VMEM = pltpu.VMEM
DMA = pltpu.SemaphoreType.DMA


def up_to(value, unit):
    return (value + unit - 1) // unit * unit


def dot(a, b, over):
    return lax.dot_general(a, b, (((over[0],), (over[1],)), ((), ())), preferred_element_type=f32)


class Sizes:
    def __init__(self, mesh, inputs, w_qkv, w_up):
        self.fsdp, self.ctx, self.tp = mesh.shape["fsdp"], mesh.shape["ctx"], mesh.shape["tp"]
        self.images, self.rows, self.d = inputs.shape
        self.layers, self.wrows = w_qkv.shape[0], w_qkv.shape[1]
        self.zl = self.ctx // self.images
        self.chips_y = self.tp // 2
        self.chips = self.zl * self.chips_y
        self.team = self.chips * 2
        self.part = up_to(-(-self.rows // self.tp), 16)
        self.block = self.images * self.part
        self.units = self.chips * self.images
        self.tile = 2 * self.part
        self.keys = self.units * self.tile
        self.wide = w_qkv.shape[3] // self.zl
        self.heads = self.wide // HEAD_DIM
        self.ff = w_up.shape[2] // self.zl
        self.ffw = up_to(2 * self.ff, 128)
        self.down_at = self.ff // 128 * 128
        self.down_shift = self.ff - self.down_at
        self.ffp = self.ffw - self.down_at
        self.headp = up_to(self.wide, 128)
        self.qkvp = up_to(3 * self.wide, 128)
        self.attnp = up_to(4 * self.wide, 128)
        self.wrowsp = up_to(self.wrows, 16)
        self.groups = self.fsdp * self.ctx


class Place:
    def __init__(self, sz):
        self.sz = sz
        self.f, self.c, self.t = lax.axis_index("fsdp"), lax.axis_index("ctx"), lax.axis_index("tp")
        self.zh, self.zl = self.c // sz.zl, self.c % sz.zl
        self.y, self.k = self.t // 2, self.t % 2
        self.chip = self.zl * sz.chips_y + self.y
        self.slot = 2 * self.chip + self.k

    def chip_at(self, step):
        sz = self.sz
        zl = (self.zl + step // sz.chips_y) % sz.zl
        y = (self.y + step % sz.chips_y) % sz.chips_y
        return zl, y

    def chip_back(self, step):
        sz = self.sz
        zl = (self.zl + sz.zl - step // sz.chips_y) % sz.zl
        y = (self.y + sz.chips_y - step % sz.chips_y) % sz.chips_y
        return zl, y

    def index(self, chip):
        return chip[0] * self.sz.chips_y + chip[1]

    def device(self, chip):
        return (self.f, self.zh * self.sz.zl + chip[0], 2 * chip[1] + self.k)

    @property
    def twin(self):
        return (self.f, self.c, self.t + 1 - 2 * self.k)


    def ctx_ahead(self, step):
        sz = self.sz
        return (self.zh + step // sz.zl) % sz.images * sz.zl + (self.zl + step % sz.zl) % sz.zl

    def ctx_back(self, step):
        sz = self.sz
        zh = (self.zh + sz.images - step // sz.zl) % sz.images
        return zh * sz.zl + (self.zl + sz.zl - step % sz.zl) % sz.zl


def split_refs(refs, *counts):
    out, at = [], 0
    for count in counts:
        out.append(refs[at:at + count])
        at += count
    assert at == len(refs)
    return out


class Greeting:
    def __init__(self, others):
        self.count = len(others)
        self.barrier = pltpu.get_barrier_semaphore()
        for other in others:
            pl.semaphore_signal(self.barrier, inc=1, device_id=other, device_id_type=MESH)

    def wait(self):
        pl.semaphore_wait(self.barrier, self.count)


def send(src, dst, send_sem, recv_sem, device):
    return pltpu.make_async_remote_copy(
        src_ref=src, dst_ref=dst, send_sem=send_sem, recv_sem=recv_sem, device_id=device, device_id_type=MESH
    )


def team_peers(pc):
    return [pc.device(pc.chip_at(step)) for step in range(1, pc.sz.chips)] + [pc.twin]


def line_peers(pc):
    sz = pc.sz
    return [(pc.f, pc.c, 2 * ((pc.y + dy) % sz.chips_y) + 1 - pc.k) for dy in range(1, sz.chips_y)]


def weight_peers(pc, team=False):
    sz = pc.sz
    first = sz.zl if team else 1
    return [(pc.f, pc.ctx_ahead(step), pc.t) for step in range(first, sz.ctx)] + [
        ((pc.f + jump) % sz.fsdp, pc.c, pc.t) for jump in range(1, sz.fsdp)
    ]


def pick(step, values):
    if isinstance(step, int):
        return values[step]
    out = jnp.int32(values[0])
    for i in range(1, len(values)):
        out = jnp.where(step == i, jnp.int32(values[i]), out)
    return out


def when(condition, run):
    if isinstance(condition, (bool, int)):
        if condition:
            run()
    else:
        pl.when(condition)(run)


class Routes:
    def __init__(self, sz):
        self.sz = sz
        pieces = range(sz.images)
        z = [dz * sz.chips_y for dz in range(1, sz.zl)]
        y = list(range(1, sz.chips_y))
        self.straight = z + y
        self.turned = [dz + dy for dz in z for dy in y]
        own = [(0, p) for p in pieces]
        near = [(b, p) for p in pieces for b in self.straight]
        far = [(b, p) for p in pieces for b in self.turned]
        self.arriving = own + near + far
        self.leaving = far + [(b, p) for b in z for p in pieces] + [(b, p) for b in y for p in pieces] + own


def backs(order):
    return [b for b, _ in order]


def pieces_of(order):
    return [p for _, p in order]


class Gather:
    def __init__(self, pc, buf, sems, turn_z=()):
        self.pc, self.buf, self.sems = pc, buf, sems
        self.routes = Routes(pc.sz)
        self.order = self.routes.arriving
        self.turn_z = turn_z

    def put(self, low):
        sz = self.pc.sz
        self.buf[self.pc.slot] = low.reshape(sz.images, sz.part, sz.d)

    def move(self, kind, back, piece, slot, device):
        return send(self.buf.at[slot, piece], self.buf.at[slot, piece], self.sems.at[kind, back, piece],
                    self.sems.at[kind + 1, back, piece], device)

    def near(self, back, piece, slot):
        return self.move(2, back, piece, slot, self.pc.twin)

    def start(self):
        pc = self.pc
        for piece in range(pc.sz.images):
            for step in self.routes.straight:
                self.move(0, step, piece, pc.slot, pc.device(pc.chip_at(step))).start()
            self.near(0, piece, pc.slot).start()

    def relays(self, back, piece):
        sz = self.pc.sz
        if back == 0 or back in self.routes.turned:
            return []
        if back % sz.chips_y == 0:
            return [] if piece in self.turn_z else [(back + dy, dy) for dy in range(1, sz.chips_y)]
        return [(back + dz * sz.chips_y, dz * sz.chips_y) for dz in range(1, sz.zl)] if piece in self.turn_z else []

    def forward(self, step):
        pc, order = self.pc, self.order
        back, piece = pick(step, backs(order)), pick(step, pieces_of(order))
        slot = 2 * pc.index(pc.chip_back(back)) + pc.k

        def other():
            self.move(0, back, piece, slot, pc.twin).wait_recv()
            self.near(back, piece, slot).start()

        when(back > 0, other)
        for at, (b, p) in enumerate(order):
            for seen, ahead in self.relays(b, p):
                when(step == at, self.move(0, seen, p, slot, pc.device(pc.chip_at(ahead))).start)

    def ready(self, step):
        pc = self.pc
        back, piece = pick(step, backs(self.order)), pick(step, pieces_of(self.order))
        at = pc.index(pc.chip_back(back))
        self.near(back, piece, 2 * at + 1 - pc.k).wait_recv()
        return at * pc.sz.images + piece, at, piece

    def ahead(self, step):
        if isinstance(step, int):
            if step + 1 < len(self.order):
                self.forward(step + 1)
        else:
            pl.when(step + 1 < len(self.order))(lambda: self.forward(step + 1))

    def tokens(self, at, piece):
        sz = self.pc.sz
        return self.buf[pl.ds(2 * at, 2), piece].reshape(sz.tile, sz.d)

    def finish(self):
        pc = self.pc
        for b, p in self.order:
            if b:
                self.move(0, b, p, pc.slot, pc.twin).wait_send()
            self.near(b, p, pc.slot).wait_send()


class Scatter:
    def __init__(self, pc, bufs, sems, turn):
        self.pc, self.sems, self.turn = pc, sems, turn
        self.both, self.keep, self.tsend, self.trecv, self.rsend, self.rrecv = bufs
        self.routes = Routes(pc.sz)
        self.order = self.routes.leaving if turn else self.routes.arriving

    def near(self, back, piece):
        return send(self.tsend.at[back, piece], self.trecv.at[back, piece], self.sems.at[0, back, piece],
                    self.sems.at[1, back, piece], self.pc.twin)

    def far(self, back, piece):
        pc, sz = self.pc, self.pc.sz
        to = back
        if self.turn:
            if isinstance(back, int):
                to = back % sz.chips_y or back
            else:
                dy = lax.rem(back, jnp.int32(sz.chips_y))
                to = jnp.where(dy > 0, dy, back)
        return send(self.rsend.at[back, piece], self.rrecv.at[back, piece], self.sems.at[2, back, piece],
                    self.sems.at[3, back, piece], pc.device(pc.chip_back(to)))

    def at(self, step):
        return pick(step, backs(self.order)), pick(step, pieces_of(self.order))

    def unit(self, step):
        back, piece = self.at(step)
        return self.pc.index(self.pc.chip_back(back)) * self.pc.sz.images + piece

    def push(self, step, partial):
        pc = self.pc
        back, piece = self.at(step)
        self.both[...] = partial.reshape(2, pc.sz.part, partial.shape[-1])
        self.tsend[back, piece] = self.both[1 - pc.k].astype(bf16)
        self.near(back, piece).start()
        self.keep[back, piece] = self.both[pc.k]
        pl.when(step > 0)(lambda: self.relay(step - 1))

    def relay(self, step):
        sz = self.pc.sz
        back, piece = self.at(step)
        self.near(back, piece).wait_recv()
        self.keep[back, piece] += self.trecv[back, piece].astype(f32)
        if self.turn:
            for at, (b, p) in enumerate(self.order):
                if b and b % sz.chips_y == 0:

                    def extra(b=b, p=p):
                        for dy in range(1, sz.chips_y):
                            self.far(b + dy, p).wait_recv()
                            self.keep[b, p] += self.rrecv[b + dy, p].astype(f32)

                    when(step == at, extra)

        def leave():
            self.rsend[back, piece] = self.keep[back, piece].astype(bf16)
            self.far(back, piece).start()

        when(back > 0, leave)

    def flush(self):
        self.relay(self.pc.sz.units - 1)

    def finish(self):
        sz = self.pc.sz
        total = self.keep[0]
        for back in range(1, sz.chips):
            if self.turn and back in self.routes.turned:
                continue
            for piece in range(sz.images):
                self.far(back, piece).wait_recv()
            total = total + self.rrecv[back].astype(f32)
        for back, piece in self.order:
            self.near(back, piece).wait_send()
            if back:
                self.far(back, piece).wait_send()
        return total.reshape(sz.block, sz.d)


def team_scratch(sz, phases):
    n = (sz.chips, sz.images)
    return [
        VMEM((2, sz.part, sz.d), f32),
        VMEM(n + (sz.part, sz.d), f32),
        VMEM(n + (sz.part, sz.d), bf16),
        VMEM(n + (sz.part, sz.d), bf16),
        VMEM(n + (sz.part, sz.d), bf16),
        VMEM(n + (sz.part, sz.d), bf16),
        DMA((phases, 4) + n),
        DMA((phases, 4) + n),
    ]


def normalised(values):
    centre = jnp.mean(values, axis=-1, keepdims=True)
    centred = values - centre
    spread = jnp.mean(centred * centred, axis=-1, keepdims=True)
    inverse = lax.rsqrt(spread + norm_eps)
    return centred * inverse, inverse


def norm_back(values, gain, grad):
    high, inverse = normalised(values)
    scaled = grad * gain
    term = inverse * (
        scaled
        - jnp.mean(scaled, axis=-1, keepdims=True)
        - high * jnp.mean(scaled * high, axis=-1, keepdims=True)
    )
    return term, jnp.sum(grad * high, axis=0, keepdims=True), jnp.sum(grad, axis=0, keepdims=True)


def lanes_of(shape):
    return lax.broadcasted_iota(jnp.int32, shape, len(shape) - 1)


def unpack_out(sz, w_ref, o_ref):
    at = 3 * sz.wide // 128 * 128
    shift = 3 * sz.wide - at

    def step(i, carry):
        rows = pl.ds(pl.multiple_of(i * 128, 128), 128)
        piece = pltpu.roll(w_ref[rows, at:at + sz.headp].astype(f32), sz.headp - shift, 1)
        o_ref[rows, :] = jnp.where(lanes_of(piece.shape) < sz.wide, piece, 0.0).astype(bf16)
        return carry

    lax.fori_loop(0, sz.d // 128, step, 0)


def take(sz, values, kind):
    at = kind * sz.wide // 128 * 128
    shift = kind * sz.wide - at
    piece = values[:, at:at + sz.headp]
    if shift:
        piece = pltpu.roll(piece, sz.headp - shift, 1)
    return jnp.where(lanes_of(piece.shape) < sz.wide, piece, 0.0)


def head_of(values, head):
    lanes = lanes_of(values.shape)
    mine = (lanes >= head * HEAD_DIM) & (lanes < (head + 1) * HEAD_DIM)
    return jnp.where(mine, values, jnp.zeros_like(values))


def probabilities(q_head, keys, valid):
    scores = dot(q_head, keys, (1, 1)) * HEAD_DIM ** (-0.5)
    scores = jnp.where(valid > 0.0, scores, masked_score)
    weights = jnp.exp(scores - jnp.max(scores, axis=-1, keepdims=True))
    return weights / jnp.sum(weights, axis=-1, keepdims=True)


FF_TURN = (1,)


class Jobs:
    def __init__(self, **places):
        self.places = places

    def run(self, place):
        for job in self.places.get(place, ()):
            job()

    def at(self, place, step):
        for when_step, jobs in self.places.get(place, {}).items():

            def run(jobs=jobs):
                for job in jobs:
                    job()

            when(step == when_step, run)


class Copies:
    def __init__(self, sems):
        self.sems, self.made = sems, []

    def start(self, src, dst):
        copy = pltpu.make_async_copy(src, dst, self.sems.at[len(self.made)])
        self.made.append(copy)
        copy.start()
        return copy

    def wait(self):
        for copy in self.made:
            copy.wait()


class Fetch:
    def __init__(self, pc, own, everything, sems):
        self.pc, self.own, self.all, self.sems = pc, own, everything, sems

    def rows(self, group):
        rows = self.pc.sz.wrowsp
        return self.all.at[pl.ds(pl.multiple_of(group * rows, 16), rows)]

    def along_ctx(self, step):
        pc = self.pc
        c = pc.ctx_ahead(step)
        return send(self.own.at[c % pc.sz.zl], self.rows(pc.f * pc.sz.ctx + pc.c), self.sems.at[0, 0, step],
                    self.sems.at[0, 1, step], (pc.f, c, pc.t))

    def own_copy(self):
        pc = self.pc
        return pltpu.make_async_copy(self.own.at[pc.zl], self.rows(pc.f * pc.sz.ctx + pc.c), self.sems.at[0, 0, 0])

    def along_fsdp(self, jump, step):
        pc, sz = self.pc, self.pc.sz
        rows = self.rows(pc.f * sz.ctx + pc.ctx_back(step))
        return send(rows, rows, self.sems.at[jump, 0, step], self.sems.at[jump, 1, step],
                    ((pc.f + jump) % sz.fsdp, pc.c, pc.t))

    def start(self):
        self.own_copy().start()
        for step in range(1, min(3, self.pc.sz.ctx)):
            self.along_ctx(step).start()

    def pass_own(self):
        self.own_copy().wait()
        for jump in range(1, self.pc.sz.fsdp):
            self.along_fsdp(jump, 0).start()

    def pass_on(self, step):
        if step >= self.pc.sz.ctx:
            return
        self.along_ctx(step).wait_recv()
        if step + 2 < self.pc.sz.ctx:
            self.along_ctx(step + 2).start()
        for jump in range(1, self.pc.sz.fsdp):
            self.along_fsdp(jump, step).start()

    def pass_rest(self):
        for step in range(3, self.pc.sz.ctx):
            self.pass_on(step)

    def part(self, step):
        return functools.partial(self.pass_on, step)

    def finish(self):
        sz = self.pc.sz
        for step in range(sz.ctx):
            if step:
                self.along_ctx(step).wait_send()
            for jump in range(1, sz.fsdp):
                self.along_fsdp(jump, step).wait()


class Give:
    def __init__(self, pc, dw, recv, got, sems):
        self.pc, self.dw, self.recv, self.got, self.sems = pc, dw, recv, got, sems
        self.order = list(range(pc.sz.ctx - 1, -1, -1))

    def rows(self, group):
        rows = self.pc.sz.wrowsp
        return pl.ds(pl.multiple_of(group * rows, 16), rows)

    def along_fsdp(self, jump, step):
        pc, sz = self.pc, self.pc.sz
        f = (pc.f + jump) % sz.fsdp
        return send(self.dw.at[self.rows(f * sz.ctx + pc.ctx_ahead(step))], self.got.at[jump - 1, step],
                    self.sems.at[jump, 0, step], self.sems.at[jump, 1, step], (f, pc.c, pc.t))

    def along_ctx(self, step):
        pc = self.pc
        return send(self.got.at[0, step], self.recv.at[pc.c], self.sems.at[0, 0, step], self.sems.at[0, 1, step],
                    (pc.f, pc.ctx_ahead(step), pc.t))

    def from_ctx(self, step):
        pc = self.pc
        return send(self.got.at[0, step], self.recv.at[pc.ctx_back(step)], self.sems.at[0, 0, step],
                    self.sems.at[0, 1, step], (pc.f, pc.ctx_back(step), pc.t))

    def own_copy(self):
        return pltpu.make_async_copy(self.got.at[0, 0], self.recv.at[self.pc.c], self.sems.at[0, 0, 0])

    def start(self):
        for step in self.order[:2]:
            for jump in range(1, self.pc.sz.fsdp):
                self.along_fsdp(jump, step).start()

    def pass_on(self, step):
        pc, sz = self.pc, self.pc.sz
        for jump in range(1, sz.fsdp):
            self.along_fsdp(jump, step).wait_recv()
            if step >= 2:
                self.along_fsdp(jump, step - 2).start()
        total = self.dw[self.rows(pc.f * sz.ctx + pc.ctx_ahead(step))].astype(f32)
        for jump in range(1, sz.fsdp):
            total = total + self.got[jump - 1, step].astype(f32)
        self.got[0, step] = total.astype(bf16)
        if step:
            self.along_ctx(step).start()
        else:
            self.own_copy().start()

    def pass_early(self):
        for step in self.order[:-3]:
            self.pass_on(step)

    def part(self, step):
        return functools.partial(self.pass_on, step)

    def finish(self):
        sz = self.pc.sz
        self.own_copy().wait()
        for step in range(sz.ctx):
            if step:
                self.from_ctx(step).wait_recv()
                self.along_ctx(step).wait_send()
            for jump in range(1, sz.fsdp):
                self.along_fsdp(jump, step).wait_send()


def mover_sems(sz):
    return DMA((sz.fsdp, 2, sz.ctx))


def chosen(sz, group, lanes_shape):
    row = lax.broadcasted_iota(jnp.int32, lanes_shape, 0)
    col = lax.broadcasted_iota(jnp.int32, lanes_shape, 1)
    return jnp.where((row - group * sz.wrows == col) & (col < sz.wrows), 1.0, 0.0).astype(bf16)


def drop_padding(sz, src, dst):
    for at in range(0, dst.shape[-1], 128):
        lanes = slice(at, at + 128)

        def step(group, total):
            rows = pl.ds(pl.multiple_of(group * sz.wrowsp, 16), sz.wrowsp)
            return total + dot(chosen(sz, group, (sz.d, sz.wrowsp)), src[rows, lanes], (1, 0))

        dst[:, lanes] = lax.fori_loop(0, sz.groups, step, jnp.zeros((sz.d, 128), f32)).astype(bf16)


def add_padding(sz, src, dst):
    def step(group, carry):
        rows = pl.ds(pl.multiple_of(group * sz.wrowsp, 16), sz.wrowsp)
        for at in range(0, dst.shape[-1], 128):
            lanes = slice(at, at + 128)
            dst[rows, lanes] = dot(chosen(sz, group, (sz.d, sz.wrowsp)), src[:, lanes], (0, 0)).astype(bf16)
        return carry

    lax.fori_loop(0, sz.groups, step, 0)


def by_unit(sz, values):
    values = values.reshape(sz.chips, 2, sz.images, sz.part, values.shape[-1])
    return jnp.swapaxes(values, 1, 2).reshape(sz.keys, values.shape[-1])


def shift_lanes(values, start, count, at, width):
    have = values.shape[-1]
    first, last = start // 128 * 128, up_to(start + count, 128)
    to = at // 128 * 128
    span = max(last - first, up_to(at + count, 128) - to)
    piece = values[:, first:min(last, have)].astype(f32)
    if piece.shape[-1] < span:
        piece = jnp.pad(piece, ((0, 0), (0, span - piece.shape[-1])))
    turn = ((at - to) - (start - first)) % span
    if turn:
        piece = pltpu.roll(piece, turn, 1)
    lanes = lanes_of(piece.shape)
    piece = jnp.where((lanes >= at - to) & (lanes < at - to + count), piece, 0.0)
    piece = piece[:, 0:min(span, width - to)]
    return jnp.pad(piece, ((0, 0), (to, width - to - piece.shape[-1])))


def half_of(pc, values, count, width):
    out = shift_lanes(values, 0, count, 0, width)
    for j in range(1, pc.sz.zl):
        out = jnp.where(pc.zl == j, shift_lanes(values, j * count, count, 0, width), out)
    return out


def piece_of(pc, values):
    sz = pc.sz
    values = values.astype(f32)
    over = sz.tp * sz.part - sz.rows
    if over:
        values = jnp.concatenate([values, jnp.zeros((over, sz.d), f32)], axis=0)
    out = values[0:sz.part]
    for t in range(1, sz.tp):
        out = jnp.where(pc.t == t, values[t * sz.part:(t + 1) * sz.part], out)
    return out


def steps_below(values, unit, count):
    out = jnp.zeros_like(values)
    for m in range(1, count):
        out = out + jnp.where(values >= m * unit, 1, 0)
    return out


def key_valid(pc, count):
    sz = pc.sz
    row = lax.broadcasted_iota(jnp.int32, (1, sz.keys), 1)
    unit = steps_below(row, sz.tile, sz.units)
    within = row - unit * sz.tile
    core = steps_below(within, sz.part, 2)
    chip = steps_below(unit, sz.images, sz.chips)
    zl = steps_below(chip, sz.chips_y, sz.zl)
    t = 2 * (chip - zl * sz.chips_y) + core
    token = t * sz.part + within - core * sz.part
    position = ((unit - chip * sz.images) * sz.zl + zl) * sz.rows + token
    return jnp.where((token < sz.rows) & (position < count), 1.0, 0.0)


def own_valid(pc, count):
    sz = pc.sz
    row = lax.broadcasted_iota(jnp.int32, (sz.block, 1), 0)
    piece = steps_below(row, sz.part, sz.images)
    token = pc.t * sz.part + row - piece * sz.part
    position = (piece * sz.zl + pc.zl) * sz.rows + token
    return jnp.where((token < sz.rows) & (position < count), 1.0, 0.0)


def attn_forward(pc, jobs, gather, w_ref, stream, qv, resid, valid_ref, q_ref, k_ref, v_ref, mixed_ref, o_ref,
                 scatter):
    sz = pc.sz
    unpack_out(sz, w_ref, o_ref)

    def project(step, carry):
        unit, at, piece = gather.ready(step)
        both3 = dot(gather.tokens(at, piece), w_ref[:, 0:sz.qkvp], (1, 0))
        gather.ahead(step)
        q_ref[unit] = (take(sz, both3, 0) + qv[0:1, :]).astype(bf16)
        k_ref[unit] = take(sz, both3, 1).astype(bf16)
        v_ref[unit] = (take(sz, both3, 2) + qv[1:2, :]).astype(bf16)
        jobs.at("project", step)
        return carry

    lax.fori_loop(0, sz.units, project, 0)
    gather.finish()

    def attend(step, carry):
        unit = scatter.unit(step)
        keys = k_ref[...].reshape(sz.keys, sz.headp)
        values = v_ref[...].reshape(sz.keys, sz.headp)
        queries = q_ref[unit]
        total = jnp.zeros((sz.tile, sz.headp), f32)
        for head in range(sz.heads):
            probs = probabilities(head_of(queries, head), keys, valid_ref[...])
            total = total + dot(probs.astype(bf16), head_of(values, head), (1, 0))
        mixed = total.astype(bf16)
        mixed_ref[unit] = mixed
        scatter.push(step, dot(mixed, o_ref[...], (1, 1)))
        jobs.at("attend", step)
        return carry

    lax.fori_loop(0, sz.units, attend, 0)
    scatter.flush()
    jobs.run("flush")
    return stream + (scatter.finish() + resid)


def ff_forward(pc, jobs, gather, w_ref, middle_ref, upb, resid, pre_ref, hidden_ref, scatter):
    sz = pc.sz

    def feed(step, carry):
        unit, at, piece = gather.ready(step)
        pre = dot(gather.tokens(at, piece), w_ref[:, 0:sz.ffp], (1, 0)) + upb
        gather.ahead(step)
        pre_ref[unit] = pre
        hidden = 0.5 * pre * (1.0 + jnp.tanh(gelu_root * (pre + gelu_cubic * pre * pre * pre)))
        hidden = jnp.where(lanes_of(hidden.shape) < sz.ff, hidden, 0.0)
        if sz.down_shift:
            hidden = pltpu.roll(hidden, sz.down_shift, 1)
        hidden = hidden.astype(bf16)
        hidden_ref[unit] = hidden
        scatter.push(step, dot(hidden, w_ref[:, sz.down_at:], (1, 1)))
        jobs.at("feed", step)
        return carry

    lax.fori_loop(0, sz.units, feed, 0)
    scatter.flush()
    jobs.run("flush")
    gather.finish()
    return middle_ref[...] + (scatter.finish() + resid)


def norm_low(values, gain, shift):
    high, _ = normalised(values)
    return (high * gain + shift).astype(bf16)


def forward_kernel(sz, *refs):
    n = sz.layers
    aligned = sz.wrowsp == sz.wrows
    ins, outs, scratch = refs[:12], refs[12:12 + 13 * n + 1], refs[12 + 13 * n + 1:]
    (count_ref, in_ref, cot_ref, wqkv_ref, wout_ref, wup_ref, wdown_ref, gain_ref, shift_ref, qv_ref, upb_ref,
     resid_ref) = ins
    saved, (wattn_outs, wff_outs, ends_ref) = outs[:11 * n], split_refs(outs[11 * n:], n, n, 1)
    saved = [saved[l * 11:(l + 1) * 11] for l in range(n)]
    ends_ref = ends_ref[0]
    (own_attn, own_ff, all_attn, all_ff, swap_ref, mine_ref, n_ref, q_ref, k_ref, v_ref, mixed_ref, pre_ref,
     hidden_ref, stream_ref, middle_ref, valid_ref, o_ref, tsems, csems, wsems), team, joined = split_refs(
        scratch, 20, 8, 0 if aligned else 2)
    bufs, (gsems, ssems) = team[:6], team[6:]
    pc = Place(sz)
    greeting = Greeting(team_peers(pc) + weight_peers(pc, True))

    def pack(ref, pieces):
        total = None
        for values, start, count, at in pieces:
            piece = shift_lanes(values, start, count, at, ref.shape[-1])
            total = piece if total is None else total + piece
        ref[0:sz.wrows, :] = total.astype(bf16)
        if not aligned:
            ref[sz.wrows:, :] = jnp.zeros((sz.wrowsp - sz.wrows, ref.shape[-1]), bf16)

    def pack_attn(layer):
        full = sz.wide * sz.zl
        for half in range(sz.zl):
            pieces = [(wqkv_ref[layer], kind * full + half * sz.wide, sz.wide, kind * sz.wide) for kind in range(3)]
            pack(own_attn.at[layer, half], pieces + [(wout_ref[layer], half * sz.wide, sz.wide, 3 * sz.wide)])

    def pack_ff(layer):
        for half in range(sz.zl):
            pack(own_ff.at[layer, half], [(wup_ref[layer], half * sz.ff, sz.ff, 0),
                                          (wdown_ref[layer], half * sz.ff, sz.ff, sz.ff)])

    for image in range(sz.images):
        swap_ref[image, 0] = piece_of(pc, in_ref[image]).astype(bf16)
        swap_ref[image, 1] = piece_of(pc, cot_ref[image]).astype(bf16)
    pack_attn(0)
    attn = [Fetch(pc, own_attn.at[l], all_attn.at[l], wsems.at[2 * l]) for l in range(n)]
    ff = [Fetch(pc, own_ff.at[l], all_ff.at[l], wsems.at[2 * l + 1]) for l in range(n)]
    copies = Copies(csems)

    def swap(step):
        zh = (pc.zh + step) % sz.images
        return send(swap_ref.at[zh], mine_ref.at[pc.zh], tsems.at[0, step], tsems.at[1, step],
                    (pc.f, zh * sz.zl + pc.zl, pc.t))

    greeting.wait()
    for step in range(1, sz.images):
        swap(step).start()
    attn[0].start()
    mine_ref[pc.zh] = swap_ref[pc.zh]
    count = count_ref[pc.zh]
    valid_ref[...] = key_valid(pc, count)
    for step in range(1, sz.images):
        swap(step).wait()
    stream_ref[0] = mine_ref[:, 0].reshape(sz.block, sz.d).astype(f32)
    gathers = [Gather(pc, n_ref.at[i], gsems.at[i], FF_TURN if i % 2 or i == 0 else ()) for i in range(2 * n)]
    scatters = [Scatter(pc, bufs, ssems.at[i], i % 2 == 0) for i in range(2 * n)]
    gathers[0].put(norm_low(stream_ref[0], gain_ref[0, 0:1, :], shift_ref[0, 0:1, :]))
    gathers[0].start()
    attn[0].pass_own()
    pack_ff(0)
    attn[0].pass_on(1)
    for layer in range(1, n):
        pack_attn(layer)
    attn[0].pass_on(2)
    ff[0].start()
    ends_ref[...] = mine_ref[:, 1].reshape(sz.block, sz.d).astype(f32) * own_valid(pc, count)
    attn[0].pass_rest()
    ff[0].pass_own()
    for layer in range(1, n):
        pack_ff(layer)
    attn[0].finish()

    def ready(fetch, refs, kind, layer, out):
        ref = refs.at[layer]
        if not aligned:
            drop_padding(sz, ref, joined[kind])
            ref = joined[kind]
            pltpu.sync_copy(ref, out)
        else:
            copies.start(ref, out)
        return ref

    for l in range(n):
        more = l + 1 < n
        w = ready(attn[l], all_attn, 0, l, wattn_outs[l])
        qv = half_of(pc, qv_ref[l], sz.wide, sz.headp)
        jobs = Jobs(
            project={sz.units - 2: [ff[l].part(1)]},
            attend={2: [ff[l].part(2)], sz.units - 1: ([attn[l + 1].start] if more else [])},
            flush=[ff[l].pass_rest] + ([attn[l + 1].pass_own] if more else []),
        )
        middle_ref[l] = attn_forward(
            pc, jobs, gathers[2 * l], w, stream_ref[l], qv, resid_ref[l, 0:1, :], valid_ref,
            q_ref.at[l], k_ref.at[l], v_ref.at[l], mixed_ref.at[l], o_ref, scatters[2 * l],
        )
        gathers[2 * l + 1].put(norm_low(middle_ref[l], gain_ref[l, 1:2, :], shift_ref[l, 1:2, :]))
        gathers[2 * l + 1].start()
        for ref, to in ((stream_ref.at[l], 0), (middle_ref.at[l], 1), (n_ref.at[2 * l], 2), (q_ref.at[l], 4),
                        (k_ref.at[l], 5), (v_ref.at[l], 6), (mixed_ref.at[l], 7)):
            copies.start(ref, saved[l][to])
        ff[l].finish()
        w = ready(ff[l], all_ff, 1, l, wff_outs[l])
        upb = half_of(pc, upb_ref[l:l + 1, :], sz.ff, sz.ffp)
        if more:
            jobs = Jobs(
                feed={1: [attn[l + 1].part(1)], 3: [attn[l + 1].part(2)], 5: [ff[l + 1].start],
                      6: [attn[l + 1].pass_rest], 7: [ff[l + 1].pass_own]},
            )
        else:
            jobs = Jobs()
        out = ff_forward(pc, jobs, gathers[2 * l + 1], w, middle_ref.at[l], upb, resid_ref[l, 1:2, :],
                         pre_ref.at[l], hidden_ref.at[l], scatters[2 * l + 1])
        stream_ref[l + 1] = out
        if more:
            gathers[2 * l + 2].put(norm_low(out, gain_ref[l + 1, 0:1, :], shift_ref[l + 1, 0:1, :]))
            gathers[2 * l + 2].start()
            attn[l + 1].finish()
        for ref, to in ((n_ref.at[2 * l + 1], 3), (pre_ref.at[l], 8), (hidden_ref.at[l], 9)):
            copies.start(ref, saved[l][to])
    copies.start(stream_ref.at[n], saved[0][10])
    copies.start(valid_ref, saved[n - 1][10])
    copies.wait()


def forward_call(sz, *operands):
    n = sz.layers
    own, team = ((sz.block, sz.d), f32), ((sz.team, sz.images, sz.part, sz.d), bf16)
    head, hidden = ((sz.units, sz.tile, sz.headp), bf16), (sz.units, sz.tile, sz.ffp)
    shapes = []
    for l in range(n):
        last = ((1, sz.keys), f32) if l == n - 1 else own
        shapes += [own, own, team, team, head, head, head, head, (hidden, f32), (hidden, bf16), last]
    shapes += [((sz.d, sz.attnp), bf16)] * n + [((sz.d, sz.ffw), bf16)] * n + [own]
    vmem, hbm = pl.BlockSpec(memory_space=pltpu.VMEM), pl.BlockSpec(memory_space=pl.ANY)
    padded = sz.groups * sz.wrowsp
    scratch = [
        VMEM((n, sz.zl, sz.wrowsp, sz.attnp), bf16), VMEM((n, sz.zl, sz.wrowsp, sz.ffw), bf16),
        VMEM((n, padded, sz.attnp), bf16), VMEM((n, padded, sz.ffw), bf16),
        VMEM((sz.images, 2, sz.part, sz.d), bf16), VMEM((sz.images, 2, sz.part, sz.d), bf16),
        VMEM((2 * n,) + team[0], bf16),
        *[VMEM((n,) + head[0], bf16) for _ in range(4)],
        VMEM((n,) + hidden, f32), VMEM((n,) + hidden, bf16),
        VMEM((n + 1, sz.block, sz.d), f32), VMEM((n, sz.block, sz.d), f32), VMEM((1, sz.keys), f32),
        VMEM((sz.d, sz.headp), bf16),
        DMA((2, sz.images)), DMA((12 * n + 2,)), DMA((2 * n, sz.fsdp, 2, sz.ctx)),
    ] + team_scratch(sz, 2 * n)
    if sz.wrowsp != sz.wrows:
        scratch += [VMEM((sz.d, sz.attnp), bf16), VMEM((sz.d, sz.ffw), bf16)]
    return pl.pallas_call(
        functools.partial(forward_kernel, sz),
        out_shape=[jax.ShapeDtypeStruct(*s) for s in shapes],
        in_specs=[pl.BlockSpec(memory_space=pltpu.SMEM)] + [vmem] * (len(operands) - 1),
        out_specs=[hbm] * (len(shapes) - 1) + [vmem],
        scratch_shapes=scratch,
        compiler_params=params(1),
        name="forward",
    )(*operands)


def params(collective_id):
    return pltpu.CompilerParams(
        collective_id=collective_id, has_side_effects=True, vmem_limit_bytes=63 * 1024 * 1024
    )


def ff_backward(pc, jobs, gather, w_ref, n2_ref, pre_ref, hidden_ref, dup_ref, pg_ref, dw_ref, scatter):
    sz = pc.sz
    span = 384 if sz.d % 384 == 0 else 128
    dup_ref[...] = jnp.zeros_like(dup_ref)

    def feed(step, carry):
        unit, at, piece = gather.ready(step)
        back = dot(gather.tokens(at, piece), w_ref[:, sz.down_at:], (1, 0))
        gather.ahead(step)
        if sz.down_shift:
            back = pltpu.roll(back, sz.ffp - sz.down_shift, 1)
        pre = pre_ref[unit]
        bent = jnp.tanh(gelu_root * (pre + gelu_cubic * pre * pre * pre))
        slope = 0.5 * (1.0 + bent) + 0.5 * pre * (1.0 - bent * bent) * (
            gelu_root * (1.0 + 3.0 * gelu_cubic * pre * pre)
        )
        pre_grad = jnp.where(lanes_of(back.shape) < sz.ff, back * slope, 0.0).astype(bf16)
        pg_ref[unit] = pre_grad
        dup_ref[...] += jnp.sum(pre_grad.astype(f32), axis=0, keepdims=True)
        scatter.push(step, dot(pre_grad, w_ref[:, 0:sz.ffp], (1, 1)))
        jobs.at("feed", step)
        return carry

    lax.fori_loop(0, sz.units, feed, 0)
    scatter.flush()
    jobs.run("flush")

    def grads(i, carry):
        lanes = pl.ds(pl.multiple_of(i * span, 128), span)
        hidden = hidden_ref[...].reshape(sz.keys, sz.ffp)
        down = dot(by_unit(sz, gather.buf[:, :, :, lanes]), hidden, (0, 0))
        pre_grad = pg_ref[...].reshape(sz.keys, sz.ffp)
        up = dot(by_unit(sz, n2_ref[:, :, :, lanes]), pre_grad, (0, 0))
        dw_ref[lanes, 0:sz.down_at] = up[:, 0:sz.down_at].astype(bf16)
        over = sz.ffp - sz.down_at
        if over:
            dw_ref[lanes, sz.down_at:sz.ffp] = (up[:, sz.down_at:] + down[:, 0:over]).astype(bf16)
        dw_ref[lanes, sz.ffp:] = down[:, over:].astype(bf16)
        return carry

    lax.fori_loop(0, sz.d // span, grads, 0)
    jobs.run("grads")
    gather.finish()
    return scatter.finish()


def attn_backward(pc, jobs, gather, w_ref, n1_ref, q_ref, k_ref, v_ref, mixed_ref, valid_ref, dqv_ref,
                  o_ref, dk_ref, dv_ref, stack_ref, dw_ref, scatter):
    sz = pc.sz
    span = 384 if sz.d % 384 == 0 else 128
    unpack_out(sz, w_ref, o_ref)
    dk_ref[...] = jnp.zeros_like(dk_ref)
    dv_ref[...] = jnp.zeros_like(dv_ref)
    dqv_ref[...] = jnp.zeros_like(dqv_ref)
    scale = HEAD_DIM ** (-0.5)

    def attend(step, carry):
        unit, at, piece = gather.ready(step)
        mixed_grad = dot(gather.tokens(at, piece), o_ref[...], (1, 0)).astype(bf16)
        gather.ahead(step)
        keys = k_ref[...].reshape(sz.keys, sz.headp)
        values = v_ref[...].reshape(sz.keys, sz.headp)
        total = jnp.zeros((sz.tile, sz.headp), f32)
        for head in range(sz.heads):
            q_head = head_of(q_ref[unit], head)
            g_head = head_of(mixed_grad, head)
            probs = probabilities(q_head, keys, valid_ref[...])
            dprobs = dot(g_head, values, (1, 1))
            inner = jnp.sum(probs * dprobs, axis=-1, keepdims=True)
            dscores = (probs * (dprobs - inner)).astype(bf16)
            total = total + dot(dscores, head_of(keys, head), (1, 0))
            dk_ref[...] += dot(dscores, q_head, (0, 0))
            dv_ref[...] += dot(probs.astype(bf16), g_head, (0, 0))
        dq = (scale * total).astype(bf16).astype(f32)
        dqv_ref[0:1, :] += jnp.sum(dq, axis=0, keepdims=True)
        stack_ref[unit, :, 0:sz.headp] = dq.astype(bf16)
        jobs.at("attend", step)
        return carry

    lax.fori_loop(0, sz.units, attend, 0)
    gather.finish()
    jobs.run("middle")

    def back_project(step, carry):
        unit = scatter.unit(step)
        rows = pl.ds(pl.multiple_of(unit * sz.tile, sz.tile), sz.tile)
        dk = (scale * dk_ref[rows, :]).astype(bf16).astype(f32)
        dv = dv_ref[rows, :].astype(bf16).astype(f32)
        dqv_ref[1:2, :] += jnp.sum(dv, axis=0, keepdims=True)
        dq = stack_ref[unit, :, 0:sz.headp].astype(f32)
        total = jnp.pad(dq, ((0, 0), (0, sz.qkvp - sz.headp)))
        for kind, piece in ((1, dk), (2, dv)):
            start = kind * sz.wide // 128 * 128
            shift = kind * sz.wide - start
            moved = pltpu.roll(piece, shift, 1) if shift else piece
            total = total + jnp.pad(moved, ((0, 0), (start, sz.qkvp - start - sz.headp)))
        stacked = total.astype(bf16)
        stack_ref[unit] = stacked
        scatter.push(step, dot(stacked, w_ref[:, 0:sz.qkvp], (1, 1)))
        return carry

    lax.fori_loop(0, sz.units, back_project, 0)
    scatter.flush()
    jobs.run("flush")
    o_at = 3 * sz.wide // 128 * 128
    o_shift = 3 * sz.wide - o_at

    def grads(i, carry):
        lanes = pl.ds(pl.multiple_of(i * span, 128), span)
        stacked = stack_ref[...].reshape(sz.keys, sz.qkvp)
        dqkv = dot(by_unit(sz, n1_ref[:, :, :, lanes]), stacked, (0, 0))
        mixed = mixed_ref[...].reshape(sz.keys, sz.headp)
        dout = dot(by_unit(sz, gather.buf[:, :, :, lanes]), mixed, (0, 0))
        if o_shift:
            dout = pltpu.roll(dout, o_shift, 1)
        total = jnp.pad(dqkv, ((0, 0), (0, sz.attnp - sz.qkvp))) + jnp.pad(
            dout, ((0, 0), (o_at, sz.attnp - o_at - sz.headp))
        )
        dw_ref[lanes, 0:sz.attnp] = total.astype(bf16)
        return carry

    lax.fori_loop(0, sz.d // span, grads, 0)
    jobs.run("grads")
    return scatter.finish()


def backward_kernel(sz, *refs):
    n = sz.layers
    aligned = sz.wrowsp == sz.wrows
    saved = [refs[l * 11:(l + 1) * 11] for l in range(n)]
    wattn_ins, wff_ins, (cot_ref, gain_ref), outs, scratch = split_refs(
        refs[11 * n:], n, n, 2, 2 * n + 2, len(refs) - 11 * n - 2 * n - 2 - 2 * n - 2)
    attn_outs, ff_outs, (whole_ref, small_ref) = split_refs(outs, n, n, 2)
    (stream_ref, middle_ref, n1_ref, n2_ref, q_ref, k_ref, v_ref, mixed_ref, pre_ref, hidden_ref, valid_ref, out_ref,
     wattn_ref, wff_ref, gl_ref, ml_ref, pg_ref, o_ref, dk_ref, dv_ref, stack_ref, dwattn_ref, dwff_ref, got_attn,
     got_ff, dqv_ref, dup_ref, grad_ref, ends_ref, first, from_tp, from_ctx, from_fsdp, sum_tp, sum_ctx,
     lsems, wsems, esems, ysems, tsems), team, padded = split_refs(scratch, 40, 8, 0 if aligned else 2)
    bufs, (gsems, ssems) = team[:6], team[6:]
    pc = Place(sz)
    greeting = Greeting(team_peers(pc) + weight_peers(pc, True) + line_peers(pc))
    copies = Copies(lsems)
    into = [stream_ref, middle_ref, n1_ref, n2_ref, q_ref, k_ref, v_ref, mixed_ref, pre_ref, hidden_ref]
    loads = [None] * n

    def load(l, kinds):
        return [copies.start(saved[l][kind], into[kind].at[l]) for kind in kinds]

    ff_loads, attn_loads = [None] * n, [None] * n
    out_load = copies.start(saved[0][10], out_ref)
    for l in reversed(range(n)):
        ff_loads[l] = [copies.start(wff_ins[l], wff_ref.at[l])] + load(l, (8, 3, 9, 1))
        attn_loads[l] = [copies.start(wattn_ins[l], wattn_ref.at[l])] + load(l, (4, 5, 6, 7, 2, 0))
        if l == n - 1:
            attn_loads[l].append(copies.start(saved[l][10], valid_ref))
    give_attn = [Give(pc, dwattn_ref if aligned else padded[0], attn_outs[l], got_attn.at[l], wsems.at[2 * l])
                 for l in range(n)]
    give_ff = [Give(pc, dwff_ref if aligned else padded[1], ff_outs[l], got_ff.at[l], wsems.at[2 * l + 1])
               for l in range(n)]

    def begin(give, dw, kind):
        def run():
            if not aligned:
                add_padding(sz, dw, padded[kind])
            give.start()

        return run

    def swap(kind, step):
        zh = (pc.zh + step) % sz.images
        return send(ends_ref.at[kind, zh], whole_ref.at[kind, pc.t, pc.zh], esems.at[kind, 0, step],
                    esems.at[kind, 1, step], (pc.f, zh * sz.zl + pc.zl, pc.t))

    def own_end(kind):
        return pltpu.make_async_copy(ends_ref.at[kind, pc.zh], whole_ref.at[kind, pc.t, pc.zh], esems.at[kind, 0, 0])

    def spread(kind, step):
        return send(whole_ref.at[kind, pc.t], whole_ref.at[kind, pc.t], ysems.at[kind, 0, step],
                    ysems.at[kind, 1, step], (pc.f, pc.c, (pc.t + step) % sz.tp))

    def spread_from(kind, step):
        back = (pc.t + sz.tp - step) % sz.tp
        return send(whole_ref.at[kind, back], whole_ref.at[kind, back], ysems.at[kind, 0, step],
                    ysems.at[kind, 1, step], (pc.f, pc.c, back))

    def swap_start(kind):
        own_end(kind).start()
        for step in range(1, sz.images):
            swap(kind, step).start()

    def spread_start(kind):
        own_end(kind).wait()
        for step in range(1, sz.images):
            swap(kind, step).wait()
        for step in range(1, sz.tp):
            spread(kind, step).start()

    def spread_wait(kind):
        for step in range(1, sz.tp):
            spread_from(kind, step).wait_recv()
            spread(kind, step).wait_send()

    def over_tp(step):
        return send(first, from_tp.at[step - 1], tsems.at[0, 0, step], tsems.at[0, 1, step],
                    (pc.f, pc.c, (pc.t + step) % sz.tp))

    def over_ctx(step):
        return send(sum_tp, from_ctx.at[step - 1], tsems.at[1, 0, step], tsems.at[1, 1, step],
                    (pc.f, pc.ctx_ahead(step), pc.t))

    def over_fsdp(step):
        return send(sum_ctx, from_fsdp.at[step - 1], tsems.at[2, 0, step], tsems.at[2, 1, step],
                    ((pc.f + step) % sz.fsdp, pc.c, pc.t))

    sum_tp[...] = jnp.zeros_like(sum_tp)
    first[...] = jnp.zeros_like(first)
    out_load.wait()
    ends_ref[0] = out_ref[...].reshape(sz.images, sz.part, sz.d).astype(bf16)
    grad_ref[...] = cot_ref[...]
    gathers = [Gather(pc, (gl_ref, ml_ref)[i % 2], gsems.at[i], FF_TURN if i % 2 == 0 else ()) for i in range(2 * n)]
    scatters = [Scatter(pc, bufs, ssems.at[i], i % 2 == 1) for i in range(2 * n)]
    greeting.wait()
    for turn in range(n):
        l = n - 1 - turn
        start = turn == 0
        low = grad_ref[...].astype(bf16)
        gathers[2 * turn].put(low)
        gathers[2 * turn].start()
        if start:
            swap_start(0)
        first[l, 5:6, :] = jnp.sum(low.astype(f32), axis=0, keepdims=True)
        for copy in ff_loads[l]:
            copy.wait()
        if start:
            jobs = Jobs(feed={4: [lambda: spread_start(0)]}, grads=[begin(give_ff[l], dwff_ref, 1)])
        else:
            after = give_attn[l + 1]
            jobs = Jobs(
                feed={1: [after.pass_early], 3: [after.part(2)], 5: [after.part(1)], 6: [after.part(0)]},
                flush=[give_ff[l + 1].finish],
                grads=[begin(give_ff[l], dwff_ref, 1)],
            )
        second = ff_backward(pc, jobs, gathers[2 * turn], wff_ref.at[l], n2_ref.at[l], pre_ref.at[l],
                             hidden_ref.at[l], dup_ref, pg_ref, dwff_ref, scatters[2 * turn])
        sum_tp[n + pc.zl, 3 * l + 2:3 * l + 3, 0:sz.ffp] = dup_ref[...]
        term, dgain, dshift = norm_back(middle_ref[l], gain_ref[l, 1:2, :], second)
        first[l, 1:2, :] = dgain
        first[l, 3:4, :] = dshift
        grad_ref[...] += term
        low = grad_ref[...].astype(bf16)
        gathers[2 * turn + 1].put(low)
        gathers[2 * turn + 1].start()
        first[l, 4:5, :] = jnp.sum(low.astype(f32), axis=0, keepdims=True)
        for copy in attn_loads[l]:
            copy.wait()
        if start:
            spread_wait(0)
        now = give_ff[l]
        jobs = Jobs(
            attend={2: [now.pass_early], 3: [now.part(2)], 5: [now.part(1)], 6: [now.part(0)]},
            flush=([] if start else [give_attn[l + 1].finish]),
            grads=[begin(give_attn[l], dwattn_ref, 0)],
        )
        below = attn_backward(pc, jobs, gathers[2 * turn + 1], wattn_ref.at[l], n1_ref.at[l], q_ref.at[l],
                              k_ref.at[l], v_ref.at[l], mixed_ref.at[l], valid_ref, dqv_ref, o_ref, dk_ref, dv_ref,
                              stack_ref, dwattn_ref, scatters[2 * turn + 1])
        sum_tp[n + pc.zl, 3 * l:3 * l + 2, 0:sz.headp] = dqv_ref[...]
        term, dgain, dshift = norm_back(stream_ref[l], gain_ref[l, 0:1, :], below)
        first[l, 0:1, :] = dgain
        first[l, 2:3, :] = dshift
        grad_ref[...] += term
    last = give_attn[0]
    ends_ref[1] = grad_ref[...].reshape(sz.images, sz.part, sz.d).astype(bf16)
    swap_start(1)
    for step in range(1, sz.tp):
        over_tp(step).start()
    last.pass_early()
    spread_start(1)
    last.pass_on(2)
    value = first[...]
    for step in range(1, sz.tp):
        over_tp(step).wait()
        value = value + from_tp[step - 1]
    sum_tp[0:n] = value
    for step in range(1, sz.ctx):
        over_ctx(step).start()
    last.pass_on(1)
    value = sum_tp[...]
    for step in range(1, sz.ctx):
        over_ctx(step).wait()
        value = value + from_ctx[step - 1]
    sum_ctx[...] = value
    for step in range(1, sz.fsdp):
        over_fsdp(step).start()
    last.pass_on(0)
    value = sum_ctx[...]
    for step in range(1, sz.fsdp):
        over_fsdp(step).wait()
        value = value + from_fsdp[step - 1]
    small_ref[...] = value
    give_ff[0].finish()
    spread_wait(1)
    last.finish()


def backward_call(sz, saved, wattn, wff, cot, gains):
    n = sz.layers
    own, team = (sz.block, sz.d), (sz.team, sz.images, sz.part, sz.d)
    head, hidden = (sz.units, sz.tile, sz.headp), (sz.units, sz.tile, sz.ffp)
    deep = up_to(max(6, 3 * n), 8)
    small = (n + sz.zl, deep, sz.d)
    ends = (sz.images, sz.part, sz.d)
    attn_sum, ff_sum = (sz.ctx, sz.wrowsp, sz.attnp), (sz.ctx, sz.wrowsp, sz.ffw)
    shapes = [(attn_sum, bf16)] * n + [(ff_sum, bf16)] * n + [((2, sz.tp) + ends, bf16), (small, f32)]
    vmem, hbm = pl.BlockSpec(memory_space=pltpu.VMEM), pl.BlockSpec(memory_space=pl.ANY)
    far, jumps = max(sz.tp, sz.ctx, sz.fsdp), max(sz.fsdp - 1, 1)
    scratch = [
        VMEM((n,) + own, f32), VMEM((n,) + own, f32), VMEM((n,) + team, bf16), VMEM((n,) + team, bf16),
        *[VMEM((n,) + head, bf16) for _ in range(4)], VMEM((n,) + hidden, f32), VMEM((n,) + hidden, bf16),
        VMEM((1, sz.keys), f32), VMEM(own, f32),
        VMEM((n, sz.d, sz.attnp), bf16), VMEM((n, sz.d, sz.ffw), bf16),
        VMEM(team, bf16), VMEM(team, bf16), VMEM(hidden, bf16), VMEM((sz.d, sz.headp), bf16),
        VMEM((sz.keys, sz.headp), f32), VMEM((sz.keys, sz.headp), f32), VMEM((sz.units, sz.tile, sz.qkvp), bf16),
        VMEM((sz.d, sz.attnp), bf16), VMEM((sz.d, sz.ffw), bf16),
        VMEM((n, jumps) + attn_sum, bf16), VMEM((n, jumps) + ff_sum, bf16),
        VMEM((2, sz.headp), f32), VMEM((1, sz.ffp), f32), VMEM(own, f32), VMEM((2,) + ends, bf16),
        VMEM((n, deep, sz.d), f32), VMEM((sz.tp - 1, n, deep, sz.d), f32),
        VMEM((max(sz.ctx - 1, 1),) + small, f32), VMEM((jumps,) + small, f32), VMEM(small, f32), VMEM(small, f32),
        DMA((12 * n + 2,)), DMA((2 * n, sz.fsdp, 2, sz.ctx)), DMA((2, 2, sz.images)), DMA((2, 2, sz.tp)),
        DMA((3, 2, far)),
    ] + team_scratch(sz, 2 * n)
    if sz.wrowsp != sz.wrows:
        padded = sz.groups * sz.wrowsp
        scratch += [VMEM((padded, sz.attnp), bf16), VMEM((padded, sz.ffw), bf16)]
    operands = (*saved, *wattn, *wff, cot, gains)
    return pl.pallas_call(
        functools.partial(backward_kernel, sz),
        out_shape=[jax.ShapeDtypeStruct(*s) for s in shapes],
        in_specs=[hbm] * (len(operands) - 2) + [vmem] * 2,
        out_specs=[hbm] * (2 * n + 1) + [vmem],
        scratch_shapes=scratch,
        compiler_params=params(2),
        name="backward",
    )(*operands)


def close_kernel(sz, *refs):
    n = sz.layers
    attn_refs, ff_refs, (whole_ref, small_ref), outs = split_refs(refs, n, n, 2, 11)
    out_ref, gin_ref, gain_ref, bias_ref, qkv_ref, qv_ref, wout_ref, up_ref, upb_ref, down_ref, resid_ref = outs
    full, ff = sz.wide * sz.zl, sz.ff * sz.zl

    def summed(ref):
        return [sum(ref[zh * sz.zl + j].astype(f32) for zh in range(sz.images)) for j in range(sz.zl)]

    def join(halves, start, count, width):
        total = None
        for j, values in enumerate(halves):
            piece = shift_lanes(values, start, count, j * count, up_to(width, 128))
            total = piece if total is None else total + piece
        return total[0:sz.wrows, 0:width]

    for layer in range(n):
        halves = summed(attn_refs[layer])
        for kind in range(3):
            at = kind * full
            qkv_ref[layer, :, at:at + full] = join(halves, kind * sz.wide, sz.wide, full)
        wout_ref[layer] = join(halves, 3 * sz.wide, sz.wide, full)
        halves = summed(ff_refs[layer])
        up_ref[layer] = join(halves, 0, sz.ff, ff)
        down_ref[layer] = join(halves, sz.ff, sz.ff, ff)
        values = small_ref[layer]
        gain_ref[layer] = values[0:2]
        bias_ref[layer] = values[2:4]
        resid_ref[layer] = values[4:6]
        total_qv, total_up = None, None
        for half in range(sz.zl):
            values = small_ref[n + half]
            qv = shift_lanes(values, 0, sz.wide, half * sz.wide, up_to(full, 128))
            up = shift_lanes(values, 0, sz.ff, half * sz.ff, up_to(ff, 128))
            total_qv = qv if total_qv is None else total_qv + qv
            total_up = up if total_up is None else total_up + up
        qv_ref[layer] = total_qv[3 * layer:3 * layer + 2, 0:full]
        upb_ref[layer:layer + 1, :] = total_up[3 * layer + 2:3 * layer + 3, 0:ff]
    for image in range(sz.images):
        rows = whole_ref[0, :, image].reshape(sz.tp * sz.part, sz.d)
        out_ref[image] = rows[0:sz.rows]
        rows = whole_ref[1, :, image].reshape(sz.tp * sz.part, sz.d)
        gin_ref[image] = rows.astype(f32)[0:sz.rows]


def close_call(sz, attn_sums, ff_sums, ends, small):
    n, full, ff = sz.layers, sz.wide * sz.zl, sz.ff * sz.zl
    tokens = (sz.images, sz.rows, sz.d)
    vec, up = ((n, 2, sz.d), f32), ((n, sz.wrows, ff), f32)
    shapes = [
        (tokens, bf16), (tokens, f32), vec, vec, ((n, sz.wrows, 3 * full), f32), ((n, 2, full), f32),
        ((n, sz.wrows, full), f32), up, ((n, ff), f32), up, vec,
    ]
    vmem = pl.BlockSpec(memory_space=pltpu.VMEM)
    results = pl.pallas_call(
        functools.partial(close_kernel, sz),
        out_shape=[jax.ShapeDtypeStruct(*s) for s in shapes],
        in_specs=[vmem] * (2 * n + 2),
        out_specs=[vmem] * len(shapes),
        compiler_params=pltpu.CompilerParams(vmem_limit_bytes=60 * 1024 * 1024),
        name="close",
    )(*attn_sums, *ff_sums, ends, small)
    results = list(results)
    results[4] = results[4].reshape(n, sz.wrows, 3, full)
    return tuple(results)


def per_device(mesh, inputs, cotangent, valid_count, norm_gain, norm_bias, w_qkv, bias_qv, w_out, w_up, bias_up,
               w_down, bias_resid):
    sz = Sizes(mesh, inputs, w_qkv, w_up)
    n = sz.layers
    *made, cot = forward_call(sz, valid_count, inputs, cotangent, w_qkv.reshape(n, sz.wrows, -1), w_out, w_up,
                              w_down, norm_gain, norm_bias, bias_qv, bias_up, bias_resid)
    saved, wattn, wff = split_refs(made, 11 * n, n, n)
    *sums, ends, small = backward_call(sz, saved, wattn, wff, cot, norm_gain)
    return close_call(sz, sums[:n], sums[n:], ends, small)


def solution(mesh):
    tokens, rows = P("fsdp", "ctx", None), P(None, ("fsdp", "ctx"), "tp")
    qkv = P(None, ("fsdp", "ctx"), None, "tp")
    qv, up = P(None, None, "tp"), P(None, "tp")
    return jax.shard_map(
        functools.partial(per_device, mesh),
        mesh=mesh,
        in_specs=(tokens, tokens, P("fsdp"), P(), P(), qkv, qv, rows, rows, up, rows, P()),
        out_specs=(tokens, tokens, P(), P(), qkv, qv, rows, rows, up, rows, P()),
        check_vma=False,
    )
```

time: 477 us -> 391 us (0.82)
  Pallas kernels: 458 us -> 384 us
  local copies, waits for them, and re-layouts: 14.5 us -> 6.28 us
    pallas_call x10 -> x2, Pallas kernels: 451 us -> 377 us  [the longest x1 198 us: backward_call(): pl.pallas_call(functools.partial(backward_kernel, sz), out_shape=[jax.Sha...]
where the time goes in v4:
time: 391 us; the launch traced here: 390 us
  Pallas kernels  384 us (98%)
  local copies, waits for them, and re-layouts  6.28 us (2%)
    pallas_call x1, Pallas kernels, backward_call(): pl.pallas_call(functools.partial(backward_kernel, sz), out_shape=[jax.Sha...  198 us
    pallas_call x1, Pallas kernels, forward_call(): pl.pallas_call(functools.partial(forward_kernel, sz), out_shape=[jax.Shap...  178 us

profile of v4, /device:TPU:0, one launch (start us, length us, event | category | flops | bytes accessed | tf_op | source)
XLA Modules:
  0.0 390.5 jit_solution(10898711708368856772)
XLA Ops:
  0.6 1.4 copy.25
  2.1 1.3 reshape.28.refs_3_
  3.3 178.3 %forward.1 = (f32[96,1152]{1,0:T(8,128)}, f32[96,1152]{1,0:T(8,128)}, bf16[8,2,48,1152]{3,2,1,0:T(8,128)(2,1)}, bf16[8,2,48,1152]{3,2,1,0:T(8,128)(2,1)}, bf16[8...) custom-call(s32[2]{0:T(128)} %refs_0_.1, ...), custom_call_target="tpu_custom_call" | custom-call | tf_op jit(solution)/shard_map/forward/pallas_call | solution.py:895
  181.6 198.3 %backward.1 = (bf16[4,144,640]{2,1,0:T(8,128)(2,1)}, bf16[4,144,640]{2,1,0:T(8,128)(2,1)}, bf16[4,144,1152]{2,1,0:T(8,128)(2,1)}, bf16[4,144,1152]{2,1,0:T(8,128...) custom-call(f32[96,1152]{1,0:T(8,128)} %get-tuple-element.55.refs_0_, ...), custom_call_target="tpu_custom_call" | custom-call | tf_op jit(solution)/shard_map/backward/pallas_call | solution.py:1246
  379.9 6.9 %close.1 = (bf16[2,184,1152]{2,1,0:T(8,128)(2,1)}, f32[2,184,1152]{2,1,0:T(8,128)}, f32[2,2,1152]{2,1,0:T(2,128)}, f32[2,2,1152]{2,1,0:T(2,128)}, f32[2,144,864]...) custom-call(bf16[4,144,640]{2,1,0:T(8,128)(2,1)} %get-tuple-element., ...), custom_call_target="tpu_custom_call" | custom-call | tf_op jit(solution)/shard_map/close/pallas_call | solution.py:1311
  386.9 2.4 reshape.29
  389.3 1.1 copy.26
